TPU v7x, 32 devices: a whole 2x2x4 slice. The times are simulated.
32 devices in a mesh: expert: 8 (over z, y), tensor: 4 (over x, core).
Axes of the slice: x: 2, y: 2, z: 4, core: 2. Of those that a mesh axis runs over, the one named last changes fastest.
Arguments:
- tokens: bfloat16 [2048, 2048], P('expert'), may hold values from -6 to 6
- cotangent: bfloat16 [2048, 2048], P('expert'), may hold values from -8 to 8
- segment_ids: int32 [8, 256], P('expert'), may hold values from 0 to 3, never falling along the last dimension, each value on 1 to 128 neighbouring positions
- routes_att: int32 [2048, 2], P('expert'), may hold values from 0 to 7, all different within a row; in each aligned block of 256 rows (0 to 255, 256 to 511, ...) at most 96 rows name the same one
- routes_mlp: int32 [2048, 2], P('expert'), may hold values from 0 to 7, all different within a row; in each aligned block of 256 rows (0 to 255, 256 to 511, ...) at most 96 rows name the same one
- gain_att: bfloat16 [2048], P('expert'), may hold values from 0.5 to 1.5
- router_att: bfloat16 [2048, 8], P('expert'), may hold values from -0.125 to 0.125
- w_query: bfloat16 [2048, 8, 2048], P('expert', None, 'tensor'), may hold values from -0.125 to 0.125
- w_key: bfloat16 [2048, 2048], P('expert', 'tensor'), may hold values from -0.125 to 0.125
- w_value: bfloat16 [2048, 2048], P('expert', 'tensor'), may hold values from -0.125 to 0.125
- w_output: bfloat16 [2048, 8, 2048], P('expert', None, 'tensor'), may hold values from -1 to 1
- gain_mlp: bfloat16 [2048], P('expert'), may hold values from 0.5 to 1.5
- router_mlp: bfloat16 [2048, 8], P('expert'), may hold values from -0.125 to 0.125
- w_gate: bfloat16 [8, 2048, 5632], P('expert', None, 'tensor'), may hold values from -0.125 to 0.125
- w_up: bfloat16 [8, 2048, 5632], P('expert', None, 'tensor'), may hold values from -0.125 to 0.125
- w_down: bfloat16 [8, 5632, 2048], P('expert', 'tensor'), may hold values from -0.078125 to 0.078125
Outputs:
- mixed_out: bfloat16 [2048, 2048], P('expert')
- grad_tokens: float32 [2048, 2048], P('expert')
- grad_gain_att: float32 [2048], P('expert')
- grad_router_att: float32 [2048, 8], P('expert')
- grad_query: float32 [2048, 8, 2048], P('expert', None, 'tensor')
- grad_key: float32 [2048, 2048], P('expert', 'tensor')
- grad_value: float32 [2048, 2048], P('expert', 'tensor')
- grad_output: float32 [2048, 8, 2048], P('expert', None, 'tensor')
- grad_gain_mlp: float32 [2048], P('expert')
- grad_router_mlp: float32 [2048, 8], P('expert')
- grad_gate: float32 [8, 2048, 5632], P('expert', None, 'tensor')
- grad_up: float32 [8, 2048, 5632], P('expert', None, 'tensor')
- grad_down: float32 [8, 5632, 2048], P('expert', 'tensor')
Inputs may be any that keep to these rules, and one draw needn't show every extreme that they name: `segment_ids`: document numbers never fall along a sequence; each document has 1 to 128 positions, one exactly that many. `routes_att`: each row names two different attention experts; in the rows of one sequence no expert is named more than 96 times, and in some sequence one expert exactly 96 times. `routes_mlp`: each row names two different feed-forward experts; in the rows of one sequence no expert is named more than 96 times, and in some sequence one expert exactly 96 times.
All inputs are finite; a program needn't handle non-finite values.
Results may differ from a plain program's by a relative error of at most 0.014.
Values may be sent and summed in bfloat16 or wider, within the bound.
No kernel may reach another device: no remote copies, remote signals or barrier semaphores. Data moves between devices by JAX's collectives and lax.ppermute only.
A program may use at most 320 MiB of HBM per device.

v0:
```python
import jax
import jax.numpy as jnp
from jax import lax
from jax.sharding import PartitionSpec as P

D = 2048
HEAD_DIM = 128
EA = 8
EXPERTS = 8
CAP = 96


EPSILON = 1e-05
ROTARY_BASE = 10000.0
PRECISE = lax.Precision.HIGHEST


def slot_table(route_pairs, count_kinds, capacity, part_count):
    flat_kind = route_pairs.reshape(-1)
    total_rows = flat_kind.shape[0]
    onehot = (flat_kind[:, None] == jnp.arange(count_kinds, dtype=jnp.int32)[None, :]).astype(
        jnp.int32
    )
    ranking = jnp.sum((jnp.cumsum(onehot, axis=0) - 1) * onehot, axis=1)
    quarter = capacity // part_count
    slot_of = ranking // quarter * (count_kinds * quarter) + flat_kind * quarter + ranking % quarter
    source_rows = (
        jnp.zeros((count_kinds * capacity,), jnp.int32)
        .at[slot_of]
        .set(jnp.arange(total_rows, dtype=jnp.int32))
    )
    filled = jnp.zeros((count_kinds * capacity,), jnp.int32).at[slot_of].set(1)
    return (source_rows, filled, slot_of.reshape(route_pairs.shape))


def angles(length, width):
    half_width = width // 2
    freqs = ROTARY_BASE ** (-(jnp.arange(half_width, dtype=jnp.float32) * 2.0 / width))
    phase = jnp.arange(length, dtype=jnp.float32)[:, None] * freqs[None, :]
    phase = jnp.concatenate([phase, phase], axis=1)
    return (jnp.cos(phase), jnp.sin(phase))


def rotate(values, cosine, sine_table):
    half_width = values.shape[-1] // 2
    turned = jnp.concatenate([-values[..., half_width:], values[..., :half_width]], axis=-1)
    return values * cosine + turned * sine_table


def pair_gates(logits, route_pairs):
    onehot = (
        route_pairs[:, :, None] == jnp.arange(logits.shape[1], dtype=jnp.int32)[None, None, :]
    ).astype(jnp.float32)
    chosen = jnp.sum(logits[:, None, :] * onehot, axis=2)
    return jax.nn.softmax(chosen, axis=-1)


def logit_grad(gate_pair, dgate_pair, route_pairs, count_kinds):
    inner = gate_pair * (dgate_pair - jnp.sum(gate_pair * dgate_pair, axis=1, keepdims=True))
    onehot = (
        route_pairs[:, :, None] == jnp.arange(count_kinds, dtype=jnp.int32)[None, None, :]
    ).astype(jnp.float32)
    return jnp.sum(inner[:, :, None] * onehot, axis=1)


def norm_back(values, factor, gain, dnormed):
    weighted = dnormed * gain
    dgain = jnp.sum(dnormed * values * factor, axis=0)
    dvalues = factor * weighted - values * factor * factor * factor * jnp.mean(
        weighted * values, axis=1, keepdims=True
    )
    return (dvalues, dgain)


def score_table(query, key_rot, allowed):
    scores = jnp.einsum(
        "tchd,uhd->chtu", query, key_rot, preferred_element_type=jnp.float32
    ) * HEAD_DIM ** (-0.5)
    return jnp.where(allowed[None, None], scores, -1e30)


def to_owners(slot_rows):
    return lax.all_to_all(slot_rows, "expert", split_axis=1, concat_axis=1, tiled=True)


def from_owners(slot_rows):
    return lax.all_to_all(slot_rows, "expert", split_axis=0, concat_axis=0, tiled=True)


def tensor_reduce(term_fn, count_rows):
    return lax.psum_scatter(
        term_fn(jnp.int32(0), count_rows * lax.axis_size("tensor")),
        "tensor",
        scatter_dimension=0,
        tiled=True,
    )


def body(
    tokens,
    cotangent,
    segment_ids,
    routes_att,
    routes_mlp,
    gain_att,
    router_att,
    w_query,
    w_key,
    w_value,
    w_output,
    gain_mlp,
    router_mlp,
    w_gate,
    w_up,
    w_down,
):
    part_count = lax.axis_size("tensor")
    devices = lax.axis_size("expert")
    group_size = devices // EXPERTS
    length = tokens.shape[0]
    quarter = CAP // part_count
    local_width = w_key.shape[1]
    local_heads = local_width // HEAD_DIM
    gain_one, route_one, query_w, key_w, value_w, output_w, gain_two, route_two = (
        lax.all_gather(gain_att, "expert", axis=0, tiled=True),
        lax.all_gather(router_att, "expert", axis=0, tiled=True),
        lax.all_gather(w_query, "expert", axis=0, tiled=True),
        lax.all_gather(w_key, "expert", axis=0, tiled=True),
        lax.all_gather(w_value, "expert", axis=0, tiled=True),
        lax.all_gather(w_output, "expert", axis=0, tiled=True),
        lax.all_gather(gain_mlp, "expert", axis=0, tiled=True),
        lax.all_gather(router_mlp, "expert", axis=0, tiled=True),
    )
    gain_one = gain_one.astype(jnp.float32)
    gain_two = gain_two.astype(jnp.float32)
    inputs = tokens.astype(jnp.float32)
    scale_one = lax.rsqrt(jnp.mean(inputs * inputs, axis=1, keepdims=True) + EPSILON)
    normed_one = (inputs * scale_one * gain_one).astype(jnp.bfloat16)
    gates_one = pair_gates(
        jnp.dot(normed_one, route_one, preferred_element_type=jnp.float32), routes_att
    )
    source_one, filled_one, slots_one = slot_table(routes_att, EA, CAP, 1)
    keep_one = filled_one[:, None].astype(jnp.bfloat16)
    rows_one = (normed_one[source_one // 2] * keep_one).reshape(EA, CAP, D)
    query_buf = jnp.einsum(
        "ecd,deh->ech", rows_one, query_w, preferred_element_type=jnp.float32
    ).reshape(EA * CAP, local_width)
    query_raw = query_buf[slots_one].reshape(length, 2, local_heads, HEAD_DIM)
    cosine, sine_table = angles(length, HEAD_DIM)
    query = rotate(query_raw, cosine[:, None, None, :], sine_table[:, None, None, :]).astype(
        jnp.bfloat16
    )
    key_raw = jnp.dot(normed_one, key_w, preferred_element_type=jnp.float32).reshape(
        length, local_heads, HEAD_DIM
    )
    key_rot = rotate(key_raw, cosine[:, None, :], sine_table[:, None, :]).astype(jnp.bfloat16)
    value_heads = (
        jnp.dot(normed_one, value_w, preferred_element_type=jnp.float32)
        .astype(jnp.bfloat16)
        .reshape(length, local_heads, HEAD_DIM)
    )
    places = jnp.arange(length)
    segment = segment_ids[0]
    allowed = (segment[:, None] == segment[None, :]) & (places[None, :] <= places[:, None])
    scores = score_table(query, key_rot, allowed)
    top_score = jnp.max(scores, axis=-1, keepdims=True)
    lse_kept = top_score + jnp.log(jnp.sum(jnp.exp(scores - top_score), axis=-1, keepdims=True))
    weights_low = jnp.exp(scores - lse_kept).astype(jnp.bfloat16)
    mixed_heads = jnp.einsum(
        "chtu,uhd->tchd", weights_low, value_heads, preferred_element_type=jnp.float32
    ).astype(jnp.bfloat16)
    flat_mixed = mixed_heads.reshape(2 * length, local_width)
    out_rows = (flat_mixed[source_one] * keep_one).reshape(EA, CAP, local_width)
    branch_buf = jnp.einsum(
        "ech,deh->ecd", out_rows, output_w, preferred_element_type=jnp.float32
    ).reshape(EA * CAP, D)
    branch = lax.psum(branch_buf[slots_one], "tensor")
    hidden_state = inputs + jnp.sum(gates_one[:, :, None] * branch, axis=1)
    scale_two = lax.rsqrt(jnp.mean(hidden_state * hidden_state, axis=1, keepdims=True) + EPSILON)
    normed_two = (hidden_state * scale_two * gain_two).astype(jnp.bfloat16)
    gates_two = pair_gates(
        jnp.dot(normed_two, route_two, preferred_element_type=jnp.float32), routes_mlp
    )
    source_two, filled_two, slots_two = slot_table(routes_mlp, EXPERTS, CAP, part_count)
    keep_two = filled_two[:, None].astype(jnp.bfloat16)

    def spread_copies(slot_rows):
        shaped = slot_rows.reshape(part_count, EXPERTS, 1, quarter, D)
        return jnp.broadcast_to(shaped, (part_count, EXPERTS, group_size, quarter, D)).reshape(
            part_count, devices, quarter, D
        )

    send_rows = spread_copies(normed_two[source_two // 2] * keep_two)
    arrived = to_owners(send_rows)
    expert_rows = arrived.reshape(-1, D)
    gate_pre = jnp.dot(expert_rows, w_gate[0], preferred_element_type=jnp.float32)
    up_pre = jnp.dot(expert_rows, w_up[0], preferred_element_type=jnp.float32)
    acted = (jax.nn.silu(gate_pre) * up_pre).astype(jnp.bfloat16)
    row_share = expert_rows.shape[0] // part_count

    def down_rows(first, count_rows):
        return jnp.dot(acted, w_down[0], preferred_element_type=jnp.float32)

    summed = tensor_reduce(down_rows, row_share)
    returned = from_owners(summed.reshape(devices, quarter, D))
    expert_part = jnp.sum(returned.reshape(EXPERTS, group_size, quarter, D), axis=1).astype(
        jnp.bfloat16
    )
    expert_all = lax.all_gather(expert_part[None], "tensor", axis=0, tiled=True).reshape(-1, D)
    expert_out = expert_all[slots_two]
    expert_float = expert_out.astype(jnp.float32)
    mixed_out = (hidden_state + jnp.sum(gates_two[:, :, None] * expert_float, axis=1)).astype(
        jnp.bfloat16
    )
    upstream = cotangent.astype(jnp.float32)
    dgates_two = jnp.sum(expert_float * upstream[:, None, :], axis=2)
    dlogits_two = logit_grad(gates_two, dgates_two, routes_mlp, EXPERTS)
    grad_router_mlp = jnp.dot(normed_two.astype(jnp.float32).T, dlogits_two, precision=PRECISE)
    dnormed_two = jnp.dot(dlogits_two, route_two.astype(jnp.float32).T, precision=PRECISE)
    dexpert = (
        (gates_two[:, :, None] * upstream[:, None, :]).astype(jnp.bfloat16).reshape(2 * length, D)
    )
    send_grads = spread_copies(dexpert[source_two] * keep_two)
    arrived_grads = to_owners(send_grads)
    dout_rows = arrived_grads.reshape(-1, D)
    dacted = jnp.einsum("rd,fd->rf", dout_rows, w_down[0], preferred_element_type=jnp.float32)
    grad_down = jnp.einsum("rf,rd->fd", acted, dout_rows, preferred_element_type=jnp.float32)[None]
    sigma = jax.nn.sigmoid(gate_pre)
    dup = (dacted * gate_pre * sigma).astype(jnp.bfloat16)
    dgate = (dacted * up_pre * sigma * (1.0 + gate_pre * (1.0 - sigma))).astype(jnp.bfloat16)
    grad_gate = jnp.einsum("rd,rf->df", expert_rows, dgate, preferred_element_type=jnp.float32)[
        None
    ]
    grad_up = jnp.einsum("rd,rf->df", expert_rows, dup, preferred_element_type=jnp.float32)[None]

    def input_rows(first, count_rows):
        return jnp.einsum(
            "rf,df->rd", dgate, w_gate[0], preferred_element_type=jnp.float32
        ) + jnp.einsum("rf,df->rd", dup, w_up[0], preferred_element_type=jnp.float32)

    dsummed = tensor_reduce(input_rows, row_share)
    dreturned = from_owners(dsummed.reshape(devices, quarter, D))
    dpart = jnp.sum(dreturned.reshape(EXPERTS, group_size, quarter, D), axis=1)
    dall = lax.all_gather(dpart[None], "tensor", axis=0, tiled=True).reshape(-1, D)
    dnormed_two = dnormed_two + jnp.sum(dall[slots_two], axis=1)
    dhidden_part, grad_gain_two = norm_back(hidden_state, scale_two, gain_two, dnormed_two)
    dhidden = upstream + dhidden_part
    dgates_one = jnp.sum(branch * dhidden[:, None, :], axis=2)
    dlogits_one = logit_grad(gates_one, dgates_one, routes_att, EA)
    grad_route_one = jnp.dot(normed_one.astype(jnp.float32).T, dlogits_one, precision=PRECISE)
    drouter_one = jnp.dot(dlogits_one, route_one.astype(jnp.float32).T, precision=PRECISE)
    dbranch = (
        (gates_one[:, :, None] * dhidden[:, None, :]).astype(jnp.bfloat16).reshape(2 * length, D)
    )
    dbranch_rows = (dbranch[source_one] * keep_one).reshape(EA, CAP, D)
    grad_output = jnp.einsum(
        "ecd,ech->deh", dbranch_rows, out_rows, preferred_element_type=jnp.float32
    )
    dmixed_buf = jnp.einsum(
        "ecd,deh->ech", dbranch_rows, output_w, preferred_element_type=jnp.float32
    ).reshape(EA * CAP, local_width)
    dmixed = dmixed_buf[slots_one].astype(jnp.bfloat16).reshape(length, 2, local_heads, HEAD_DIM)
    weights_again = jnp.exp(score_table(query, key_rot, allowed) - lse_kept)
    dweights = jnp.einsum("tchd,uhd->chtu", dmixed, value_heads, preferred_element_type=jnp.float32)
    inner_sum = jnp.sum(weights_again * dweights, axis=-1, keepdims=True)
    dscores = (weights_again * (dweights - inner_sum)).astype(jnp.bfloat16)
    dquery = jnp.einsum(
        "chtu,uhd->tchd", dscores, key_rot, preferred_element_type=jnp.float32
    ) * HEAD_DIM ** (-0.5)
    dkey = jnp.einsum(
        "chtu,tchd->uhd", dscores, query, preferred_element_type=jnp.float32
    ) * HEAD_DIM ** (-0.5)
    dvalue = jnp.einsum(
        "chtu,tchd->uhd",
        weights_again.astype(jnp.bfloat16),
        dmixed,
        preferred_element_type=jnp.float32,
    )
    dvalue = dvalue.astype(jnp.bfloat16).reshape(length, local_width)
    dquery_pre = rotate(dquery, cosine[:, None, None, :], -sine_table[:, None, None, :]).astype(
        jnp.bfloat16
    )
    dkey_pre = (
        rotate(dkey, cosine[:, None, :], -sine_table[:, None, :])
        .astype(jnp.bfloat16)
        .reshape(length, local_width)
    )
    dquery_rows = (dquery_pre.reshape(2 * length, local_width)[source_one] * keep_one).reshape(
        EA, CAP, local_width
    )
    grad_query = jnp.einsum(
        "ecd,ech->deh", rows_one, dquery_rows, preferred_element_type=jnp.float32
    )
    dnormed_buf = jnp.einsum(
        "ech,deh->ecd", dquery_rows, query_w, preferred_element_type=jnp.float32
    ).reshape(EA * CAP, D)
    grad_key = jnp.einsum("td,th->dh", normed_one, dkey_pre, preferred_element_type=jnp.float32)
    grad_value = jnp.einsum("td,th->dh", normed_one, dvalue, preferred_element_type=jnp.float32)
    dnormed_one = (
        jnp.sum(dnormed_buf[slots_one], axis=1)
        + jnp.einsum("th,dh->td", dkey_pre, key_w, preferred_element_type=jnp.float32)
        + jnp.einsum("th,dh->td", dvalue, value_w, preferred_element_type=jnp.float32)
    )
    dnormed_one = lax.psum(dnormed_one, "tensor") + drouter_one
    dinput_part, grad_gain_one = norm_back(inputs, scale_one, gain_one, dnormed_one)
    grad_tokens = dhidden + dinput_part
    shares = (
        lax.psum_scatter(grad_gain_one, "expert", scatter_dimension=0, tiled=True),
        lax.psum_scatter(grad_route_one, "expert", scatter_dimension=0, tiled=True),
        lax.psum_scatter(grad_query, "expert", scatter_dimension=0, tiled=True),
        lax.psum_scatter(grad_key, "expert", scatter_dimension=0, tiled=True),
        lax.psum_scatter(grad_value, "expert", scatter_dimension=0, tiled=True),
        lax.psum_scatter(grad_output, "expert", scatter_dimension=0, tiled=True),
        lax.psum_scatter(grad_gain_two, "expert", scatter_dimension=0, tiled=True),
        lax.psum_scatter(grad_router_mlp, "expert", scatter_dimension=0, tiled=True),
    )
    (
        gain_share,
        route_share,
        query_share,
        key_share,
        value_share,
        output_share,
        gain_mlp_share,
        router_mlp_share,
    ) = shares
    return (
        mixed_out,
        grad_tokens,
        gain_share,
        route_share,
        query_share,
        key_share,
        value_share,
        output_share,
        gain_mlp_share,
        router_mlp_share,
        grad_gate,
        grad_up,
        grad_down,
    )


def solution(mesh):
    in_specs = (
        P("expert", None),
        P("expert", None),
        P("expert", None),
        P("expert", None),
        P("expert", None),
        P("expert"),
        P("expert", None),
        P("expert", None, "tensor"),
        P("expert", "tensor"),
        P("expert", "tensor"),
        P("expert", None, "tensor"),
        P("expert"),
        P("expert", None),
        P("expert", None, "tensor"),
        P("expert", None, "tensor"),
        P("expert", "tensor", None),
    )
    out_specs = (
        P("expert", None),
        P("expert", None),
        P("expert"),
        P("expert", None),
        P("expert", None, "tensor"),
        P("expert", "tensor"),
        P("expert", "tensor"),
        P("expert", None, "tensor"),
        P("expert"),
        P("expert", None),
        P("expert", None, "tensor"),
        P("expert", None, "tensor"),
        P("expert", "tensor", None),
    )
    return jax.shard_map(body, mesh=mesh, in_specs=in_specs, out_specs=out_specs, check_vma=False)
```

profile of v0, /device:TPU:0, one launch (start us, length us, event | category | flops | bytes accessed | tf_op | source)
XLA Modules:
  0.0 2666.0 jit_solution(10051774181518132924)
XLA Ops:
  16.6 22.3 all-gather.2
  51.3 30.6 %all_gather.31 = bf16[2048,8]{0,1:T(8,128)(2,1)S(1)} all-gather(bf16[256,8]{0,1:T(8,128)(2,1)S(1)} %copy-done.69), channel_id=1, replica_groups=mesh['expert'=8,'tensor'=4] {'expert'}, dimensions={0}, use_global_device_ids=true | all-gather | bytes 36864 | tf_op jit(solution)/shard_map/all_gather | solution.py:126
  86.1 26.4 all-gather.13.cloned.1.call-done
  115.2 226.2 %all-gather.15.cloned.1.call-done = bf16[2048,8,512]{2,0,1:T(8,128)(2,1)} async-done(((bf16[256,8,512]{2,0,1:T(8,128)(2,1)}), bf16[2048,8,512]{2,0,1:T(8,128)(2,1)}) %all-gather.15.cloned.1.call-update) | async-done | bytes 16777232 | tf_op jit(solution)/shard_map/all_gather | solution.py:127
  341.4 9.5 fusion.19
  360.4 209.4 %all-gather.17.cloned.1.call-done = bf16[2048,8,512]{2,0,1:T(8,128)(2,1)} async-done(((bf16[256,8,512]{2,0,1:T(8,128)(2,1)}), bf16[2048,8,512]{2,0,1:T(8,128)(2,1)}) %all-gather.17.cloned.1.call-update) | async-done | bytes 16777232 | tf_op jit(solution)/shard_map/all_gather | solution.py:130
  569.8 13.7 fusion.50
  599.4 17.6 all-gather.3
  635.6 30.4 %all_gather.37 = bf16[2048,8]{0,1:T(8,128)(2,1)S(1)} all-gather(bf16[256,8]{0,1:T(8,128)(2,1)S(1)} %copy-done.70), channel_id=1, replica_groups=mesh['expert'=8,'tensor'=4] {'expert'}, dimensions={0}, use_global_device_ids=true | all-gather | bytes 36864 | tf_op jit(solution)/shard_map/all_gather | solution.py:132
  666.6 14.8 all-reduce.6.cloned.1.call-done
  681.3 8.9 multiply_reduce_fusion.3
  709.1 76.1 %all_to_all.20 = bf16[4,8,24,2048]{3,2,0,1:T(8,128)(2,1)} all-to-all(bf16[4,8,24,2048]{3,2,0,1:T(8,128)(2,1)S(1)} %get-tuple-element.122), channel_id=1, replica_groups=mesh['expert'=8,'tensor'=4] {'expert'}, dimensions={1} | all-to-all | bytes 6291456 | tf_op jit(solution)/shard_map/all_to_all | solution.py:83
  792.7 9.3 fusion
  802.0 57.1 %all-to-all-done = bf16[4,8,24,2048]{3,2,0,1:T(8,128)(2,1)S(1)} async-done(((bf16[4,8,24,2048]{3,2,0,1:T(8,128)(2,1)}), bf16[4,8,24,2048]{3,2,0,1:T(8,128)(2,1)S(1)}, u32[]{:S(2)}, u32[]{:S(2)}) %all-to-all-start) | async-done | bytes 3145760 | tf_op jit(solution)/shard_map/all_to_all | solution.py:83
  900.2 41.7 %reduce-scatter.9.cloned.1.call-done = f32[192,2048]{1,0:T(8,128)} async-done(((f32[768,2048]{1,0:T(8,128)}), f32[192,2048]{1,0:T(8,128)}) %reduce-scatter.9.cloned.1.call-update) | async-done | bytes 1572880 | tf_op jit(solution)/shard_map/reduce_scatter | solution.py:91
  941.9 42.5 %all_to_all.21 = f32[8,24,2048]{2,1,0:T(8,128)S(1)} all-to-all(f32[8,24,2048]{2,1,0:T(8,128)} %bitcast.202), channel_id=1, replica_groups=mesh['expert'=8,'tensor'=4] {'expert'}, dimensions={0} | all-to-all | bytes 3145728 | tf_op jit(solution)/shard_map/all_to_all | solution.py:87
  985.5 18.0 reduce-scatter.11.cloned.1.call-done
  1003.4 42.6 %all_to_all.22 = f32[8,24,2048]{2,1,0:T(8,128)} all-to-all(f32[8,24,2048]{2,1,0:T(8,128)} %bitcast.201), channel_id=1, replica_groups=mesh['expert'=8,'tensor'=4] {'expert'}, dimensions={0} | all-to-all | bytes 3145728 | tf_op jit(solution)/shard_map/all_to_all | solution.py:87
  1061.7 10.9 multiply_reduce_fusion.1
  1072.7 18.0 all-gather.21.cloned.1.call-done
  1138.4 9.6 fusion.16
  1161.7 13.9 fusion.47
  1202.9 14.8 convolution_bitcast_fusion.1
  1219.7 14.7 convolution_bitcast_fusion
  1252.3 10.1 convolution_bitcast_fusion.4
  1282.2 39.3 %all-reduce.2 = (f32[2048]{0:T(1024)S(1)}, f32[2048]{0:T(1024)S(1)}) all-reduce(f32[2048]{0:T(1024)S(1)} %get-tuple-element.95, f32[2048]{0:T(1024)S(1)} %copy-done.53), channel_id=6, replica_groups=mesh['expert'=8,'tensor'=4] {'expert'}, use_global_device_ids=true, to_apply=%region_38.39.clone | all-reduce | flops 4096 | bytes 32768
  1326.4 475.5 %reduce-scatter.15.cloned.1.call-done = f32[256,8,512]{0,2,1:T(8,128)} async-done(((f32[2048,8,512]{0,2,1:T(8,128)}), f32[256,8,512]{0,2,1:T(8,128)}) %reduce-scatter.15.cloned.1.call-update) | async-done | bytes 4194320 | tf_op jit(solution)/shard_map/reduce_scatter | solution.py:310
  1807.4 540.2 %reduce-scatter.21.cloned.1.call-done = f32[256,8,512]{0,2,1:T(8,128)} async-done(((f32[2048,8,512]{0,2,1:T(8,128)}), f32[256,8,512]{0,2,1:T(8,128)}) %reduce-scatter.21.cloned.1.call-update) | async-done | bytes 4194320 | tf_op jit(solution)/shard_map/reduce_scatter | solution.py:313
  2353.1 58.9 %reduce-scatter.23.cloned.1.call-done = f32[256,8]{0,1:T(8,128)} async-done(((f32[2048,8]{0,1:T(8,128)}), f32[256,8]{0,1:T(8,128)}) %reduce-scatter.23.cloned.1.call-update) | async-done | bytes 8208 | tf_op jit(solution)/shard_map/reduce_scatter | solution.py:315
  2411.9 64.1 %reduce-scatter.13.cloned.1.call-done = f32[256,8]{0,1:T(8,128)} async-done(((f32[2048,8]{0,1:T(8,128)}), f32[256,8]{0,1:T(8,128)}) %reduce-scatter.13.cloned.1.call-update) | async-done | bytes 8208 | tf_op jit(solution)/shard_map/reduce_scatter | solution.py:309
  2476.1 91.1 %reduce-scatter.17.cloned.1.call-done = f32[256,512]{1,0:T(8,128)} async-done(((f32[2048,512]{1,0:T(8,128)}), f32[256,512]{1,0:T(8,128)}) %reduce-scatter.17.cloned.1.call-update) | async-done | bytes 524304 | tf_op jit(solution)/shard_map/reduce_scatter | solution.py:311
  2567.1 92.2 %reduce-scatter.19.cloned.1.call-done = f32[256,512]{1,0:T(8,128)} async-done(((f32[2048,512]{1,0:T(8,128)}), f32[256,512]{1,0:T(8,128)}) %reduce-scatter.19.cloned.1.call-update) | async-done | bytes 524304 | tf_op jit(solution)/shard_map/reduce_scatter | solution.py:312
  (388 shorter events, 299.7 us)
Async XLA Ops:
  7.2 76.5 %all-gather.11.cloned.1.call-start = ((), (), s32[]{:S(2)}) async-start(), calls=%async_computation.12 | async-start | bytes 2359296 | tf_op jit(solution)/shard_map/all_gather | solution.py:129
  7.9 104.6 %all-gather.13.cloned.1.call-start = ((), (), s32[]{:S(2)}) async-start(), calls=%async_computation.13 | async-start | bytes 2359296 | tf_op jit(solution)/shard_map/all_gather | solution.py:128
  8.7 332.7 %all-gather.15.cloned.1.call-start = ((), (), s32[]{:S(2)}) async-start(), calls=%async_computation.14 | async-start | bytes 18874368 | tf_op jit(solution)/shard_map/all_gather | solution.py:127
  12.3 34.1 %copy-start.14 = (bf16[256,2048]{1,0:T(8,128)(2,1)S(1)}, bf16[256,2048]{1,0:T(8,128)(2,1)}, u32[]{:S(2)}) copy-start(bf16[256,2048]{1,0:T(8,128)(2,1)} %param.16) | copy-start | bytes 3145732
  12.3 557.5 %all-gather.17.cloned.1.call-start = ((), (), s32[]{:S(2)}) async-start(), calls=%async_computation.15 | async-start | bytes 18874368 | tf_op jit(solution)/shard_map/all_gather | solution.py:130
  16.1 665.3 %all-reduce.6.cloned.1.call-start = ((), (), s32[]{:S(2)}) async-start(), calls=%async_computation.16 | async-start | bytes 8388608 | tf_op jit(solution)/shard_map/psum | solution.py:177
  46.2 523.6 %copy-start.34 = (bf16[8,96]{1,0:T(8,128)(2,1)}, bf16[8,96]{1,0:T(8,128)(2,1)S(1)}, u32[]{:S(2)}) copy-start(bf16[8,96]{1,0:T(8,128)(2,1)S(1)} %mul.534) | copy-start | bytes 4612
  46.4 311.3 %copy-start.51 = (s32[1024]{0:T(1024)}, s32[1024]{0:T(1024)S(1)}, u32[]{:S(2)}) copy-start(s32[1024]{0:T(1024)S(1)} %get-tuple-element.142) | copy-start | bytes 12292
  47.1 65.5 %copy-start = (bf16[256,2048]{1,0:T(8,128)(2,1)}, bf16[256,2048]{1,0:T(8,128)(2,1)S(1)}, u32[]{:S(2)}) copy-start(bf16[256,2048]{1,0:T(8,128)(2,1)S(1)} %fusion.23) | copy-start | bytes 3145732
  47.1 36.1 %copy-start.71 = (s32[1,256]{1,0:T(1,128)S(1)}, s32[1,256]{1,0:T(1,128)}, u32[]{:S(2)}) copy-start(s32[1,256]{1,0:T(1,128)} %param.18) | copy-start | bytes 3076
  81.9 501.6 %copy-start.6 = (s32[1024]{0:T(1024)}, s32[1024]{0:T(1024)S(1)}, u32[]{:S(2)}) copy-start(s32[1024]{0:T(1024)S(1)} %pad_clamp_fusion.4) | copy-start | bytes 12292
  86.0 269.6 %copy-start.30 = (bf16[256,4,128]{2,1,0:T(4,128)(2,1)}, bf16[256,4,128]{2,1,0:T(4,128)(2,1)S(1)}, u32[]{:S(2)}) copy-start(bf16[256,4,128]{2,1,0:T(4,128)(2,1)S(1)} %reshape.710) | copy-start | bytes 786436
  115.2 238.8 %copy-start.32 = (bf16[256,4,128,1]{0,2,3,1:T(8,128)(2,1)}, bf16[256,4,128,1]{0,2,3,1:T(8,128)(2,1)S(1)}, u32[]{:S(2)}) copy-start(bf16[256,4,128,1]{0,2,3,1:T(8,128)(2,1)S(1)} %fusion.62) | copy-start | bytes 786436
  360.4 223.1 %copy-start.17 = (bf16[768,512]{1,0:T(8,128)(2,1)}, bf16[768,512]{1,0:T(8,128)(2,1)S(1)}, u32[]{:S(2)}) copy-start(bf16[768,512]{1,0:T(8,128)(2,1)S(1)} %gather_fusion.2) | copy-start | bytes 2359300
  597.5 19.5 copy-start.19
  598.2 29.5 %copy-start.49 = (f32[256,2]{0,1:T(2,128)}, f32[256,2]{0,1:T(2,128)S(1)}, u32[]{:S(2)}) copy-start(f32[256,2]{0,1:T(2,128)S(1)} %select_reduce_fusion.3) | copy-start | bytes 6148
  598.6 29.0 %copy-start.55 = (f32[256]{0:T(256)}, f32[256]{0:T(256)S(1)}, u32[]{:S(2)}) copy-start(f32[256]{0:T(256)S(1)} %reduce_max.27) | copy-start | bytes 3076
  666.0 26.3 copy-start.43
  666.6 23.7 copy-start.15
  785.2 73.8 %all-to-all-start = ((bf16[4,8,24,2048]{3,2,0,1:T(8,128)(2,1)}), bf16[4,8,24,2048]{3,2,0,1:T(8,128)(2,1)S(1)}, u32[]{:S(2)}, u32[]{:S(2)}) async-start(bf16[4,8,24,2048]{3,2,0,1:T(8,128)(2,1)} %get-tuple-element.123), calls=%async_computation | async-start | bytes 6291456 | tf_op jit(solution)/shard_map/all_to_all | solution.py:83
  788.9 153.1 %reduce-scatter.9.cloned.1.call-start = ((), (), s32[]{:S(2)}) async-start(), calls=%async_computation.17 | async-start | bytes 7864320 | tf_op jit(solution)/shard_map/reduce_scatter | solution.py:91
  884.8 118.6 %reduce-scatter.11.cloned.1.call-start = ((), (), s32[]{:S(2)}) async-start(), calls=%async_computation.18 | async-start | bytes 7864320 | tf_op jit(solution)/shard_map/reduce_scatter | solution.py:91
  900.1 148.5 %all-gather.19.cloned.1.call-start = ((), (), s32[]{:S(2)}) async-start(), calls=%async_computation.26 | async-start | bytes 3932160 | tf_op jit(solution)/shard_map/all_gather | solution.py:209
  985.4 60.7 %copy-start.20 = (bf16[256,2048]{1,0:T(8,128)(2,1)S(1)}, bf16[256,2048]{1,0:T(8,128)(2,1)}, u32[]{:S(2)}) copy-start(bf16[256,2048]{1,0:T(8,128)(2,1)} %param.17) | copy-start | bytes 3145732
  985.4 105.3 %all-gather.21.cloned.1.call-start = ((), (), s32[]{:S(2)}) async-start(), calls=%async_computation.27 | async-start | bytes 7864320 | tf_op jit(solution)/shard_map/all_gather | solution.py:244
  1046.1 231.7 %all-reduce.8.cloned.1.call-start = ((), (), s32[]{:S(2)}) async-start(), calls=%async_computation.19 | async-start | bytes 4194304 | tf_op jit(solution)/shard_map/psum | solution.py:304
  1202.7 599.1 %reduce-scatter.15.cloned.1.call-start = ((), (), s32[]{:S(2)}) async-start(), calls=%async_computation.21 | async-start | bytes 37748736 | tf_op jit(solution)/shard_map/reduce_scatter | solution.py:310
  1217.7 1129.8 %reduce-scatter.21.cloned.1.call-start = ((), (), s32[]{:S(2)}) async-start(), calls=%async_computation.24 | async-start | bytes 37748736 | tf_op jit(solution)/shard_map/reduce_scatter | solution.py:313
  1234.4 1177.6 %reduce-scatter.23.cloned.1.call-start = ((), (), s32[]{:S(2)}) async-start(), calls=%async_computation.25 | async-start | bytes 73728 | tf_op jit(solution)/shard_map/reduce_scatter | solution.py:315
  1236.8 1239.2 %reduce-scatter.13.cloned.1.call-start = ((), (), s32[]{:S(2)}) async-start(), calls=%async_computation.20 | async-start | bytes 73728 | tf_op jit(solution)/shard_map/reduce_scatter | solution.py:309
  1243.9 1323.2 %reduce-scatter.17.cloned.1.call-start = ((), (), s32[]{:S(2)}) async-start(), calls=%async_computation.22 | async-start | bytes 4718592 | tf_op jit(solution)/shard_map/reduce_scatter | solution.py:311
  1246.7 1412.6 %reduce-scatter.19.cloned.1.call-start = ((), (), s32[]{:S(2)}) async-start(), calls=%async_computation.23 | async-start | bytes 4718592 | tf_op jit(solution)/shard_map/reduce_scatter | solution.py:312
  (72 other events, 397.6 us)
Sparse Core Ops, SparseCore 0:
  10.1 52.3 all-gather.10
  64.6 47.8 all-gather.12
  115.3 226.0 all-gather.14
  344.0 225.7 all-gather.16
  597.6 83.6 all-reduce.5
  885.0 56.9 reduce-scatter.8
  945.0 58.3 reduce-scatter.10
  1005.6 28.5 all-gather.18
  1046.2 44.4 all-gather.20
  1202.9 51.3 all-reduce.7
  1258.0 543.7 reduce-scatter.14
  1805.5 542.0 reduce-scatter.20
  2351.5 60.3 reduce-scatter.22
  2415.7 60.2 reduce-scatter.12
  2480.1 86.9 reduce-scatter.16
  2571.6 87.6 reduce-scatter.18
where the time goes:
time: 2680 us; the launch traced here: 2670 us
  waiting for transfers between devices  1940 us (72%)
  blocking collectives  301 us (11%)
  matrix products  179 us (7%)
  local copies, waits for them, and re-layouts  162 us (6%)
  other arithmetic  67.7 us (3%)
    reduce_scatter x1, waiting for transfers between devices, body(): lax.psum_scatter(grad_output, 'expert', scatter_dimension=0, tiled=True)  540 us
    reduce_scatter x1, waiting for transfers between devices, body(): lax.psum_scatter(grad_query, 'expert', scatter_dimension=0, tiled=True)  475 us
    all_gather x1, waiting for transfers between devices, body(): lax.all_gather(w_query, 'expert', axis=0, tiled=True)  226 us
    all_gather x1, waiting for transfers between devices, body(): lax.all_gather(w_output, 'expert', axis=0, tiled=True)  209 us
    reduce_scatter x1, waiting for transfers between devices, body(): lax.psum_scatter(grad_value, 'expert', scatter_dimension=0, tiled=True)  92.2 us
    reduce_scatter x1, waiting for transfers between devices, body(): lax.psum_scatter(grad_key, 'expert', scatter_dimension=0, tiled=True)  91.1 us
    all_to_all x2, blocking collectives, from_owners(): lax.all_to_all(slot_rows, 'expert', split_axis=0, concat_axis=0, tiled=True)  85.1 us
    all_to_all x1, blocking collectives, to_owners(): lax.all_to_all(slot_rows, 'expert', split_axis=1, concat_axis=1, tiled=True)  76.1 us
  transfers between devices with their start and end apart: 17, of which 14 were waited for; matrix products, arithmetic and copies ran while one was open for 8% of the time, Pallas kernels for 0%

commit v1 on v0

v1 whole, which is shorter than its diff:
```python
import functools

import jax
import jax.numpy as jnp
from jax import lax
from jax.experimental import pallas as pl
from jax.experimental.pallas import tpu as pltpu
from jax.sharding import PartitionSpec as P

D = 2048
HEAD_DIM = 128
EA = 8
EXPERTS = 8
CAP = 96
EPSILON = 1e-05
ROTARY_BASE = 10000.0
VMEM = 56 * 1024 * 1024
F32 = jnp.float32
BF16 = jnp.bfloat16
PRECISE = lax.Precision.HIGHEST


def hop(values, axis, bit):
    size = lax.axis_size(axis)
    return lax.ppermute(values, axis, [(i, i ^ bit) for i in range(size)])


def bits_of(axis):
    size, bits = lax.axis_size(axis), []
    while 1 << len(bits) < size:
        bits.append(1 << len(bits))
    return bits[::-1]


def gather_pieces(values, axis, bits=None):
    pieces = {0: values}
    for bit in bits_of(axis) if bits is None else bits:
        for known in sorted(pieces):
            pieces[known | bit] = hop(pieces[known], axis, bit)
    return pieces


def scatter_sum(chunks, axis, bits=None, sent_as=None):
    held, came = dict(chunks), []
    for bit in (bits_of(axis) if bits is None else bits)[::-1]:
        for k in sorted(held, reverse=True):
            if k & bit:
                sent = held.pop(k)
                came.append(hop(sent.astype(sent_as or sent.dtype), axis, bit))
                held[k ^ bit] = held[k ^ bit].astype(F32) + came[-1].astype(F32)
                if k ^ bit:
                    held[k ^ bit] = held[k ^ bit].astype(sent_as or sent.dtype)
    return held[0], came


def after(values, *earlier):
    return lax.optimization_barrier((values, *earlier))[0]


def whole_spec(shape):
    zeros = (0,) * len(shape)
    return pl.BlockSpec(shape, lambda *_: zeros)


def params(*arrays):
    held = 3 * sum(one.size * one.dtype.itemsize for one in arrays) + (12 << 20)
    return pltpu.CompilerParams(vmem_limit_bytes=min(VMEM, held) if arrays else 16 << 20)


def one_of(routes, kind):
    return (routes == kind).astype(F32).astype(BF16)


def map_of(refs, kind):
    each = EA // len(refs)
    return refs[kind // each][kind % each]


def project_kernel(which, counts, *refs):
    x_refs, refs = refs[: len(counts)], refs[len(counts) :]
    w_refs = []
    for count in counts:
        w_refs.append(refs[:count])
        refs = refs[count:]
    routes_ref, outs = refs[0], refs[1:]
    for at, k in enumerate(which):
        routes = routes_ref[k // 2]
        for choice in range(2):
            total = jnp.zeros(outs[0].shape, F32)
            for x_ref, maps in zip(x_refs, w_refs):
                x = x_ref[k // 2]
                each = EA // len(maps)
                for first, w_ref in zip(range(0, EA, each), maps):
                    spread = jnp.concatenate(
                        [
                            x * one_of(routes[:, choice : choice + 1], kind)
                            for kind in range(first, first + each)
                        ],
                        axis=1,
                    )
                    flat = w_ref[...].reshape(each * x.shape[1], w_ref.shape[2])
                    total += jnp.dot(spread, flat, preferred_element_type=F32)
            outs[2 * at + choice][...] = total.astype(outs[0].dtype)


def project(which, xs, ws, routes, dtype):
    _, length, depth = xs[0].shape
    width = ws[0][0].shape[2]
    outs = [jax.ShapeDtypeStruct((length, width), dtype)] * (2 * len(which))
    maps = [one for side in ws for one in side]
    return pl.pallas_call(
        functools.partial(project_kernel, which, [len(side) for side in ws]),
        out_shape=outs,
        compiler_params=params(*xs, *maps, *outs),
    )(*xs, *maps, routes)


def contract_kernel(which, counts, parts, routes_ref, *refs):
    w_refs = []
    for count in counts:
        w_refs.append(refs[:count])
        refs = refs[count:]
    rows, outs = refs[: 2 * len(which)], refs[2 * len(which) :]
    share, depth = outs[0].shape[1], w_refs[0][0].shape[1]
    turned = (((1,), (1,)), ((), ()))
    for at, k in enumerate(which):
        routes = routes_ref[k // 2]
        first, second = rows[2 * at][...], rows[2 * at + 1][...]
        totals = [jnp.zeros((share * parts, depth), F32)] * len(counts)
        for kind in range(EA):
            ones = one_of(routes, kind)
            picked = first * ones[:, 0:1] + second * ones[:, 1:2]
            totals = [
                total
                + lax.dot_general(picked, map_of(maps, kind), turned, preferred_element_type=F32)
                for total, maps in zip(totals, w_refs)
            ]
        for b, total in enumerate(totals):
            for r in range(parts):
                outs[r][at, :, b * depth : (b + 1) * depth] = total[
                    r * share : (r + 1) * share
                ].astype(outs[r].dtype)


def contract(which, pieces, routes, ws, parts):
    rows = [half for k in which for half in pieces[k]]
    _, length, _ = routes.shape
    depth, width = ws[0][0].shape[1:]
    shape = (len(which), length // parts, depth * len(ws))
    maps = [one for side in ws for one in side]
    return pl.pallas_call(
        functools.partial(contract_kernel, which, [len(side) for side in ws], parts),
        out_shape=[
            jax.ShapeDtypeStruct(shape, BF16 if r % 2 else F32) for r in range(parts)
        ],
        compiler_params=params(*maps, *rows),
    )(routes, *maps, *rows)


def to_owners(pieces, routes, ws, parts, ties=((), ())):
    came, order = {}, sorted(pieces)
    for which, tie in zip((order[:-1], order[-1:]), ties):
        chunks = dict(enumerate(contract(tuple(which), pieces, after(routes, *tie), ws, parts)))
        summed, _ = scatter_sum(chunks, "tensor", None, BF16)
        for at, k in enumerate(which):
            came[k] = hop(summed[at].astype(BF16), "expert", k) if k else summed[at]
    return came


def arrange_kernel(parts, places, x_ref, out_ref):
    count, length, depth = out_ref.shape
    share = length // parts
    for r in range(parts):
        spot = pl.ds(pl.multiple_of((places[1] ^ r) * share, share), share)
        for j in range(count):
            out_ref[places[0] ^ j, r * share : (r + 1) * share, :] = x_ref[
                spot, j * depth : (j + 1) * depth
            ]


def arrange(places, x, parts, count):
    shape = (count, x.shape[0], x.shape[1] // count)
    return pl.pallas_call(
        functools.partial(arrange_kernel, parts),
        out_shape=jax.ShapeDtypeStruct(shape, BF16),
        grid_spec=pltpu.PrefetchScalarGridSpec(
            num_scalar_prefetch=1,
            grid=(1,),
            in_specs=[whole_spec(x.shape)],
            out_specs=whole_spec(shape),
        ),
        compiler_params=params(x),
    )(places, x)


def pack_kernel(parts, places, x_ref, routes_ref, blocks_ref, scale_ref, *outs):
    count, length, depth = blocks_ref.shape
    share = length // parts
    for r in range(parts):
        spot = pl.ds(pl.multiple_of((places[1] ^ r) * share, share), share)
        rows = slice(r * share, (r + 1) * share)
        squares = jnp.zeros((share, 1), F32)
        for j in range(count):
            block = x_ref[spot, j * depth : (j + 1) * depth]
            blocks_ref[places[0] ^ j, rows, :] = block
            wide = block.astype(F32)
            squares += jnp.sum(wide * wide, axis=1, keepdims=True)
        scale = lax.rsqrt(squares / D + EPSILON)
        scale_ref[rows, :] = scale
        if r == 0:
            high = scale.astype(BF16).astype(F32)
            middle = (scale - high).astype(BF16).astype(F32)
            routes = routes_ref[spot, :].astype(F32)
            columns = [routes[:, 0:1], routes[:, 1:2], high, middle, scale - high - middle]
            lane = lax.broadcasted_iota(jnp.int32, (share, 128), 1)
            extra = jnp.zeros((share, 128), F32)
            for at, column in enumerate(columns):
                extra = jnp.where(lane == at, column, extra)
    for at, out_ref in enumerate(outs):
        for b in range(2):
            out_ref[:, b * depth : (b + 1) * depth] = blocks_ref[2 * at + b, :share, :]
        out_ref[:, 2 * depth :] = extra.astype(BF16)


def pack(places, x, routes, parts, count):
    length, depth = x.shape[0], x.shape[1] // count
    shapes = [(count, length, depth), (length, 1)]
    shapes += [(length // parts, 2 * depth + 128)] * (count // 2)
    types = [BF16, F32] + [BF16] * (count // 2)
    blocks, scale, *chunks = pl.pallas_call(
        functools.partial(pack_kernel, parts),
        out_shape=[jax.ShapeDtypeStruct(*one) for one in zip(shapes, types)],
        grid_spec=pltpu.PrefetchScalarGridSpec(
            num_scalar_prefetch=1,
            grid=(1,),
            in_specs=[whole_spec(x.shape), whole_spec(routes.shape)],
            out_specs=[whole_spec(one) for one in shapes],
        ),
        compiler_params=params(x),
    )(places, x, routes)
    return blocks, scale, chunks


def unpack_kernel(parts, *refs):
    pieces, (gain_ref, *outs, routes_ref) = refs[:parts], refs[parts:]
    share, depth = pieces[0].shape[1], outs[0].shape[2]
    for r, piece in enumerate(pieces):
        rows = slice(r * share, (r + 1) * share)
        for k in range(piece.shape[0]):
            extra = piece[k, :, 2 * depth :].astype(F32)
            scale = extra[:, 2:3] + extra[:, 3:4] + extra[:, 4:5]
            routes_ref[k, rows, :] = extra[:, 0:2].astype(jnp.int32)
            for b, out_ref in enumerate(outs):
                values = piece[k, :, b * depth : (b + 1) * depth].astype(F32)
                out_ref[k, rows, :] = (values * scale * gain_ref[b : b + 1, :]).astype(BF16)


def unpack(pieces, gains):
    count, share, _ = pieces[0].shape
    shape = (count, share * len(pieces), gains.shape[1])
    return pl.pallas_call(
        functools.partial(unpack_kernel, len(pieces)),
        out_shape=[
            *[jax.ShapeDtypeStruct(shape, BF16)] * 2,
            jax.ShapeDtypeStruct((*shape[:2], 2), jnp.int32),
        ],
        compiler_params=params(*pieces, *pieces),
    )(*pieces, gains)


def assemble_kernel(parts, *refs):
    pieces, outs = refs[:parts], refs[parts:]
    _, share, both = pieces[0].shape
    depth = both // 2
    for r, piece in enumerate(pieces):
        for b, out_ref in enumerate(outs):
            out_ref[:, r * share : (r + 1) * share, :] = piece[:, :, b * depth : (b + 1) * depth]


def assemble(pieces):
    count, share, both = pieces[0].shape
    shape = (count, share * len(pieces), both // 2)
    return pl.pallas_call(
        functools.partial(assemble_kernel, len(pieces)),
        out_shape=[jax.ShapeDtypeStruct(shape, BF16)] * 2,
        compiler_params=params(*pieces, *pieces),
    )(*pieces)


def output_kernel(parts, places, *refs):
    pieces, out_ref = refs[:parts], refs[-1]
    count, share, depth = pieces[0].shape
    for r, piece in enumerate(pieces):
        spot = pl.ds(pl.multiple_of((places[1] ^ r) * share, share), share)
        for j in range(count):
            out_ref[spot, j * depth : (j + 1) * depth] = piece[places[0] ^ j].astype(out_ref.dtype)


def output_rows(places, pieces, dtype):
    pieces = [pieces[r] for r in sorted(pieces)]
    count, share, depth = pieces[0].shape
    shape = (share * len(pieces), count * depth)
    return pl.pallas_call(
        functools.partial(output_kernel, len(pieces)),
        out_shape=jax.ShapeDtypeStruct(shape, dtype),
        grid_spec=pltpu.PrefetchScalarGridSpec(
            num_scalar_prefetch=1,
            grid=(1,),
            in_specs=[whole_spec(one.shape) for one in pieces],
            out_specs=whole_spec(shape),
        ),
        compiler_params=params(*pieces, *pieces),
    )(places, *pieces)


def hidden_kernel(own_ref, gain_ref, *refs):
    came, (hidden_ref, scale_ref, normed_ref) = refs[:-3], refs[-3:]
    depth = own_ref.shape[2]
    squares = 0.0
    for at, one in enumerate(came):
        for b in range(2):
            hidden = own_ref[2 * at + b].astype(F32) + one[:, b * depth : (b + 1) * depth].astype(F32)
            hidden_ref[2 * at + b] = hidden
            squares += jnp.sum(hidden * hidden, axis=1, keepdims=True)
    scale = lax.rsqrt(squares / D + EPSILON)
    scale_ref[...] = scale
    for j in range(2 * len(came)):
        normed_ref[j] = (hidden_ref[j] * scale * gain_ref[j]).astype(BF16)


def hidden_rows(own, gain, came):
    came = [came[k] for k in sorted(came)]
    count, share, depth = own.shape
    return pl.pallas_call(
        hidden_kernel,
        out_shape=[
            jax.ShapeDtypeStruct(own.shape, F32),
            jax.ShapeDtypeStruct((share, 1), F32),
            jax.ShapeDtypeStruct(own.shape, BF16),
        ],
        compiler_params=params(own, own, own, own),
    )(own, gain, *came)


def dispatch_kernel(parts, places, slot_ref, routes_ref, router_ref, up_ref, *refs):
    pieces, (rows_ref, grads_ref, gates_ref) = refs[:parts], refs[parts:]
    count, _, depth = pieces[0].shape
    slots, length = rows_ref.shape[0], slot_ref.shape[1]
    logits = jnp.zeros((EXPERTS, length), F32)
    for j in range(count):
        block = jnp.concatenate([piece[j] for piece in pieces])
        logits += lax.dot_general(
            router_ref[j], block, (((1,), (1,)), ((), ())), preferred_element_type=F32
        )
    kinds = lax.broadcasted_iota(jnp.int32, (EXPERTS, length), 0)
    picked = [
        jnp.sum(jnp.where(kinds == routes_ref[c : c + 1, :], logits, 0.0), axis=0, keepdims=True)
        for c in range(2)
    ]
    top = jnp.maximum(picked[0], picked[1])
    powers = [jnp.exp(one - top) for one in picked]
    gates = [one / (powers[0] + powers[1]) for one in powers]
    slot_at = lax.broadcasted_iota(jnp.int32, (slots, length), 0)
    here = [slot_at == slot_ref[c : c + 1, :] for c in range(2)]
    gate = jnp.where(here[0], gates[0], jnp.where(here[1], gates[1], 0.0))
    gate = jnp.sum(gate, axis=1, keepdims=True)
    place = jnp.where(here[0] | here[1], 1.0, 0.0).astype(BF16)
    for j in range(count):
        lanes = slice(j * depth, (j + 1) * depth)
        block = jnp.concatenate([piece[places[0] ^ j] for piece in pieces])
        rows_ref[:, lanes] = jnp.dot(place, block, preferred_element_type=F32).astype(BF16)
        grads = jnp.dot(place, up_ref[places[0] ^ j], preferred_element_type=F32)
        grads_ref[:, lanes] = (grads * gate).astype(BF16)
    for c in range(2):
        gates_ref[c : c + 1, :] = gates[c]


def dispatch(places, slot, routes, router, up, pieces, slots):
    pieces = [pieces[r] for r in sorted(pieces)]
    operands = (slot, routes, router, up, *pieces)
    shapes = [(slots, D), (slots, D), slot.shape]
    return pl.pallas_call(
        functools.partial(dispatch_kernel, len(pieces)),
        out_shape=[
            jax.ShapeDtypeStruct(shape, dtype) for shape, dtype in zip(shapes, (BF16, BF16, F32))
        ],
        grid_spec=pltpu.PrefetchScalarGridSpec(
            num_scalar_prefetch=1,
            grid=(1,),
            in_specs=[whole_spec(one.shape) for one in operands],
            out_specs=[whole_spec(shape) for shape in shapes],
        ),
        compiler_params=params(up, up, *pieces),
    )(places, *operands)


def combine_kernel(parts, weigh, places, slot_ref, values_ref, *refs):
    extra, outs = refs[: 2 * weigh], refs[2 * weigh :]
    count, share, depth = outs[0].shape
    slots, length = values_ref.shape[0], slot_ref.shape[1]
    slot_at = lax.broadcasted_iota(jnp.int32, (slots, length), 0)
    here = [slot_at == slot_ref[c : c + 1, :] for c in range(2)]
    if weigh:
        gates_ref, grads_ref = extra
        place = jnp.where(
            here[0], gates_ref[0:1, :], jnp.where(here[1], gates_ref[1:2, :], 0.0)
        ).astype(BF16)
        weighted = jnp.sum(
            values_ref[...].astype(F32) * grads_ref[...].astype(F32), axis=1, keepdims=True
        )
        for c in range(2):
            outs[-1][c : c + 1, :] = jnp.sum(
                jnp.where(here[c], weighted, 0.0), axis=0, keepdims=True
            )
    else:
        place = jnp.where(here[0] | here[1], 1.0, 0.0).astype(BF16)
    over_slots = (((0,), (0,)), ((), ()))
    for j in range(count):
        total = lax.dot_general(
            place, values_ref[:, j * depth : (j + 1) * depth], over_slots, preferred_element_type=F32
        ).astype(BF16)
        for r in range(parts):
            outs[r][places[0] ^ j] = total[r * share : (r + 1) * share]


def combine(places, slot, values, parts, count, *extra):
    slots, length = values.shape[0], slot.shape[1]
    shape = (count, length // parts, D // count)
    outs = [jax.ShapeDtypeStruct(shape, BF16)] * parts
    outs += [jax.ShapeDtypeStruct((2, length), F32)] * bool(extra)
    operands = (slot, values, *extra)
    return pl.pallas_call(
        functools.partial(combine_kernel, parts, 1 if extra else 0),
        out_shape=outs,
        grid_spec=pltpu.PrefetchScalarGridSpec(
            num_scalar_prefetch=1,
            grid=(1,),
            in_specs=[whole_spec(one.shape) for one in operands],
            out_specs=[whole_spec(one.shape) for one in outs],
        ),
        compiler_params=params(values, *extra, *outs),
    )(places, *operands)


def map_grads_kernel(n_x, n_sides, *refs):
    x_refs, routes_refs = refs[:n_x], refs[n_x : n_x + n_sides]
    outs, (turned, picked) = refs[-2 - n_x // n_sides : -2], refs[-2:]
    rows = refs[n_x + n_sides : -2 - n_x // n_sides]
    count, length, depth = x_refs[0].shape
    blocks = n_x // n_sides
    for at, x_ref in enumerate(x_refs):
        side, block = at // blocks, at % blocks
        for k in range(count):
            here = slice((side * count + k) * length, (side * count + k + 1) * length)
            turned[block * depth : (block + 1) * depth, here] = x_ref[k].T
    for kind in range(EA):
        for side, routes_ref in enumerate(routes_refs):
            for k in range(count):
                ones = one_of(routes_ref[k], kind)
                at = side * count + k
                picked[at * length : (at + 1) * length, :] = (
                    rows[2 * at][...] * ones[:, 0:1] + rows[2 * at + 1][...] * ones[:, 1:2]
                )
        for block, out_ref in enumerate(outs):
            out_ref[:, kind, :] = jnp.dot(
                turned[block * depth : (block + 1) * depth, :],
                picked[...],
                preferred_element_type=F32,
            ).astype(out_ref.dtype)


def map_grads(sides, routes, rows, dtypes):
    xs = [x for side in sides for x in side]
    count, length, depth = xs[0].shape
    width = rows[0].shape[1]
    total = len(sides) * count * length
    return pl.pallas_call(
        functools.partial(map_grads_kernel, len(xs), len(sides)),
        out_shape=[jax.ShapeDtypeStruct((depth, EA, width), dtype) for dtype in dtypes],
        scratch_shapes=[
            pltpu.VMEM((depth * len(dtypes), total), BF16),
            pltpu.VMEM((total, width), BF16),
        ],
        compiler_params=pltpu.CompilerParams(vmem_limit_bytes=VMEM),
    )(*xs, *routes, *rows)


def turn(values, cosine, sine):
    return values * cosine + pltpu.roll(values, HEAD_DIM // 2, 1) * sine


def rows_kernel(x_ref, *refs):
    pieces, out_ref = refs[:-1], refs[-1]
    total = jnp.zeros(out_ref.shape, F32)
    for j, piece in enumerate(pieces):
        total += jnp.dot(x_ref[j], piece[...], preferred_element_type=F32)
    out_ref[...] = total


def dense_rows(x, pieces):
    _, length, depth = x.shape
    width = pieces[0].shape[1]
    return pl.pallas_call(
        rows_kernel,
        out_shape=jax.ShapeDtypeStruct((length, width), F32),
        compiler_params=params(x, *pieces),
    )(x, *pieces)


def rows_back_kernel(drows_ref, *refs):
    pieces, out_ref = refs[:-1], refs[-1]
    parts, share = out_ref.shape[0], out_ref.shape[2]
    for j, piece in enumerate(pieces):
        total = lax.dot_general(
            drows_ref[...], piece[...], (((1,), (1,)), ((), ())), preferred_element_type=F32
        ).astype(BF16)
        for r in range(parts):
            out_ref[r, j] = total[r * share : (r + 1) * share]


def dense_rows_back(drows, pieces, parts):
    length, width = drows.shape
    depth = pieces[0].shape[0]
    shape = (parts, len(pieces), length // parts, depth)
    return pl.pallas_call(
        rows_back_kernel,
        out_shape=jax.ShapeDtypeStruct(shape, BF16),
        compiler_params=params(drows, *pieces),
    )(drows, *pieces)


def dense_grad_kernel(which, x_ref, y_ref, rows_ref, other_ref, *outs):
    for at, (k, out_ref) in enumerate(zip(which, outs)):
        total = jnp.dot(x_ref[k].T, rows_ref[...], preferred_element_type=F32)
        total += jnp.dot(y_ref[k // 2].T, other_ref[...], preferred_element_type=F32)
        out_ref[...] = total.astype(out_ref.dtype)


def dense_grad(which, x, y, rows, other, dtype):
    _, length, depth = x.shape
    width = rows.shape[1]
    outs = [jax.ShapeDtypeStruct((depth, width), dtype)] * len(which)
    return pl.pallas_call(
        functools.partial(dense_grad_kernel, which),
        out_shape=outs,
        compiler_params=params(x, y, rows, other, *outs),
    )(x, y, rows, other)


def allowed_of(seg_col, seg_row, place_col, place_row):
    return (seg_col[...] == seg_row[...]) & (place_row[...] <= place_col[...])


def attend_kernel(
    first_ref, second_ref, dense_ref, gates_ref, cos_ref, sin_ref, seg_col, seg_row, place_col, place_row, query_ref, key_ref, lse_ref, mixed_ref, *send_refs
):
    width = first_ref.shape[1]
    heads = width // HEAD_DIM
    cosine, sine = cos_ref[...], sin_ref[...]
    allowed = allowed_of(seg_col, seg_row, place_col, place_row)
    for head in range(heads):
        at = head * HEAD_DIM
        key_at, value_at = slice(at, at + HEAD_DIM), slice(width + at, width + at + HEAD_DIM)
        key = turn(dense_ref[:, key_at], cosine, sine).astype(BF16)
        value = dense_ref[:, value_at].astype(BF16)
        key_ref[:, key_at] = key
        key_ref[:, value_at] = value
        for choice, raw_ref in enumerate((first_ref, second_ref)):
            here = slice(choice * width + at, choice * width + at + HEAD_DIM)
            query = turn(raw_ref[:, key_at], cosine, sine).astype(BF16)
            query_ref[:, here] = query
            scores = lax.dot_general(
                query, key, (((1,), (1,)), ((), ())), preferred_element_type=F32
            ) * HEAD_DIM ** (-0.5)
            scores = jnp.where(allowed, scores, -1e30)
            top = jnp.max(scores, axis=1, keepdims=True)
            lse = top + jnp.log(jnp.sum(jnp.exp(scores - top), axis=1, keepdims=True))
            lse_ref[:, choice * heads + head : choice * heads + head + 1] = lse
            probs = jnp.exp(scores - lse).astype(BF16)
            mixed = jnp.dot(probs, value, preferred_element_type=F32).astype(BF16)
            mixed_ref[:, here] = mixed
            send_refs[choice][:, key_at] = (
                mixed.astype(F32) * gates_ref[:, choice : choice + 1]
            ).astype(BF16)


def attend(raw, dense, gates, tables):
    length, width = raw[0].shape
    return pl.pallas_call(
        attend_kernel,
        out_shape=[
            jax.ShapeDtypeStruct((length, 2 * width), BF16),
            jax.ShapeDtypeStruct((length, 2 * width), BF16),
            jax.ShapeDtypeStruct((length, 2 * width // HEAD_DIM), F32),
            jax.ShapeDtypeStruct((length, 2 * width), BF16),
            *[jax.ShapeDtypeStruct((length, width), BF16)] * 2,
        ],
        compiler_params=pltpu.CompilerParams(vmem_limit_bytes=24 << 20),
    )(*raw, dense, gates, *tables)


def attend_back_kernel(
    query_ref, key_ref, lse_ref, mixed_ref, first_ref, second_ref, gates_ref, cos_ref, sin_ref, seg_col, seg_row, place_col, place_row, *refs
):
    dquery_refs, (dkey_ref, dgates_ref) = refs[:2], refs[2:]
    length = query_ref.shape[0]
    width = query_ref.shape[1] // 2
    heads = width // HEAD_DIM
    cosine, sine = cos_ref[...], sin_ref[...]
    allowed = allowed_of(seg_col, seg_row, place_col, place_row)
    turned = (((1,), (1,)), ((), ()))
    dgates = [jnp.zeros((length, 1), F32), jnp.zeros((length, 1), F32)]
    for head in range(heads):
        at = head * HEAD_DIM
        key_at, value_at = slice(at, at + HEAD_DIM), slice(width + at, width + at + HEAD_DIM)
        key, value = key_ref[:, key_at], key_ref[:, value_at]
        dkey = jnp.zeros((length, HEAD_DIM), F32)
        dvalue = jnp.zeros((length, HEAD_DIM), F32)
        for choice, pull_ref in enumerate((first_ref, second_ref)):
            here = slice(choice * width + at, choice * width + at + HEAD_DIM)
            query, pull = query_ref[:, here], pull_ref[:, key_at]
            dgates[choice] += jnp.sum(mixed_ref[:, here].astype(F32) * pull, axis=1, keepdims=True)
            dmixed = (pull * gates_ref[:, choice : choice + 1]).astype(BF16)
            scores = lax.dot_general(query, key, turned, preferred_element_type=F32) * HEAD_DIM ** (-0.5)
            scores = jnp.where(allowed, scores, -1e30)
            probs = jnp.exp(scores - lse_ref[:, choice * heads + head : choice * heads + head + 1])
            dprobs = lax.dot_general(dmixed, value, turned, preferred_element_type=F32)
            inner = jnp.sum(probs * dprobs, axis=1, keepdims=True)
            dscores = (probs * (dprobs - inner)).astype(BF16)
            dquery = jnp.dot(dscores, key, preferred_element_type=F32) * HEAD_DIM ** (-0.5)
            dquery_refs[choice][:, key_at] = turn(dquery, cosine, -sine).astype(BF16)
            dkey += jnp.dot(dscores.T, query, preferred_element_type=F32)
            dvalue += jnp.dot(probs.astype(BF16).T, dmixed, preferred_element_type=F32)
        dkey_ref[:, key_at] = turn(dkey * HEAD_DIM ** (-0.5), cosine, -sine).astype(BF16)
        dkey_ref[:, value_at] = dvalue.astype(BF16)
    for choice in range(2):
        dgates_ref[:, choice : choice + 1] = dgates[choice]


def attend_back(query, key, lse, mixed, pull, gates, tables):
    length, width = pull[0].shape
    return pl.pallas_call(
        attend_back_kernel,
        out_shape=[
            *[jax.ShapeDtypeStruct((length, width), BF16)] * 2,
            jax.ShapeDtypeStruct(key.shape, BF16),
            jax.ShapeDtypeStruct(gates.shape, F32),
        ],
        compiler_params=pltpu.CompilerParams(vmem_limit_bytes=24 << 20),
    )(query, key, lse, mixed, *pull, gates, *tables)


def angles(places):
    half = HEAD_DIM // 2
    freqs = ROTARY_BASE ** (-(jnp.arange(half, dtype=F32) * 2.0 / HEAD_DIM))
    phase = places.astype(F32)[:, None] * freqs[None, :]
    cosine, sine = jnp.cos(phase), jnp.sin(phase)
    return jnp.concatenate([cosine, cosine], axis=1), jnp.concatenate([-sine, sine], axis=1)


def chosen_of(routes, kinds):
    return (routes[:, :, None] == jnp.arange(kinds, dtype=jnp.int32)).astype(F32)


def pair_gates(logits, chosen):
    return jax.nn.softmax(jnp.sum(logits[:, None, :] * chosen, axis=2), axis=-1)


def logit_grad(gates, weighted, chosen):
    inner = weighted - gates * jnp.sum(weighted, axis=1, keepdims=True)
    return jnp.sum(inner[:, :, None] * chosen, axis=1)


def slots_of(chosen, quarter):
    named = jnp.sum(chosen, axis=1)
    rows = named.shape[0]
    before = (jnp.arange(rows)[:, None] > jnp.arange(rows)[None, :]).astype(F32)
    rank = jnp.sum((before @ named)[:, None, :] * chosen, axis=2).astype(jnp.int32)
    kind = jnp.sum(chosen * jnp.arange(chosen.shape[2], dtype=F32), axis=2).astype(jnp.int32)
    return rank // quarter, kind * quarter + rank % quarter


def body(
    tokens,
    cotangent,
    segment_ids,
    routes_att,
    routes_mlp,
    gain_att,
    router_att,
    w_query,
    w_key,
    w_value,
    w_output,
    gain_mlp,
    router_mlp,
    w_gate,
    w_up,
    w_down,
):
    parts = lax.axis_size("tensor")
    devices = lax.axis_size("expert")
    group = devices // EXPERTS
    length = tokens.shape[0]
    share = length // parts
    quarter = CAP // parts
    depth = gain_att.shape[0]
    width = w_key.shape[1]
    me = lax.axis_index("expert")
    part = lax.axis_index("tensor")
    places = jnp.stack([me, part]).astype(jnp.int32)
    order = part ^ jnp.arange(parts)
    far = bits_of("expert")[:-1]
    mine = range(0, devices, 2)

    def by_part(values):
        shaped = values.reshape(parts, share, *values.shape[1:])
        return jnp.take(shaped, order, axis=0).reshape(values.shape)

    def gather_far(first, second):
        halves = [gather_pieces(one, "expert", far) for one in (first, second)]
        return {k: (halves[0][k], halves[1][k]) for k in mine}

    def pair(values):
        return hop(values, "expert", 1)

    own_meta = jnp.concatenate(
        [gain_att, gain_mlp, router_att.T.reshape(-1), router_mlp.T.reshape(-1)]
    ).reshape(18, depth)
    pair_meta = pair(own_meta)

    def swap(sent):
        return jnp.stack([hop(one, "expert", k) if k else one for k, one in zip(mine, sent)])

    by_block = swap([jnp.stack([own_meta, pair_meta])] * len(mine)).reshape(devices, 18, depth)
    gain_one, gain_two = by_block[:, :1].astype(F32), by_block[:, 1:2].astype(F32)
    route_one, route_two = by_block[:, 2 : 2 + EA], by_block[:, 2 + EA :]

    belt = []

    def on_belt(values):
        belt.append(pair(after(values, belt[-2]) if len(belt) > 1 else values))
        return belt[-1]

    query_own = w_query.transpose(1, 0, 2)
    query_pair = [on_belt(query_own[at : at + 2]) for at in range(0, EA, 2)]
    query_ws = [[query_own], query_pair]

    blocks, scale_one, chunks = pack(places, tokens, routes_att, parts, devices)
    chunks[1] = after(chunks[1], by_block)
    came = after(swap(chunks), belt[0])
    token_pieces = gather_pieces(came, "tensor")
    dense_pieces = gather_pieces(
        after(jnp.concatenate([w_key, w_value], axis=1), came), "expert", far
    )
    normed_own, normed_pair, routes_far = unpack(
        [after(token_pieces[r], belt[2]) if r == 3 else token_pieces[r] for r in range(parts)],
        by_block[:2, 0].astype(F32),
    )
    normed_far = [normed_own, normed_pair]
    for k in mine:
        dense_pieces[k ^ 1] = on_belt(dense_pieces[k])
    dense_pieces = [dense_pieces[j] for j in range(devices)]
    normed_blocks = (blocks.astype(F32) * scale_one * gain_one).astype(BF16)
    output_own = after(w_output, normed_own).transpose(1, 0, 2)
    output_pair = [on_belt(output_own[at : at + 2]) for at in range(0, EA, 2)]
    output_ws = [[output_own], output_pair]
    routes_one = by_part(after(routes_att, normed_own))

    chosen_one = chosen_of(routes_one, EA)
    gates_one = pair_gates(
        jnp.einsum("jtd,jkd->tk", normed_blocks, route_one, preferred_element_type=F32), chosen_one
    )

    def project_sum(xs, ws, ties=((), ())):
        late = [k for k in mine if not k & 2]
        early = [k for k in mine if k & 2][::-1]
        found = project(tuple(early), xs, ws, routes_far, BF16)
        rest = project(tuple(late), [after(xs[0], *found, *ties[0]), xs[1]], ws, routes_far, F32)
        sums, came = [], []
        for choice in range(2):
            chunks = dict(zip(early, found[choice::2])) | dict(zip(late, rest[choice::2]))
            total, here = scatter_sum(chunks, "expert", far, BF16)
            sums.append(after(total, *ties[1]))
            came.append(here)
        return sums, rest, came

    raw, started, _ = project_sum(normed_far, query_ws)
    dense_raw = dense_rows(normed_blocks, dense_pieces)
    at_row = (order[:, None] * share + jnp.arange(share)).reshape(-1).astype(jnp.int32)
    at_row = after(at_row, *started)
    segment = by_part(after(segment_ids, *started)[0])
    tables = (*angles(at_row), segment[:, None], segment[None, :], at_row[:, None], at_row[None, :])

    routes_mlp = after(routes_mlp, *started)
    chosen_two = chosen_of(routes_mlp, EXPERTS)
    slot_part, slot = slots_of(chosen_two, quarter)
    slot = by_part(jnp.where(slot_part == part, slot, -1)).T
    routes_two = by_part(routes_mlp).T
    own_chosen = routes_two[:, None, :share] == jnp.arange(EXPERTS, dtype=jnp.int32)[None, :, None]
    own_chosen = own_chosen.astype(F32)
    up = arrange(places, after(cotangent, *started), parts, devices)
    own_up = up[:, :share].astype(F32)
    slots = EXPERTS * quarter

    raw = after(raw, slot, routes_two, own_chosen, up, *tables)
    query, key, lse, mixed, *mixed_sent = attend(raw, dense_raw, gates_one, tables)
    mixed_pieces = gather_far(*mixed_sent)
    branch = to_owners(mixed_pieces, routes_far, output_ws, parts)
    own_tokens = blocks[:, :share]
    hidden, scale_two, own_two = hidden_rows(own_tokens, gain_two, branch)

    rows, dexpert, gates_two = dispatch(
        places, slot, routes_two, route_two, up, gather_pieces(own_two, "tensor"), slots
    )

    def to_experts(values):
        shaped = values.reshape(EXPERTS, 1, quarter, D)
        shaped = jnp.broadcast_to(shaped, (EXPERTS, group, quarter, D)).reshape(devices, quarter, D)
        return lax.all_to_all(shaped, "expert", 0, 0, tiled=True).reshape(devices * quarter, D)

    def back_home(summed):
        summed = summed.astype(BF16).reshape(devices, quarter, D)
        back = lax.all_to_all(summed, "expert", 0, 0, tiled=True)
        back = back.reshape(EXPERTS, group, quarter, D)
        if group > 1:
            back = jnp.sum(back.astype(F32), axis=1).astype(BF16)
        return back.reshape(slots, D)

    turned = (((1,), (1,)), ((), ()))

    def forward(half):
        gate_pre = jnp.dot(half, w_gate[0], preferred_element_type=F32)
        up_pre = jnp.dot(half, w_up[0], preferred_element_type=F32)
        return gate_pre, up_pre, (jax.nn.silu(gate_pre) * up_pre).astype(BF16)

    def backward(half, gate_pre, up_pre):
        dacted = lax.dot_general(half, w_down[0], turned, preferred_element_type=F32)
        sigma = jax.nn.sigmoid(gate_pre)
        dup = (dacted * gate_pre * sigma).astype(BF16)
        dgate = (dacted * up_pre * sigma * (1.0 + gate_pre * (1.0 - sigma))).astype(BF16)
        dinput = lax.dot_general(dgate, w_gate[0], turned, preferred_element_type=F32)
        dinput += lax.dot_general(dup, w_up[0], turned, preferred_element_type=F32)
        return dgate, dup, dinput.astype(BF16)

    assert parts == 4
    came_rows = to_experts(rows)
    far_rows = hop(came_rows, "tensor", 2)
    row_halves = [jnp.concatenate([came_rows, hop(came_rows, "tensor", 1)])]
    pre = [forward(row_halves[0])]
    came_grads = to_experts(after(dexpert, came_rows))
    far_grads = hop(came_grads, "tensor", 2)
    far_rows = after(far_rows, came_grads, pre[0][2])
    row_halves.append(jnp.concatenate([far_rows, hop(far_rows, "tensor", 1)]))
    pre.append(forward(row_halves[1]))
    far_grads = after(far_grads, pre[1][2])
    grad_halves = [
        jnp.concatenate([one, hop(one, "tensor", 1)]) for one in (came_grads, far_grads)
    ]
    expert_part = [
        jnp.dot(acted, w_down[0], preferred_element_type=F32).astype(BF16)
        for _, _, acted in pre[::-1]
    ][::-1]

    def sum_far(half):
        far_chunk, last = jnp.split(half, 2)
        return (far_chunk.astype(F32) + hop(last, "tensor", 1).astype(F32)).astype(BF16)

    def sum_near(half, came):
        chunk, last = jnp.split(half, 2)
        return chunk.astype(F32) + hop(last, "tensor", 1).astype(F32) + came.astype(F32)

    expert_far = sum_far(expert_part[1])
    expert_out = back_home(sum_near(expert_part[0], hop(expert_far, "tensor", 2)))
    back_far = backward(
        after(grad_halves[1], *expert_part), *pre[1][:2]
    )
    input_far = sum_far(back_far[2])
    back_near = backward(
        after(grad_halves[0], input_far), *pre[0][:2]
    )
    dreturned = back_home(sum_near(back_near[2], hop(input_far, "tensor", 2)))

    expert_rows, dout_rows = jnp.concatenate(row_halves), jnp.concatenate(grad_halves)
    acted = jnp.concatenate([one[2] for one in pre])
    dgate = jnp.concatenate([back_near[0], back_far[0]])
    dup = jnp.concatenate([back_near[1], back_far[1]])
    acted, dgate, dup = after((acted, dgate, dup), back_near[2])
    grad_down = jnp.einsum("rf,rd->fd", acted, dout_rows, preferred_element_type=F32)[None]
    grad_gate = jnp.einsum("rd,rf->df", expert_rows, dgate, preferred_element_type=F32)[None]
    grad_up = jnp.einsum("rd,rf->df", expert_rows, dup, preferred_element_type=F32)[None]

    *out_chunks, weighted = combine(places, slot, expert_out, parts, devices, gates_two, dexpert)
    weighted, _ = scatter_sum(
        {r: weighted[:, r * share : (r + 1) * share] for r in range(parts)}, "tensor"
    )
    moe, _ = scatter_sum(dict(enumerate(out_chunks)), "tensor")
    dreturned = after(dreturned, grad_down, grad_gate, grad_up)
    back_chunks = combine(places, slot, dreturned, parts, devices)
    own_gates_two = gates_two[:, :share]
    inner = weighted - own_gates_two * jnp.sum(weighted, axis=0, keepdims=True)
    own_dlogits = jnp.sum(inner[:, None, :] * own_chosen, axis=0)
    dnormed = scatter_sum(dict(enumerate(back_chunks)), "tensor")[0] + jnp.einsum(
        "kt,jkd->jtd", own_dlogits, route_two.astype(F32), precision=PRECISE
    )
    pulled = dnormed * gain_two
    inner_mean = jnp.sum(pulled * hidden, axis=(0, 2), keepdims=True) / D
    dhidden = own_up + scale_two * pulled - hidden * (scale_two * scale_two * scale_two * inner_mean)

    sent = dhidden.astype(BF16)
    up_pieces = gather_pieces(swap(
        [jnp.concatenate([sent[k], sent[k ^ 1]], axis=1) for k in mine]
    ), "tensor")
    dhidden_far = assemble([up_pieces[r] for r in range(parts)])
    pull, started, arrived = project_sum(dhidden_far, output_ws)
    pair_normed = pair(after(normed_far[1], *started))
    pair_blocks = pair(after(normed_blocks[1::2], *started))
    pair_routes = pair(after(routes_far, *started).astype(BF16).transpose(0, 2, 1))
    pair_routes = pair_routes.transpose(0, 2, 1).astype(jnp.int32)
    grad_output, pair_grad = map_grads(
        [[after(dhidden_far[0], *started), dhidden_far[1]]],
        [routes_far],
        [half for k in mine for half in mixed_pieces[k]],
        (F32, BF16),
    )
    pair_grad = pair(pair_grad)
    mixed_out = output_rows(
        places, gather_pieces(after((hidden + moe).astype(BF16), *started), "tensor"), BF16
    )
    def to_features(partial):
        count = partial.shape[0]
        chunks = jnp.take(partial.transpose(1, 0, 2), me ^ jnp.arange(devices), axis=0)[:, None]
        chunks = jnp.broadcast_to(chunks, (devices, parts, count, depth)).reshape(-1, count, depth)
        return jnp.sum(lax.all_to_all(chunks, ("expert", "tensor"), 0, 0, tiled=True), axis=0)

    part_gain_two = jnp.sum(dnormed * hidden * scale_two, axis=1)[None]
    part_route_two = jnp.einsum(
        "kt,jtd->kjd", own_dlogits, own_two.astype(F32), precision=PRECISE
    )

    small_two = to_features(after(jnp.concatenate([part_gain_two, part_route_two]), *started))
    pull = after(pull, small_two, grad_output, pair_normed, pair_blocks)
    *dqueries, ddense, dgates_one = attend_back(query, key, lse, mixed, pull, gates_one, tables)
    pair_dense = pair(ddense)
    dquery_pieces = gather_far(*dqueries)
    pair_dquery = {k: [pair(one) for one in dquery_pieces[k]] for k in mine}
    dnormed_came = to_owners(
        dquery_pieces,
        routes_far,
        query_ws,
        parts,
        ((pair_dense, *pair_dquery[0]), pair_dquery[2]),
    )
    dense_back = dense_rows_back(after(ddense, *dquery_pieces[2]), dense_pieces, parts)
    dense_share, _ = scatter_sum({r: dense_back[r] for r in range(parts)}, "tensor")
    dgates_one, _ = scatter_sum(
        {r: dgates_one[r * share : (r + 1) * share] for r in range(parts)}, "tensor"
    )
    grad_chunks = {}
    for which, dtype in (
        (tuple(k for k in mine if k & 2)[::-1], BF16),
        (tuple(k for k in mine if not k & 2), F32),
    ):
        found = dense_grad(which, normed_blocks, pair_blocks, ddense, pair_dense, dtype)
        grad_chunks.update(zip(which, found))
    grad_dense, dense_came = scatter_sum(grad_chunks, "expert", far, BF16)
    (grad_query,) = map_grads(
        [[normed_far[0]], [pair_normed]],
        [routes_far, pair_routes],
        [half for side in (dquery_pieces, pair_dquery) for k in mine for half in side[k]],
        (F32,),
    )
    grad_key, grad_value = grad_dense[:, :width], grad_dense[:, width:]

    own_gates, own_scale = gates_one[:share], scale_one[:share]
    own_dlogits_one = logit_grad(own_gates, own_gates * dgates_one, chosen_one[:share])
    dnormed_came[0] = after(dnormed_came[0], *pair_dquery[4], *pair_dquery[6])
    whole = jnp.stack(
        [
            dnormed_came[k][:, b * depth : (b + 1) * depth].astype(F32)
            for k in mine
            for b in range(2)
        ]
    )
    dnormed_one = whole + dense_share + jnp.einsum(
        "tk,jkd->jtd", own_dlogits_one, route_one.astype(F32), precision=PRECISE
    )
    pulled_one = dnormed_one * gain_one
    token_rows = own_tokens.astype(F32)
    inner_one = jnp.sum(pulled_one * token_rows, axis=(0, 2), keepdims=True) / D
    own_grad = (
        dhidden
        + own_scale * pulled_one
        - token_rows * (own_scale * own_scale * own_scale * inner_one)
    )
    own_grad = after(own_grad.astype(BF16), *dense_came[:-1])
    grad_pieces = gather_pieces(own_grad, "tensor")
    grad_tokens = output_rows(places, {**grad_pieces, 3: after(grad_pieces[3], grad_dense)}, F32)
    part_gain_one = jnp.sum(dnormed_one * token_rows * own_scale, axis=1)[None]
    part_route_one = jnp.einsum(
        "tk,jtd->kjd", own_dlogits_one, normed_blocks[:, :share].astype(F32), precision=PRECISE
    )

    small_one = to_features(jnp.concatenate([part_gain_one, part_route_one]))
    return (
        mixed_out,
        grad_tokens,
        small_one[0],
        small_one[1:].T,
        grad_query,
        grad_key,
        grad_value,
        grad_output + pair_grad.astype(F32),
        small_two[0],
        small_two[1:].T,
        grad_gate,
        grad_up,
        grad_down,
    )


def solution(mesh):
    in_specs = (
        P("expert", None),
        P("expert", None),
        P("expert", None),
        P("expert", None),
        P("expert", None),
        P("expert"),
        P("expert", None),
        P("expert", None, "tensor"),
        P("expert", "tensor"),
        P("expert", "tensor"),
        P("expert", None, "tensor"),
        P("expert"),
        P("expert", None),
        P("expert", None, "tensor"),
        P("expert", None, "tensor"),
        P("expert", "tensor", None),
    )
    out_specs = (
        P("expert", None),
        P("expert", None),
        P("expert"),
        P("expert", None),
        P("expert", None, "tensor"),
        P("expert", "tensor"),
        P("expert", "tensor"),
        P("expert", None, "tensor"),
        P("expert"),
        P("expert", None),
        P("expert", None, "tensor"),
        P("expert", None, "tensor"),
        P("expert", "tensor", None),
    )
    return jax.shard_map(body, mesh=mesh, in_specs=in_specs, out_specs=out_specs, check_vma=False)
```

time: 2680 us -> 693 us (0.26)
  waiting for transfers between devices: 1940 us -> 215 us
  blocking collectives: 301 us -> 23.8 us
  starting transfers between devices: 4.48 us -> 123 us
  Pallas kernels: 0 us -> 90.6 us
  local copies, waits for them, and re-layouts: 162 us -> 74 us
  matrix products: 179 us -> 97.1 us
    reduce_scatter x8 -> x0, waiting for transfers between devices: 1380 us -> none  [the longest x1 540 us: body(): lax.psum_scatter(grad_output, 'expert', scatter_dimension=0, tiled=True)]
    all_gather x6 -> x0, waiting for transfers between devices: 480 us -> none  [the longest x1 226 us: body(): lax.all_gather(w_query, 'expert', axis=0, tiled=True)]
    ppermute x0 -> x125, waiting for transfers between devices: none -> 209 us  [hop(): return lax.ppermute(values, axis, [(i, i ^ bit) for i in range(size)])]
    all_to_all x3 -> x1, blocking collectives: 161 us -> 23.8 us  [to_experts(): lax.all_to_all(shaped, 'expert', 0, 0, tiled=True)]
    all_gather x4 -> x0, blocking collectives: 101 us -> none  [the longest x1 30.6 us: body(): lax.all_gather(router_att, 'expert', axis=0, tiled=True)]
    ppermute x0 -> x125, starting transfers between devices: none -> 100 us  [hop(): return lax.ppermute(values, axis, [(i, i ^ bit) for i in range(size)])]
    pallas_call x0 -> x26, Pallas kernels: none -> 90.6 us  [the longest x2 23.7 us: map_grads(): pl.pallas_call(functools.partial(map_grads_kernel, len(xs), len(sides)),...]
    dot_general x32 -> x21, matrix products: 176 us -> 97.1 us  [the longest x2 13.1 us: backward(): lax.dot_general(half, w_down[0], turned, preferred_element_type=F32)]
  transfers between devices with their start and end apart: 17 -> 130, of which waited for: 14 -> 48; matrix products, arithmetic and copies ran while one was open for 8% -> 27% of each run, Pallas kernels for 0% -> 12%
where the time goes in v1:
time: 693 us; the launch traced here: 682 us
  waiting for transfers between devices  215 us (31%)
  starting transfers between devices  123 us (18%)
  matrix products  97.1 us (14%)
  Pallas kernels  90.6 us (13%)
  local copies, waits for them, and re-layouts  74 us (11%)
  other arithmetic  54.2 us (8%)
  blocking collectives  23.8 us (3%)
    ppermute x125, waiting for transfers between devices, hop(): return lax.ppermute(values, axis, [(i, i ^ bit) for i in range(size)])  209 us
    ppermute x125, starting transfers between devices, hop(): return lax.ppermute(values, axis, [(i, i ^ bit) for i in range(size)])  100 us
    unnamed x339, local copies, waits for them, and re-layouts  42.3 us
    all_to_all x1, blocking collectives, to_experts(): lax.all_to_all(shaped, 'expert', 0, 0, tiled=True)  23.8 us
    pallas_call x2, Pallas kernels, map_grads(): pl.pallas_call(functools.partial(map_grads_kernel, len(xs), len(sides)),...  23.7 us
    pallas_call x4, Pallas kernels, project(): pl.pallas_call(functools.partial(project_kernel, which, [len(side) for si...  21.1 us
  transfers between devices with their start and end apart: 130, of which 48 were waited for; matrix products, arithmetic and copies ran while one was open for 27% of the time, Pallas kernels for 12%

profile of v1, /device:TPU:0, one launch (start us, length us, event | category | flops | bytes accessed | tf_op | source)
XLA Modules:
  0.0 681.7 jit_solution(4095682482714570076)
XLA Ops:
  38.8 6.2 collective-permute-done.18.refs_4_.refs_2_
  45.6 10.6 %collective-permute-done.11.refs_5_.refs_3_ = bf16[2,256,512]{2,1,0:T(8,128)(2,1)S(1)} collective-permute-done((bf16[2,256,512]{2,1,0:T(8,128)(2,1)}, bf16[2,256,512]{2,1,0:T(8,128)(2,1)S(1)}, u32[]{:S(2)}, u32[]{:S(2)}) %collective-permute-start.11) | collective-permute-done | bytes 524320 | tf_op jit(solution)/shard_map/ppermute | solution.py:25
  58.3 7.4 %collective-permute-done.19.refs_6_.refs_4_ = bf16[2,256,512]{2,1,0:T(8,128)(2,1)S(1)} collective-permute-done((bf16[2,256,512]{2,1,0:T(8,128)(2,1)}, bf16[2,256,512]{2,1,0:T(8,128)(2,1)S(1)}, u32[]{:S(2)}, u32[]{:S(2)}) %collective-permute-start.19) | collective-permute-done | bytes 524320 | tf_op jit(solution)/shard_map/ppermute | solution.py:25
  69.0 5.4 shard_map.257
  139.1 9.5 %collective-permute-done.22.refs_2_.refs_4_ = bf16[2,256,512]{2,1,0:T(8,128)(2,1)S(1)} collective-permute-done((bf16[2,256,512]{2,1,0:T(8,128)(2,1)}, bf16[2,256,512]{2,1,0:T(8,128)(2,1)S(1)}, u32[]{:S(2)}, u32[]{:S(2)}) %collective-permute-start.22) | collective-permute-done | bytes 524320 | tf_op jit(solution)/shard_map/ppermute | solution.py:25
  161.7 5.6 collective-permute-done.41.refs_6_.refs_10_
  173.0 5.5 collective-permute-done.32.refs_8_.refs_6_
  208.7 23.8 %all_to_all.30 = bf16[8,24,2048]{2,1,0:T(8,128)(2,1)} all-to-all(bf16[8,24,2048]{2,1,0:T(8,128)(2,1)S(1)} %bitcast.265), channel_id=1, replica_groups=mesh['expert'=8,'tensor'=4] {'expert'}, dimensions={0} | all-to-all | bytes 1572864 | tf_op jit(solution)/shard_map/all_to_all | solution.py:820
  238.6 5.7 fusion.22
  244.3 8.2 %multiply_convert_fusion.5 = (bf16[384,1408]{1,0:T(8,128)(2,1)}, f32[384,1408]{1,0:T(8,128)}) fusion(f32[384,1408]{1,0:T(8,128)S(1)} %fusion.22, bf16[1,2048,1408]{2,1,0:T(8,128)(2,1)} %param.34, bf16[192,2048]{1,0:T(8,128)(2,1)} %collective-permute-done.49, bf16[192,2048]{1,0:T(8,128)(2,1)} %bitcast.27), kind=kOutput, calls=%fused_computation.55 | convolution fusion | flops 2220982272 | bytes 12746752 | tf_op jit(solution)/shard_map/dot_general | solution.py:834
  252.9 6.5 all-to-all-done.1
  265.4 5.4 fusion.20
  274.9 8.0 %collective-permute-done.59 = bf16[192,2048]{1,0:T(8,128)(2,1)S(1)} collective-permute-done((bf16[192,2048]{1,0:T(8,128)(2,1)}, bf16[192,2048]{1,0:T(8,128)(2,1)S(1)}, u32[]{:S(2)}, u32[]{:S(2)}) %collective-permute-start.59) | collective-permute-done | bytes 786464 | tf_op jit(solution)/shard_map/ppermute | solution.py:25
  290.3 6.3 multiply_convert_fusion.3
  300.9 7.3 %add_convert_fusion.1 = bf16[384,2048]{1,0:T(8,128)(2,1)S(1)} fusion(f32[384,2048]{1,0:T(8,128)} %fusion.10, bf16[384,1408]{1,0:T(8,128)(2,1)S(1)} %get-tuple-element.276, bf16[1,2048,1408]{2,1,0:T(8,128)(2,1)} %param.33), kind=kOutput, calls=%fused_computation.43 | convolution fusion | flops 2216165376 | bytes 11567104 | tf_op jit(solution)/shard_map/dot_general | solution.py:842
  315.0 6.8 %multiply_convert_fusion.1 = (bf16[384,1408]{1,0:T(8,128)(2,1)}, bf16[384,1408]{1,0:T(8,128)(2,1)S(1)}) fusion(f32[384,1408]{1,0:T(8,128)} %copy-done.158, f32[384,1408]{1,0:T(8,128)} %get-tuple-element.321, bf16[384,2048]{1,0:T(8,128)(2,1)S(1)} %pad_maximum_fusion.5, bf16[1,1408,2048]{2,1,0:T(8,128)(2,1)S(1)} %bitcast.310), kind=kOutput, calls=%fused_computation.50 | convolution fusion | flops 2221621248 | bytes 13828096 | tf_op jit(solution)/shard_map/dot_general | solution.py:838
  340.9 5.4 add_convert_fusion
  346.5 9.4 %convolution_bitcast_fusion.1 = f32[1,2048,1408]{2,1,0:T(8,128)} fusion(bf16[768,1408]{1,0:T(8,128)(2,1)S(1)} %pad_maximum_fusion.2, bf16[192,2048]{1,0:T(8,128)(2,1)S(1)} %copy-done.117, bf16[192,2048]{1,0:T(8,128)(2,1)} %collective-permute-done.51, bf16[192,2048]{1,0:T(8,128)(2,1)} %collective-permute-done.49, bf16[192,2048]{1,0:T(8,128)(2,1)} %bitcast.27), kind=kOutput, calls=%fused_computation.7 | convolution fusion | flops 4441767936 | bytes 16842752 | tf_op jit(solution)/shard_map/rd,rf->df/dot_general | solution.py:890
  358.3 6.0 all-to-all-start.3
  364.3 10.1 %convolution_bitcast_fusion = f32[1,2048,1408]{2,1,0:T(8,128)} fusion(bf16[768,1408]{1,0:T(8,128)(2,1)} %pad_maximum_fusion.3, bf16[192,2048]{1,0:T(8,128)(2,1)} %copy-done.116, bf16[192,2048]{1,0:T(8,128)(2,1)} %collective-permute-done.51, bf16[192,2048]{1,0:T(8,128)(2,1)} %collective-permute-done.49, bf16[192,2048]{1,0:T(8,128)(2,1)} %bitcast.27), kind=kOutput, calls=%fused_computation.6 | convolution fusion | flops 4441767936 | bytes 16842752 | tf_op jit(solution)/shard_map/rd,rf->df/dot_general | solution.py:891
  374.5 9.2 %convolution_bitcast_fusion.2 = f32[1,1408,2048]{2,1,0:T(8,128)} fusion(bf16[768,1408]{1,0:T(8,128)(2,1)S(1)} %copy-done.111, bf16[192,2048]{1,0:T(8,128)(2,1)S(1)} %copy-done.121, bf16[192,2048]{1,0:T(8,128)(2,1)S(1)} %copy-done.119, bf16[192,2048]{1,0:T(8,128)(2,1)S(1)} %copy-done.123, bf16[192,2048]{1,0:T(8,128)(2,1)} %bitcast.32), kind=kOutput, calls=%fused_computation.8 | convolution fusion | flops 4441767936 | bytes 16842752 | tf_op jit(solution)/shard_map/rf,rd->fd/dot_general | solution.py:889
  399.1 7.1 %collective-permute-done.66 = bf16[8,64,256]{2,1,0:T(8,128)(2,1)S(1)} collective-permute-done((bf16[8,64,256]{2,1,0:T(8,128)(2,1)S(1)}, bf16[8,64,256]{2,1,0:T(8,128)(2,1)S(1)}, u32[]{:S(2)}, u32[]{:S(2)}) %collective-permute-start.66) | collective-permute-done | bytes 262176 | tf_op jit(solution)/shard_map/ppermute | solution.py:25
  429.0 5.7 shard_map.269
  461.4 11.8 %shard_map.272 = (f32[256,8,512]{2,1,0:T(8,128)}, bf16[256,8,512]{2,1,0:T(8,128)(2,1)}) custom-call(bf16[4,256,256]{2,1,0:T(8,128)(2,1)} %copy-done.29, bf16[4,256,256]{2,1,0:T(8,128)(2,1)} %copy-done.30, s32[4,256,2]{2,1,0:T(8,128)} %copy-done.3, bf16[256,512]{1,0:T(8,128)(2,1)} %copy-done.44, bf16[256,512]{1,0:T(8,128)(2,1)} %copy-done.45, ...), custom_call_target="tpu_custom_call" | custom-call | tf_op jit(solution)/shard_map/pallas_call | solution.py:477
  483.0 11.3 %collective-permute-done.84 = bf16[256,512]{1,0:T(8,128)(2,1)S(1)} collective-permute-done((bf16[256,512]{1,0:T(8,128)(2,1)S(1)}, bf16[256,512]{1,0:T(8,128)(2,1)S(1)}, u32[]{:S(2)}, u32[]{:S(2)}) %collective-permute-start.84) | collective-permute-done | bytes 262176 | tf_op jit(solution)/shard_map/ppermute | solution.py:25
  525.8 7.2 %collective-permute-done.91.refs_8_.refs_7_ = bf16[256,512]{1,0:T(8,128)(2,1)} collective-permute-done((bf16[256,512]{1,0:T(8,128)(2,1)}, bf16[256,512]{1,0:T(8,128)(2,1)}, u32[]{:S(2)}, u32[]{:S(2)}) %collective-permute-start.91) | collective-permute-done | bytes 262176 | tf_op jit(solution)/shard_map/ppermute | solution.py:25
  538.1 8.3 %collective-permute-done.92.refs_9_.refs_8_ = bf16[256,512]{1,0:T(8,128)(2,1)S(1)} collective-permute-done((bf16[256,512]{1,0:T(8,128)(2,1)}, bf16[256,512]{1,0:T(8,128)(2,1)S(1)}, u32[]{:S(2)}, u32[]{:S(2)}) %collective-permute-start.92) | collective-permute-done | bytes 262176 | tf_op jit(solution)/shard_map/ppermute | solution.py:25
  557.5 5.6 shard_map.274
  585.7 11.9 %shard_map.280 = f32[256,8,512]{2,1,0:T(8,128)} custom-call(bf16[4,256,256]{2,1,0:T(8,128)(2,1)} %copy-done.28, bf16[4,256,256]{2,1,0:T(8,128)(2,1)} %collective-permute-done.85.refs_1_, s32[4,256,2]{2,1,0:T(8,128)} %copy-done.3, s32[4,256,2]{2,1,0:T(8,128)} %convert_bitcast_fusion.refs_3_, bf16[256,512]{1,0:T(8,128)(2,1)} %get-tuple-element.234.refs_5_.refs_4_, ...), custom_call_target="tpu_custom_call" | custom-call | tf_op jit(solution)/shard_map/pallas_call | solution.py:477
  616.1 5.3 collective-permute-done.113
  631.2 14.7 %collective-permute-done.118 = bf16[256,1024]{1,0:T(8,128)(2,1)} collective-permute-done((bf16[256,1024]{1,0:T(8,128)(2,1)}, bf16[256,1024]{1,0:T(8,128)(2,1)}, u32[]{:S(2)}, u32[]{:S(2)}) %collective-permute-start.118) | collective-permute-done | bytes 524320 | tf_op jit(solution)/shard_map/ppermute | solution.py:25
  663.0 12.2 %collective-permute-done.122 = bf16[256,1024]{1,0:T(8,128)(2,1)S(1)} collective-permute-done((bf16[256,1024]{1,0:T(8,128)(2,1)}, bf16[256,1024]{1,0:T(8,128)(2,1)S(1)}, u32[]{:S(2)}, u32[]{:S(2)}) %collective-permute-start.122) | collective-permute-done | bytes 524320 | tf_op jit(solution)/shard_map/ppermute | solution.py:25
  (780 shorter events, 408.6 us)
Async XLA Ops:
  35.9 30.3 %collective-permute-start.17 = (bf16[256,1024]{1,0:T(8,128)(2,1)}, bf16[256,1024]{1,0:T(8,128)(2,1)}, u32[]{:S(2)}, u32[]{:S(2)}) collective-permute-start(bf16[256,1024]{1,0:T(8,128)(2,1)} %pad_maximum_fusion.11.refs_0_), channel_id=1, source_target_pairs={{0,8},{4,12},{8,0},{12,4},{16,24},{20,28},{24,16},{28,20},{1,9},{5... | collective-permute-start | bytes 1572872 | tf_op jit(solution)/shard_map/ppermute | solution.py:25
  36.0 31.7 %collective-permute-start.12 = (bf16[256,1024]{1,0:T(8,128)(2,1)}, bf16[256,1024]{1,0:T(8,128)(2,1)}, u32[]{:S(2)}, u32[]{:S(2)}) collective-permute-start(bf16[256,1024]{1,0:T(8,128)(2,1)} %pad_maximum_fusion.11.refs_0_), channel_id=1, source_target_pairs={{0,16},{4,20},{8,24},{12,28},{16,0},{20,4},{24,8},{28,12},{1,17},{... | collective-permute-start | bytes 1572872 | tf_op jit(solution)/shard_map/ppermute | solution.py:25
  65.7 31.3 %collective-permute-start.13 = (bf16[256,1024]{1,0:T(8,128)(2,1)}, bf16[256,1024]{1,0:T(8,128)(2,1)}, u32[]{:S(2)}, u32[]{:S(2)}) collective-permute-start(bf16[256,1024]{1,0:T(8,128)(2,1)} %pad_maximum_fusion.11.refs_0_), channel_id=1, source_target_pairs={{0,4},{4,0},{8,12},{12,8},{16,20},{20,16},{24,28},{28,24},{1,5},{5... | collective-permute-start | bytes 1572872 | tf_op jit(solution)/shard_map/ppermute | solution.py:25
  66.2 32.8 %collective-permute-start.20 = (bf16[256,1024]{1,0:T(8,128)(2,1)}, bf16[256,1024]{1,0:T(8,128)(2,1)}, u32[]{:S(2)}, u32[]{:S(2)}) collective-permute-start(bf16[256,1024]{1,0:T(8,128)(2,1)} %collective-permute-done.17.refs_2_), channel_id=1, source_target_pairs={{0,4},{4,0},{8,12},{12,8},{16,20},{20,16},{24,28},{28,24},{1,5},{5... | collective-permute-start | bytes 1572872 | tf_op jit(solution)/shard_map/ppermute | solution.py:25
  67.8 31.7 %collective-permute-start.16 = (bf16[256,1024]{1,0:T(8,128)(2,1)}, bf16[256,1024]{1,0:T(8,128)(2,1)}, u32[]{:S(2)}, u32[]{:S(2)}) collective-permute-start(bf16[256,1024]{1,0:T(8,128)(2,1)} %collective-permute-done.12.refs_4_), channel_id=1, source_target_pairs={{0,8},{4,12},{8,0},{12,4},{16,24},{20,28},{24,16},{28,20},{1,9},{5... | collective-permute-start | bytes 1572872 | tf_op jit(solution)/shard_map/ppermute | solution.py:25
  86.2 36.6 %collective-permute-start.25 = (bf16[256,512]{1,0:T(8,128)(2,1)}, bf16[256,512]{1,0:T(8,128)(2,1)}, u32[]{:S(2)}, u32[]{:S(2)}) collective-permute-start(bf16[256,512]{1,0:T(8,128)(2,1)} %copy-done.104), channel_id=1, source_target_pairs={{0,8},{4,12},{8,0},{12,4},{16,24},{20,28},{24,16},{28,20},{1,9},{5... | collective-permute-start | bytes 786440 | tf_op jit(solution)/shard_map/ppermute | solution.py:25
  122.8 25.8 %collective-permute-start.22 = (bf16[2,256,512]{2,1,0:T(8,128)(2,1)}, bf16[2,256,512]{2,1,0:T(8,128)(2,1)S(1)}, u32[]{:S(2)}, u32[]{:S(2)}) collective-permute-start(bf16[2,256,512]{2,1,0:T(8,128)(2,1)} %get-tuple-element.155), channel_id=1, source_target_pairs={{0,4},{4,0},{8,12},{12,8},{16,20},{20,16},{24,28},{28,24},{1,5},{5... | collective-permute-start | bytes 1572872 | tf_op jit(solution)/shard_map/ppermute | solution.py:25
  138.6 28.8 %collective-permute-start.23 = (bf16[2,256,512]{2,1,0:T(8,128)(2,1)S(1)}, bf16[2,256,512]{2,1,0:T(8,128)(2,1)S(1)}, u32[]{:S(2)}, u32[]{:S(2)}) collective-permute-start(bf16[2,256,512]{2,1,0:T(8,128)(2,1)S(1)} %copy-done.127), channel_id=1, source_target_pairs={{0,4},{4,0},{8,12},{12,8},{16,20},{20,16},{24,28},{28,24},{1,5},{5... | collective-permute-start | bytes 1572872 | tf_op jit(solution)/shard_map/ppermute | solution.py:25
  234.3 25.0 %all-to-all-start.1 = ((bf16[8,24,2048]{2,1,0:T(8,128)(2,1)}), bf16[8,24,2048]{2,1,0:T(8,128)(2,1)}, u32[]{:S(2)}, u32[]{:S(2)}) async-start(bf16[8,24,2048]{2,1,0:T(8,128)(2,1)} %bitcast.264), calls=%async_computation.1 | async-start | bytes 1572864 | tf_op jit(solution)/shard_map/all_to_all | solution.py:820
  285.6 42.1 %collective-permute-start.50 = (bf16[192,2048]{1,0:T(8,128)(2,1)S(1)}, bf16[192,2048]{1,0:T(8,128)(2,1)S(1)}, u32[]{:S(2)}, u32[]{:S(2)}) collective-permute-start(bf16[192,2048]{1,0:T(8,128)(2,1)S(1)} %split.33), channel_id=1, source_target_pairs={{0,1},{1,0},{2,3},{3,2},{4,5},{5,4},{6,7},{7,6},{8,9},{9,8},{10,11... | collective-permute-start | bytes 2359304 | tf_op jit(solution)/shard_map/ppermute | solution.py:25
  286.1 23.7 %collective-permute-start.58 = (bf16[192,2048]{1,0:T(8,128)(2,1)}, bf16[192,2048]{1,0:T(8,128)(2,1)S(1)}, u32[]{:S(2)}, u32[]{:S(2)}) collective-permute-start(bf16[192,2048]{1,0:T(8,128)(2,1)} %bitcast.32), channel_id=1, source_target_pairs={{0,1},{1,0},{2,3},{3,2},{4,5},{5,4},{6,7},{7,6},{8,9},{9,8},{10,11... | collective-permute-start | bytes 2359304 | tf_op jit(solution)/shard_map/ppermute | solution.py:25
  313.3 42.7 %collective-permute-start.63 = (bf16[192,2048]{1,0:T(8,128)(2,1)}, bf16[192,2048]{1,0:T(8,128)(2,1)}, u32[]{:S(2)}, u32[]{:S(2)}) collective-permute-start(bf16[192,2048]{1,0:T(8,128)(2,1)} %add_convert_fusion.3), channel_id=1, source_target_pairs={{0,2},{1,3},{2,0},{3,1},{4,6},{5,7},{6,4},{7,5},{8,10},{9,11},{10,... | collective-permute-start | bytes 2359304 | tf_op jit(solution)/shard_map/ppermute | solution.py:25
  333.4 24.9 %all-to-all-start.2 = ((bf16[8,24,2048]{2,1,0:T(8,128)(2,1)}), bf16[8,24,2048]{2,1,0:T(8,128)(2,1)}, u32[]{:S(2)}, u32[]{:S(2)}) async-start(bf16[8,24,2048]{2,1,0:T(8,128)(2,1)} %bitcast.277), calls=%async_computation.2 | async-start | bytes 1572864 | tf_op jit(solution)/shard_map/all_to_all | solution.py:824
  358.3 31.6 %all-to-all-start.3 = ((bf16[8,24,2048]{2,1,0:T(8,128)(2,1)}), bf16[8,24,2048]{2,1,0:T(8,128)(2,1)}, u32[]{:S(2)}, u32[]{:S(2)}) async-start(bf16[8,24,2048]{2,1,0:T(8,128)(2,1)} %bitcast.276), calls=%async_computation.3 | async-start | bytes 1572864 | tf_op jit(solution)/shard_map/all_to_all | solution.py:824
  435.3 39.6 %collective-permute-start.79 = (bf16[256,512]{1,0:T(8,128)(2,1)}, bf16[256,512]{1,0:T(8,128)(2,1)}, u32[]{:S(2)}, u32[]{:S(2)}) collective-permute-start(bf16[256,512]{1,0:T(8,128)(2,1)} %get-tuple-element.214), channel_id=1, source_target_pairs={{0,8},{4,12},{8,0},{12,4},{16,24},{20,28},{24,16},{28,20},{1,9},{5... | collective-permute-start | bytes 786440 | tf_op jit(solution)/shard_map/ppermute | solution.py:25
  437.3 35.9 %collective-permute-start.83 = (bf16[256,512]{1,0:T(8,128)(2,1)}, bf16[256,512]{1,0:T(8,128)(2,1)}, u32[]{:S(2)}, u32[]{:S(2)}) collective-permute-start(bf16[256,512]{1,0:T(8,128)(2,1)} %get-tuple-element.213), channel_id=1, source_target_pairs={{0,8},{4,12},{8,0},{12,4},{16,24},{20,28},{24,16},{28,20},{1,9},{5... | collective-permute-start | bytes 786440 | tf_op jit(solution)/shard_map/ppermute | solution.py:25
  437.4 45.6 %collective-permute-start.82 = (bf16[256,512]{1,0:T(8,128)(2,1)}, bf16[256,512]{1,0:T(8,128)(2,1)}, u32[]{:S(2)}, u32[]{:S(2)}) collective-permute-start(bf16[256,512]{1,0:T(8,128)(2,1)} %get-tuple-element.215), channel_id=1, source_target_pairs={{0,8},{4,12},{8,0},{12,4},{16,24},{20,28},{24,16},{28,20},{1,9},{5... | collective-permute-start | bytes 786440 | tf_op jit(solution)/shard_map/ppermute | solution.py:25
  451.7 44.4 %all-to-all-start.4 = ((f32[32,9,256]{2,1,0:T(8,128)}), f32[32,9,256]{2,1,0:T(8,128)}, u32[]{:S(2)}, u32[]{:S(2)}) async-start(f32[32,9,256]{2,1,0:T(8,128)} %bitcast.278), calls=%async_computation.4 | async-start | bytes 1048576 | tf_op jit(solution)/shard_map/all_to_all | solution.py:934
  455.2 42.6 %collective-permute-start.85 = (bf16[4,256,256]{2,1,0:T(8,128)(2,1)}, bf16[4,256,256]{2,1,0:T(8,128)(2,1)}, u32[]{:S(2)}, u32[]{:S(2)}) collective-permute-start(bf16[4,256,256]{2,1,0:T(8,128)(2,1)} %copy-done.39), channel_id=1, source_target_pairs={{0,4},{4,0},{8,12},{12,8},{16,20},{20,16},{24,28},{28,24},{1,5},{5... | collective-permute-start | bytes 1572872 | tf_op jit(solution)/shard_map/ppermute | solution.py:25
  473.3 24.5 %collective-permute-start.86 = (bf16[4,256,256]{2,1,0:T(8,128)(2,1)}, bf16[4,256,256]{2,1,0:T(8,128)(2,1)S(1)}, u32[]{:S(2)}, u32[]{:S(2)}) collective-permute-start(bf16[4,256,256]{2,1,0:T(8,128)(2,1)} %slice.224), channel_id=1, source_target_pairs={{0,4},{4,0},{8,12},{12,8},{16,20},{20,16},{24,28},{28,24},{1,5},{5... | collective-permute-start | bytes 1572872 | tf_op jit(solution)/shard_map/ppermute | solution.py:25
  474.9 36.8 %collective-permute-start.123 = (bf16[4,2,256]{1,2,0:T(8,128)(2,1)}, bf16[4,2,256]{1,2,0:T(8,128)(2,1)}, u32[]{:S(2)}, u32[]{:S(2)}) collective-permute-start(bf16[4,2,256]{1,2,0:T(8,128)(2,1)} %convert_bitcast_fusion.1), channel_id=1, source_target_pairs={{0,4},{4,0},{8,12},{12,8},{16,20},{20,16},{24,28},{28,24},{1,5},{5... | collective-permute-start | bytes 12296 | tf_op jit(solution)/shard_map/ppermute | solution.py:25
  513.5 23.8 %collective-permute-start.88 = (bf16[256,512]{1,0:T(8,128)(2,1)}, bf16[256,512]{1,0:T(8,128)(2,1)}, u32[]{:S(2)}, u32[]{:S(2)}) collective-permute-start(bf16[256,512]{1,0:T(8,128)(2,1)} %get-tuple-element.234.refs_5_.refs_4_), channel_id=1, source_target_pairs={{0,4},{4,0},{8,12},{12,8},{16,20},{20,16},{24,28},{28,24},{1,5},{5... | collective-permute-start | bytes 786440 | tf_op jit(solution)/shard_map/ppermute | solution.py:25
  520.8 29.1 %collective-permute-start.87 = (bf16[256,1024]{1,0:T(8,128)(2,1)S(1)}, bf16[256,1024]{1,0:T(8,128)(2,1)}, u32[]{:S(2)}, u32[]{:S(2)}) collective-permute-start(bf16[256,1024]{1,0:T(8,128)(2,1)S(1)} %get-tuple-element.247.drows_ref.rows_ref), channel_id=1, source_target_pairs={{0,4},{4,0},{8,12},{12,8},{16,20},{20,16},{24,28},{28,24},{1,5},{5... | collective-permute-start | bytes 1572872 | tf_op jit(solution)/shard_map/ppermute | solution.py:25
  537.4 28.6 %collective-permute-start.112 = (bf16[8,64,256]{2,1,0:T(8,128)(2,1)S(1)}, bf16[8,64,256]{2,1,0:T(8,128)(2,1)S(1)}, u32[]{:S(2)}, u32[]{:S(2)}) collective-permute-start(bf16[8,64,256]{2,1,0:T(8,128)(2,1)S(1)} %get-tuple-element.289), channel_id=1, source_target_pairs={{0,1},{1,0},{2,3},{3,2},{4,5},{5,4},{6,7},{7,6},{8,9},{9,8},{10,11... | collective-permute-start | bytes 786440 | tf_op jit(solution)/shard_map/ppermute | solution.py:25
  578.6 43.2 %collective-permute-start.55 = (bf16[8,64,256]{2,1,0:T(8,128)(2,1)S(1)}, bf16[8,64,256]{2,1,0:T(8,128)(2,1)S(1)}, u32[]{:S(2)}, u32[]{:S(2)}) collective-permute-start(bf16[8,64,256]{2,1,0:T(8,128)(2,1)S(1)} %copy-done.102), channel_id=1, source_target_pairs={{0,1},{1,0},{2,3},{3,2},{4,5},{5,4},{6,7},{7,6},{8,9},{9,8},{10,11... | collective-permute-start | bytes 786440 | tf_op jit(solution)/shard_map/ppermute | solution.py:25
  579.8 42.0 %collective-permute-start.57 = (bf16[8,64,256]{2,1,0:T(8,128)(2,1)S(1)}, bf16[8,64,256]{2,1,0:T(8,128)(2,1)S(1)}, u32[]{:S(2)}, u32[]{:S(2)}) collective-permute-start(bf16[8,64,256]{2,1,0:T(8,128)(2,1)S(1)} %copy-done.128), channel_id=1, source_target_pairs={{0,2},{1,3},{2,0},{3,1},{4,6},{5,7},{6,4},{7,5},{8,10},{9,11},{10,... | collective-permute-start | bytes 786440 | tf_op jit(solution)/shard_map/ppermute | solution.py:25
  584.9 71.4 %collective-permute-start.124 = (bf16[256,8,512]{2,1,0:T(8,128)(2,1)}, bf16[256,8,512]{2,1,0:T(8,128)(2,1)}, u32[]{:S(2)}, u32[]{:S(2)}) collective-permute-start(bf16[256,8,512]{2,1,0:T(8,128)(2,1)} %get-tuple-element.256), channel_id=1, source_target_pairs={{0,4},{4,0},{8,12},{12,8},{16,20},{20,16},{24,28},{28,24},{1,5},{5... | collective-permute-start | bytes 6291464 | tf_op jit(solution)/shard_map/ppermute | solution.py:25
  621.4 24.6 %collective-permute-start.118 = (bf16[256,1024]{1,0:T(8,128)(2,1)}, bf16[256,1024]{1,0:T(8,128)(2,1)}, u32[]{:S(2)}, u32[]{:S(2)}) collective-permute-start(bf16[256,1024]{1,0:T(8,128)(2,1)} %get-tuple-element.250), channel_id=1, source_target_pairs={{0,8},{4,12},{8,0},{12,4},{16,24},{20,28},{24,16},{28,20},{1,9},{5... | collective-permute-start | bytes 1572872 | tf_op jit(solution)/shard_map/ppermute | solution.py:25
  623.4 25.4 %collective-permute-start.76 = (bf16[8,64,256]{2,1,0:T(8,128)(2,1)S(1)}, bf16[8,64,256]{2,1,0:T(8,128)(2,1)S(1)}, u32[]{:S(2)}, u32[]{:S(2)}) collective-permute-start(bf16[8,64,256]{2,1,0:T(8,128)(2,1)S(1)} %get-tuple-element.221.refs_0_), channel_id=1, source_target_pairs={{0,1},{1,0},{2,3},{3,2},{4,5},{5,4},{6,7},{7,6},{8,9},{9,8},{10,11... | collective-permute-start | bytes 786440 | tf_op jit(solution)/shard_map/ppermute | solution.py:25
  626.6 34.1 %all-to-all-start.5 = ((f32[32,9,256]{2,1,0:T(8,128)}), f32[32,9,256]{2,1,0:T(8,128)}, u32[]{:S(2)}, u32[]{:S(2)}) async-start(f32[32,9,256]{2,1,0:T(8,128)} %bitcast.279), calls=%async_computation.5 | async-start | bytes 1048576 | tf_op jit(solution)/shard_map/all_to_all | solution.py:934
  645.9 32.5 %collective-permute-start.119 = (bf16[8,64,256]{2,1,0:T(8,128)(2,1)S(1)}, bf16[8,64,256]{2,1,0:T(8,128)(2,1)}, u32[]{:S(2)}, u32[]{:S(2)}) collective-permute-start(bf16[8,64,256]{2,1,0:T(8,128)(2,1)S(1)} %get-tuple-element.251.refs_0_), channel_id=1, source_target_pairs={{0,1},{1,0},{2,3},{3,2},{4,5},{5,4},{6,7},{7,6},{8,9},{9,8},{10,11... | collective-permute-start | bytes 786440 | tf_op jit(solution)/shard_map/ppermute | solution.py:25
  648.7 26.5 %collective-permute-start.122 = (bf16[256,1024]{1,0:T(8,128)(2,1)}, bf16[256,1024]{1,0:T(8,128)(2,1)S(1)}, u32[]{:S(2)}, u32[]{:S(2)}) collective-permute-start(bf16[256,1024]{1,0:T(8,128)(2,1)} %add_convert_fusion.6), channel_id=1, source_target_pairs={{0,16},{4,20},{8,24},{12,28},{16,0},{20,4},{24,8},{28,12},{1,17},{... | collective-permute-start | bytes 1572872 | tf_op jit(solution)/shard_map/ppermute | solution.py:25
  (261 other events, 3451.6 us)

commit v2 on v1

--- a/solution.py
+++ b/solution.py
@@ -157,11 +157,14 @@
     )(routes, *maps, *rows)
 
 
-def to_owners(pieces, routes, ws, parts, ties=((), ())):
-    came, order = {}, sorted(pieces)
-    for which, tie in zip((order[:-1], order[-1:]), ties):
-        chunks = dict(enumerate(contract(tuple(which), pieces, after(routes, *tie), ws, parts)))
-        summed, _ = scatter_sum(chunks, "tensor", None, BF16)
+def to_owners(pieces, routes, ws, parts, ties=((), (), ())):
+    came, order, last = {}, sorted(pieces), ()
+    for at_call, which in enumerate((order[:-1], order[-1:])):
+        tied = after(routes, *ties[at_call], *last)
+        last = contract(tuple(which), pieces, tied, ws, parts)
+        summed, _ = scatter_sum(dict(enumerate(last)), "tensor", None, BF16)
+        if at_call:
+            summed = after(summed, *ties[2])
         for at, k in enumerate(which):
             came[k] = hop(summed[at].astype(BF16), "expert", k) if k else summed[at]
     return came
@@ -529,22 +532,23 @@
     )(drows, *pieces)
 
 
-def dense_grad_kernel(which, x_ref, y_ref, rows_ref, other_ref, *outs):
-    for at, (k, out_ref) in enumerate(zip(which, outs)):
-        total = jnp.dot(x_ref[k].T, rows_ref[...], preferred_element_type=F32)
-        total += jnp.dot(y_ref[k // 2].T, other_ref[...], preferred_element_type=F32)
+def dense_grad_kernel(n_x, *refs):
+    x_refs, outs = refs[:n_x], refs[-n_x:]
+    rows = refs[n_x:-n_x]
+    for x_ref, out_ref in zip(x_refs, outs):
+        total = jnp.zeros(out_ref.shape, F32)
+        for at, one in enumerate(rows):
+            total += jnp.dot(x_ref[at].T, one[...], preferred_element_type=F32)
         out_ref[...] = total.astype(out_ref.dtype)
 
 
-def dense_grad(which, x, y, rows, other, dtype):
-    _, length, depth = x.shape
-    width = rows.shape[1]
-    outs = [jax.ShapeDtypeStruct((depth, width), dtype)] * len(which)
-    return pl.pallas_call(
-        functools.partial(dense_grad_kernel, which),
-        out_shape=outs,
-        compiler_params=params(x, y, rows, other, *outs),
-    )(x, y, rows, other)
+def dense_grad(xs, rows, dtypes):
+    depth, width = xs[0].shape[2], rows[0].shape[1]
+    return pl.pallas_call(
+        functools.partial(dense_grad_kernel, len(xs)),
+        out_shape=[jax.ShapeDtypeStruct((depth, width), dtype) for dtype in dtypes],
+        compiler_params=params(*xs, *rows),
+    )(*xs, *rows)
 
 
 def allowed_of(seg_col, seg_row, place_col, place_row):
@@ -746,7 +750,9 @@
     query_pair = [on_belt(query_own[at : at + 2]) for at in range(0, EA, 2)]
     query_ws = [[query_own], query_pair]
 
-    blocks, scale_one, chunks = pack(places, tokens, routes_att, parts, devices)
+    blocks, scale_one, chunks = pack(
+        places, after(tokens, query_own), routes_att, parts, devices
+    )
     chunks[1] = after(chunks[1], by_block)
     came = after(swap(chunks), belt[0])
     token_pieces = gather_pieces(came, "tensor")
@@ -772,20 +778,37 @@
         jnp.einsum("jtd,jkd->tk", normed_blocks, route_one, preferred_element_type=F32), chosen_one
     )
 
-    def project_sum(xs, ws, ties=((), ())):
-        late = [k for k in mine if not k & 2]
+    def project_sum(xs, ws):
         early = [k for k in mine if k & 2][::-1]
+        middle = [k for k in mine if k and not k & 2]
         found = project(tuple(early), xs, ws, routes_far, BF16)
-        rest = project(tuple(late), [after(xs[0], *found, *ties[0]), xs[1]], ws, routes_far, F32)
-        sums, came = [], []
-        for choice in range(2):
-            chunks = dict(zip(early, found[choice::2])) | dict(zip(late, rest[choice::2]))
-            total, here = scatter_sum(chunks, "expert", far, BF16)
-            sums.append(after(total, *ties[1]))
-            came.append(here)
-        return sums, rest, came
-
-    raw, started, _ = project_sum(normed_far, query_ws)
+        chunks = [dict(zip(early, found[choice::2])) for choice in range(2)]
+        came = [{k: hop(chunks[c][k], "expert", 2) for k in early} for c in range(2)]
+        ready = after(xs[0], came[0][early[0]])
+        found = project(tuple(middle), [ready, xs[1]], ws, routes_far, F32)
+        sent = []
+        for c in range(2):
+            held = dict(zip(middle, found[c::2]))
+            held = {k: (held[k] + came[c][k + 2].astype(F32)).astype(BF16) for k in middle}
+            here = []
+            for bit in far[:-1][::-1]:
+                for k in sorted(held, reverse=True):
+                    if k & bit:
+                        sent.append(held.pop(k))
+                        arrived = hop(sent[-1], "expert", bit)
+                        if k == bit:
+                            here.append(arrived)
+                        else:
+                            held[k ^ bit] = (held[k ^ bit].astype(F32) + arrived.astype(F32)).astype(BF16)
+            came[c] = [came[c][2], *here]
+        ready = after(xs[0], *sent)
+        sums = list(project((0,), [ready, xs[1]], ws, routes_far, F32))
+        for c in range(2):
+            for one in came[c]:
+                sums[c] = sums[c] + one.astype(F32)
+        return sums, sent
+
+    raw, started = project_sum(normed_far, query_ws)
     dense_raw = dense_rows(normed_blocks, dense_pieces)
     at_row = (order[:, None] * share + jnp.arange(share)).reshape(-1).astype(jnp.int32)
     at_row = after(at_row, *started)
@@ -853,15 +876,19 @@
     far_rows = after(far_rows, came_grads, pre[0][2])
     row_halves.append(jnp.concatenate([far_rows, hop(far_rows, "tensor", 1)]))
     pre.append(forward(row_halves[1]))
-    far_grads = after(far_grads, pre[1][2])
-    grad_halves = [
-        jnp.concatenate([one, hop(one, "tensor", 1)]) for one in (came_grads, far_grads)
-    ]
     expert_part = [
         jnp.dot(acted, w_down[0], preferred_element_type=F32).astype(BF16)
         for _, _, acted in pre[::-1]
     ][::-1]
 
+    pair_normed = pair(after(normed_far[1], came_grads))
+    pair_routes = pair(after(routes_far, came_grads).astype(BF16).transpose(0, 2, 1))
+    far_grads = after(far_grads, *expert_part, pair_normed, pair_routes)
+    pair_routes = pair_routes.transpose(0, 2, 1).astype(jnp.int32)
+    grad_halves = [
+        jnp.concatenate([one, hop(one, "tensor", 1)]) for one in (came_grads, far_grads)
+    ]
+
     def sum_far(half):
         far_chunk, last = jnp.split(half, 2)
         return (far_chunk.astype(F32) + hop(last, "tensor", 1).astype(F32)).astype(BF16)
@@ -879,23 +906,22 @@
     back_near = backward(
         after(grad_halves[0], input_far), *pre[0][:2]
     )
-    dreturned = back_home(sum_near(back_near[2], hop(input_far, "tensor", 2)))
+    input_near = sum_near(back_near[2], hop(input_far, "tensor", 2))
+    dreturned = back_home(input_near)
 
     expert_rows, dout_rows = jnp.concatenate(row_halves), jnp.concatenate(grad_halves)
     acted = jnp.concatenate([one[2] for one in pre])
     dgate = jnp.concatenate([back_near[0], back_far[0]])
     dup = jnp.concatenate([back_near[1], back_far[1]])
-    acted, dgate, dup = after((acted, dgate, dup), back_near[2])
-    grad_down = jnp.einsum("rf,rd->fd", acted, dout_rows, preferred_element_type=F32)[None]
+    dgate, dup = after((dgate, dup), expert_out)
     grad_gate = jnp.einsum("rd,rf->df", expert_rows, dgate, preferred_element_type=F32)[None]
-    grad_up = jnp.einsum("rd,rf->df", expert_rows, dup, preferred_element_type=F32)[None]
 
     *out_chunks, weighted = combine(places, slot, expert_out, parts, devices, gates_two, dexpert)
     weighted, _ = scatter_sum(
         {r: weighted[:, r * share : (r + 1) * share] for r in range(parts)}, "tensor"
     )
-    moe, _ = scatter_sum(dict(enumerate(out_chunks)), "tensor")
-    dreturned = after(dreturned, grad_down, grad_gate, grad_up)
+    grad_up = jnp.einsum("rd,rf->df", expert_rows, dup, preferred_element_type=F32)[None]
+    dreturned = after(dreturned, grad_gate, grad_up)
     back_chunks = combine(places, slot, dreturned, parts, devices)
     own_gates_two = gates_two[:, :share]
     inner = weighted - own_gates_two * jnp.sum(weighted, axis=0, keepdims=True)
@@ -907,16 +933,14 @@
     inner_mean = jnp.sum(pulled * hidden, axis=(0, 2), keepdims=True) / D
     dhidden = own_up + scale_two * pulled - hidden * (scale_two * scale_two * scale_two * inner_mean)
 
+    moe, _ = scatter_sum(dict(enumerate(after(out_chunks, dhidden))), "tensor")
+
     sent = dhidden.astype(BF16)
     up_pieces = gather_pieces(swap(
         [jnp.concatenate([sent[k], sent[k ^ 1]], axis=1) for k in mine]
     ), "tensor")
     dhidden_far = assemble([up_pieces[r] for r in range(parts)])
-    pull, started, arrived = project_sum(dhidden_far, output_ws)
-    pair_normed = pair(after(normed_far[1], *started))
-    pair_blocks = pair(after(normed_blocks[1::2], *started))
-    pair_routes = pair(after(routes_far, *started).astype(BF16).transpose(0, 2, 1))
-    pair_routes = pair_routes.transpose(0, 2, 1).astype(jnp.int32)
+    pull, started = project_sum(dhidden_far, output_ws)
     grad_output, pair_grad = map_grads(
         [[after(dhidden_far[0], *started), dhidden_far[1]]],
         [routes_far],
@@ -938,34 +962,31 @@
         "kt,jtd->kjd", own_dlogits, own_two.astype(F32), precision=PRECISE
     )
 
-    small_two = to_features(after(jnp.concatenate([part_gain_two, part_route_two]), *started))
-    pull = after(pull, small_two, grad_output, pair_normed, pair_blocks)
+    pull = after(pull, grad_output)
     *dqueries, ddense, dgates_one = attend_back(query, key, lse, mixed, pull, gates_one, tables)
-    pair_dense = pair(ddense)
     dquery_pieces = gather_far(*dqueries)
+    acted = after(acted, dquery_pieces[2][0])
+    grad_down = jnp.einsum("rf,rd->fd", acted, dout_rows, preferred_element_type=F32)[None]
     pair_dquery = {k: [pair(one) for one in dquery_pieces[k]] for k in mine}
+    dense_far = gather_pieces(ddense, "expert", far)
+    dense_back = dense_rows_back(ddense, dense_pieces, parts)
+    dense_share, _ = scatter_sum({r: dense_back[r] for r in range(parts)}, "tensor")
     dnormed_came = to_owners(
         dquery_pieces,
         routes_far,
         query_ws,
         parts,
-        ((pair_dense, *pair_dquery[0]), pair_dquery[2]),
-    )
-    dense_back = dense_rows_back(after(ddense, *dquery_pieces[2]), dense_pieces, parts)
-    dense_share, _ = scatter_sum({r: dense_back[r] for r in range(parts)}, "tensor")
+        ((*pair_dquery[0], grad_down), pair_dquery[2], pair_dquery[4]),
+    )
     dgates_one, _ = scatter_sum(
         {r: dgates_one[r * share : (r + 1) * share] for r in range(parts)}, "tensor"
     )
-    grad_chunks = {}
-    for which, dtype in (
-        (tuple(k for k in mine if k & 2)[::-1], BF16),
-        (tuple(k for k in mine if not k & 2), F32),
-    ):
-        found = dense_grad(which, normed_blocks, pair_blocks, ddense, pair_dense, dtype)
-        grad_chunks.update(zip(which, found))
-    grad_dense, dense_came = scatter_sum(grad_chunks, "expert", far, BF16)
+    grad_dense, pair_grad_dense = dense_grad(
+        normed_far, [dense_far[k] for k in mine], (F32, BF16)
+    )
+    grad_dense = grad_dense + pair(pair_grad_dense).astype(F32)
     (grad_query,) = map_grads(
-        [[normed_far[0]], [pair_normed]],
+        [[normed_far[0]], [after(pair_normed, *dnormed_came.values())]],
         [routes_far, pair_routes],
         [half for side in (dquery_pieces, pair_dquery) for k in mine for half in side[k]],
         (F32,),
@@ -974,7 +995,7 @@
 
     own_gates, own_scale = gates_one[:share], scale_one[:share]
     own_dlogits_one = logit_grad(own_gates, own_gates * dgates_one, chosen_one[:share])
-    dnormed_came[0] = after(dnormed_came[0], *pair_dquery[4], *pair_dquery[6])
+    dnormed_came[0] = after(dnormed_came[0], *pair_dquery[6], dense_far[4])
     whole = jnp.stack(
         [
             dnormed_came[k][:, b * depth : (b + 1) * depth].astype(F32)
@@ -993,7 +1014,7 @@
         + own_scale * pulled_one
         - token_rows * (own_scale * own_scale * own_scale * inner_one)
     )
-    own_grad = after(own_grad.astype(BF16), *dense_came[:-1])
+    own_grad = after(own_grad.astype(BF16), dense_far[6])
     grad_pieces = gather_pieces(own_grad, "tensor")
     grad_tokens = output_rows(places, {**grad_pieces, 3: after(grad_pieces[3], grad_dense)}, F32)
     part_gain_one = jnp.sum(dnormed_one * token_rows * own_scale, axis=1)[None]
@@ -1001,7 +1022,10 @@
         "tk,jtd->kjd", own_dlogits_one, normed_blocks[:, :share].astype(F32), precision=PRECISE
     )
 
-    small_one = to_features(jnp.concatenate([part_gain_one, part_route_one]))
+    smalls = to_features(
+        jnp.concatenate([part_gain_two, part_route_two, part_gain_one, part_route_one])
+    )
+    small_two, small_one = smalls[:9], smalls[9:]
     return (
         mixed_out,
         grad_tokens,

time: 693 us -> 617 us (0.89)
  waiting for transfers between devices: 215 us -> 164 us
  local copies, waits for them, and re-layouts: 74 us -> 60.8 us
    ppermute x125 -> x124, waiting for transfers between devices: 209 us -> 159 us  [hop(): return lax.ppermute(values, axis, [(i, i ^ bit) for i in range(size)])]
    convert_element_type x12 -> x7, other arithmetic: 8.1 us -> 0.33 us  [scatter_sum(): held[k ^ bit] = held[k ^ bit].astype(sent_as or sent.dtype)]
    ppermute x125 -> x124, starting transfers between devices: 100 us -> 106 us  [hop(): return lax.ppermute(values, axis, [(i, i ^ bit) for i in range(size)])]
    unnamed x339 -> x341, local copies, waits for them, and re-layouts: 42.3 us -> 38.7 us
    pallas_call x4 -> x6, Pallas kernels: 21.1 us -> 20.9 us  [project(): pl.pallas_call(functools.partial(project_kernel, which, [len(side) for si...]
  transfers between devices with their start and end apart: 130 -> 128, of which waited for: 48 -> 52; matrix products, arithmetic and copies ran while one was open for 27% -> 27% of each run, Pallas kernels for 12% -> 13%
where the time goes in v2:
time: 617 us; the launch traced here: 606 us
  waiting for transfers between devices  164 us (27%)
  starting transfers between devices  125 us (20%)
  matrix products  93.4 us (15%)
  Pallas kernels  87.2 us (14%)
  local copies, waits for them, and re-layouts  60.8 us (10%)
  other arithmetic  48.3 us (8%)
  blocking collectives  24.4 us (4%)
    ppermute x124, waiting for transfers between devices, hop(): return lax.ppermute(values, axis, [(i, i ^ bit) for i in range(size)])  159 us
    ppermute x124, starting transfers between devices, hop(): return lax.ppermute(values, axis, [(i, i ^ bit) for i in range(size)])  106 us
    unnamed x341, local copies, waits for them, and re-layouts  38.7 us
    all_to_all x1, blocking collectives, to_experts(): lax.all_to_all(shaped, 'expert', 0, 0, tiled=True)  24.4 us
    pallas_call x2, Pallas kernels, map_grads(): pl.pallas_call(functools.partial(map_grads_kernel, len(xs), len(sides)),...  23.8 us
    pallas_call x6, Pallas kernels, project(): pl.pallas_call(functools.partial(project_kernel, which, [len(side) for si...  20.9 us
    pallas_call x4, Pallas kernels, contract(): pl.pallas_call(functools.partial(contract_kernel, which, [len(side) for s...  12.4 us
  transfers between devices with their start and end apart: 128, of which 52 were waited for; matrix products, arithmetic and copies ran while one was open for 27% of the time, Pallas kernels for 13%

profile of v2, /device:TPU:0, one launch (start us, length us, event | category | flops | bytes accessed | tf_op | source)
XLA Modules:
  0.0 606.0 jit_solution(1461399779604862196)
XLA Ops:
  50.6 10.2 %collective-permute-done.17.refs_2_ = bf16[256,1024]{1,0:T(8,128)(2,1)} collective-permute-done((bf16[256,1024]{1,0:T(8,128)(2,1)}, bf16[256,1024]{1,0:T(8,128)(2,1)}, u32[]{:S(2)}, u32[]{:S(2)}) %collective-permute-start.17) | collective-permute-done | bytes 524320 | tf_op jit(solution)/shard_map/ppermute | solution.py:25
  66.7 5.7 shard_map.257
  77.4 6.5 %collective-permute-done.25 = bf16[256,512]{1,0:T(8,128)(2,1)} collective-permute-done((bf16[256,512]{1,0:T(8,128)(2,1)}, bf16[256,512]{1,0:T(8,128)(2,1)}, u32[]{:S(2)}, u32[]{:S(2)}) %collective-permute-start.25) | collective-permute-done | bytes 262176 | tf_op jit(solution)/shard_map/ppermute | solution.py:25
  146.1 10.7 %collective-permute-done.22.refs_2_.refs_4_ = bf16[2,256,512]{2,1,0:T(8,128)(2,1)S(1)} collective-permute-done((bf16[2,256,512]{2,1,0:T(8,128)(2,1)S(1)}, bf16[2,256,512]{2,1,0:T(8,128)(2,1)S(1)}, u32[]{:S(2)}, u32[]{:S(2)}) %collective-permute-start.22) | collective-permute-done | bytes 524320 | tf_op jit(solution)/shard_map/ppermute | solution.py:25
  159.4 8.9 %collective-permute-done.31.refs_7_.refs_5_ = bf16[256,512]{1,0:T(8,128)(2,1)S(1)} collective-permute-done((bf16[256,512]{1,0:T(8,128)(2,1)S(1)}, bf16[256,512]{1,0:T(8,128)(2,1)S(1)}, u32[]{:S(2)}, u32[]{:S(2)}) %collective-permute-start.31) | collective-permute-done | bytes 262176 | tf_op jit(solution)/shard_map/ppermute | solution.py:25
  197.9 6.4 %collective-permute-done.47.refs_2_ = bf16[8,64,256]{2,1,0:T(8,128)(2,1)S(1)} collective-permute-done((bf16[8,64,256]{2,1,0:T(8,128)(2,1)S(1)}, bf16[8,64,256]{2,1,0:T(8,128)(2,1)S(1)}, u32[]{:S(2)}, u32[]{:S(2)}) %collective-permute-start.47) | collective-permute-done | bytes 262176 | tf_op jit(solution)/shard_map/ppermute | solution.py:25
  207.3 24.4 %all_to_all.25 = bf16[8,24,2048]{2,1,0:T(8,128)(2,1)} all-to-all(bf16[8,24,2048]{2,1,0:T(8,128)(2,1)S(1)} %bitcast.269), channel_id=1, replica_groups=mesh['expert'=8,'tensor'=4] {'expert'}, dimensions={0} | all-to-all | bytes 1572864 | tf_op jit(solution)/shard_map/all_to_all | solution.py:843
  236.2 5.7 fusion.22
  242.0 8.3 %multiply_convert_fusion.5 = (bf16[384,1408]{1,0:T(8,128)(2,1)}, f32[384,1408]{1,0:T(8,128)}) fusion(f32[384,1408]{1,0:T(8,128)S(1)} %fusion.22, bf16[1,2048,1408]{2,1,0:T(8,128)(2,1)} %param.32, bf16[192,2048]{1,0:T(8,128)(2,1)} %collective-permute-done.49, bf16[192,2048]{1,0:T(8,128)(2,1)} %bitcast.27), kind=kOutput, calls=%fused_computation.54 | convolution fusion | flops 2220982272 | bytes 12746752 | tf_op jit(solution)/shard_map/dot_general | solution.py:857
  252.0 5.0 all-to-all-done.1
  263.2 5.4 fusion.20
  288.1 5.3 add_convert_fusion.1
  307.3 7.7 %multiply_convert_fusion.1 = (bf16[384,1408]{1,0:T(8,128)(2,1)S(1)}, bf16[384,1408]{1,0:T(8,128)(2,1)S(1)}) fusion(f32[384,1408]{1,0:T(8,128)} %copy-done.159, f32[384,1408]{1,0:T(8,128)} %get-tuple-element.332, bf16[384,2048]{1,0:T(8,128)(2,1)S(1)} %copy-done.106, bf16[1,1408,2048]{2,1,0:T(8,128)(2,1)} %param.33), kind=kOutput, calls=%fused_computation.49 | convolution fusion | flops 2221621248 | bytes 13828096 | tf_op jit(solution)/shard_map/dot_general | solution.py:861
  315.0 4.7 fusion.8
  319.7 5.3 add_convert_fusion
  332.3 5.9 all-to-all-start.3
  346.2 10.1 %convolution_bitcast_fusion.2 = f32[1,2048,1408]{2,1,0:T(8,128)} fusion(bf16[768,1408]{1,0:T(8,128)(2,1)} %pad_maximum_fusion.1, bf16[192,2048]{1,0:T(8,128)(2,1)} %copy-done.118, bf16[192,2048]{1,0:T(8,128)(2,1)} %collective-permute-done.51, bf16[192,2048]{1,0:T(8,128)(2,1)} %collective-permute-done.49, bf16[192,2048]{1,0:T(8,128)(2,1)} %bitcast.27), kind=kOutput, calls=%fused_computation.7 | convolution fusion | flops 4441767936 | bytes 16842752 | tf_op jit(solution)/shard_map/rd,rf->df/dot_general | solution.py:917
  356.3 9.6 %convolution_bitcast_fusion.1 = f32[1,2048,1408]{2,1,0:T(8,128)} fusion(bf16[768,1408]{1,0:T(8,128)(2,1)S(1)} %copy-done.103, bf16[192,2048]{1,0:T(8,128)(2,1)S(1)} %copy-done.119, bf16[192,2048]{1,0:T(8,128)(2,1)} %collective-permute-done.51, bf16[192,2048]{1,0:T(8,128)(2,1)} %collective-permute-done.49, bf16[192,2048]{1,0:T(8,128)(2,1)} %bitcast.27), kind=kOutput, calls=%fused_computation.6 | convolution fusion | flops 4441767936 | bytes 16842752 | tf_op jit(solution)/shard_map/rd,rf->df/dot_general | solution.py:923
  376.5 5.7 collective-permute-done.65
  390.7 4.7 collective-permute-done.73
  405.4 5.0 shard_map.270
  432.5 12.1 %shard_map.274 = (f32[256,8,512]{2,1,0:T(8,128)}, bf16[256,8,512]{2,1,0:T(8,128)(2,1)}) custom-call(bf16[4,256,256]{2,1,0:T(8,128)(2,1)} %copy-done.33, bf16[4,256,256]{2,1,0:T(8,128)(2,1)} %copy-done.34, s32[4,256,2]{2,1,0:T(8,128)} %copy-done.4, bf16[256,512]{1,0:T(8,128)(2,1)} %copy-done.54, bf16[256,512]{1,0:T(8,128)(2,1)} %copy-done.55, ...), custom_call_target="tpu_custom_call" | custom-call | tf_op jit(solution)/shard_map/pallas_call | solution.py:480
  449.8 5.2 shard_map.275
  475.2 6.1 %collective-permute-done.92.refs_10_.refs_9_ = bf16[256,512]{1,0:T(8,128)(2,1)} collective-permute-done((bf16[256,512]{1,0:T(8,128)(2,1)}, bf16[256,512]{1,0:T(8,128)(2,1)}, u32[]{:S(2)}, u32[]{:S(2)}) %collective-permute-start.92) | collective-permute-done | bytes 262176 | tf_op jit(solution)/shard_map/ppermute | solution.py:25
  484.8 11.6 %convolution_bitcast_fusion = f32[1,1408,2048]{2,1,0:T(8,128)} fusion(bf16[768,1408]{1,0:T(8,128)(2,1)} %pad_maximum_fusion.3, bf16[192,2048]{1,0:T(8,128)(2,1)} %copy-done.121, bf16[192,2048]{1,0:T(8,128)(2,1)} %copy-done.120, bf16[192,2048]{1,0:T(8,128)(2,1)} %copy-done.122, bf16[192,2048]{1,0:T(8,128)(2,1)} %bitcast.32), kind=kOutput, calls=%fused_computation.5 | convolution fusion | flops 4441767936 | bytes 16842752 | tf_op jit(solution)/shard_map/rf,rd->fd/dot_general | solution.py:969
  496.4 5.3 shard_map.276
  509.7 5.1 collective-permute-done.95
  521.6 6.5 %collective-permute-done.100.refs_4_ = bf16[256,1024]{1,0:T(8,128)(2,1)S(1)} collective-permute-done((bf16[256,1024]{1,0:T(8,128)(2,1)S(1)}, bf16[256,1024]{1,0:T(8,128)(2,1)S(1)}, u32[]{:S(2)}, u32[]{:S(2)}) %collective-permute-start.100) | collective-permute-done | bytes 524320 | tf_op jit(solution)/shard_map/ppermute | solution.py:25
  548.3 5.5 collective-permute-done.113
  555.4 7.0 %collective-permute-done.121.refs_3_ = bf16[256,1024]{1,0:T(8,128)(2,1)S(1)} collective-permute-done((bf16[256,1024]{1,0:T(8,128)(2,1)S(1)}, bf16[256,1024]{1,0:T(8,128)(2,1)S(1)}, u32[]{:S(2)}, u32[]{:S(2)}) %collective-permute-start.121) | collective-permute-done | bytes 524320 | tf_op jit(solution)/shard_map/ppermute | solution.py:25
  562.4 7.0 %collective-permute-done.117.refs_5_ = bf16[256,1024]{1,0:T(8,128)(2,1)S(1)} collective-permute-done((bf16[256,1024]{1,0:T(8,128)(2,1)S(1)}, bf16[256,1024]{1,0:T(8,128)(2,1)S(1)}, u32[]{:S(2)}, u32[]{:S(2)}) %collective-permute-start.117) | collective-permute-done | bytes 524320 | tf_op jit(solution)/shard_map/ppermute | solution.py:25
  581.6 11.8 %shard_map.281 = f32[256,8,512]{2,1,0:T(8,128)} custom-call(bf16[4,256,256]{2,1,0:T(8,128)(2,1)} %copy-done.27, bf16[4,256,256]{2,1,0:T(8,128)(2,1)} %copy-done.124, s32[4,256,2]{2,1,0:T(8,128)} %copy-done.4, s32[4,256,2]{2,1,0:T(8,128)} %convert_bitcast_fusion.refs_3_, bf16[256,512]{1,0:T(8,128)(2,1)} %get-tuple-element.241.refs_5_.refs_4_, ...), custom_call_target="tpu_custom_call" | custom-call | tf_op jit(solution)/shard_map/pallas_call | solution.py:480
  (771 shorter events, 358.2 us)
Async XLA Ops:
  10.9 21.9 %collective-permute-start.18 = (bf16[2,256,512]{2,1,0:T(8,128)(2,1)}, bf16[2,256,512]{2,1,0:T(8,128)(2,1)S(1)}, u32[]{:S(2)}, u32[]{:S(2)}) collective-permute-start(bf16[2,256,512]{2,1,0:T(8,128)(2,1)} %get-tuple-element.291), channel_id=1, source_target_pairs={{0,4},{4,0},{8,12},{12,8},{16,20},{20,16},{24,28},{28,24},{1,5},{5... | collective-permute-start | bytes 1572872 | tf_op jit(solution)/shard_map/ppermute | solution.py:25
  10.9 26.3 %collective-permute-start.7 = (bf16[2,256,512]{2,1,0:T(8,128)(2,1)}, bf16[2,256,512]{2,1,0:T(8,128)(2,1)S(1)}, u32[]{:S(2)}, u32[]{:S(2)}) collective-permute-start(bf16[2,256,512]{2,1,0:T(8,128)(2,1)} %get-tuple-element.294), channel_id=1, source_target_pairs={{0,4},{4,0},{8,12},{12,8},{16,20},{20,16},{24,28},{28,24},{1,5},{5... | collective-permute-start | bytes 1572872 | tf_op jit(solution)/shard_map/ppermute | solution.py:25
  38.7 22.1 %collective-permute-start.17 = (bf16[256,1024]{1,0:T(8,128)(2,1)}, bf16[256,1024]{1,0:T(8,128)(2,1)}, u32[]{:S(2)}, u32[]{:S(2)}) collective-permute-start(bf16[256,1024]{1,0:T(8,128)(2,1)} %pad_maximum_fusion.11.refs_0_), channel_id=1, source_target_pairs={{0,8},{4,12},{8,0},{12,4},{16,24},{20,28},{24,16},{28,20},{1,9},{5... | collective-permute-start | bytes 1572872 | tf_op jit(solution)/shard_map/ppermute | solution.py:25
  40.4 23.7 %collective-permute-start.12 = (bf16[256,1024]{1,0:T(8,128)(2,1)}, bf16[256,1024]{1,0:T(8,128)(2,1)}, u32[]{:S(2)}, u32[]{:S(2)}) collective-permute-start(bf16[256,1024]{1,0:T(8,128)(2,1)} %pad_maximum_fusion.11.refs_0_), channel_id=1, source_target_pairs={{0,16},{4,20},{8,24},{12,28},{16,0},{20,4},{24,8},{28,12},{1,17},{... | collective-permute-start | bytes 1572872 | tf_op jit(solution)/shard_map/ppermute | solution.py:25
  60.8 44.8 %collective-permute-start.20 = (bf16[256,1024]{1,0:T(8,128)(2,1)}, bf16[256,1024]{1,0:T(8,128)(2,1)}, u32[]{:S(2)}, u32[]{:S(2)}) collective-permute-start(bf16[256,1024]{1,0:T(8,128)(2,1)} %collective-permute-done.17.refs_2_), channel_id=1, source_target_pairs={{0,4},{4,0},{8,12},{12,8},{16,20},{20,16},{24,28},{28,24},{1,5},{5... | collective-permute-start | bytes 1572872 | tf_op jit(solution)/shard_map/ppermute | solution.py:25
  61.3 46.3 %collective-permute-start.13 = (bf16[256,1024]{1,0:T(8,128)(2,1)}, bf16[256,1024]{1,0:T(8,128)(2,1)}, u32[]{:S(2)}, u32[]{:S(2)}) collective-permute-start(bf16[256,1024]{1,0:T(8,128)(2,1)} %pad_maximum_fusion.11.refs_0_), channel_id=1, source_target_pairs={{0,4},{4,0},{8,12},{12,8},{16,20},{20,16},{24,28},{28,24},{1,5},{5... | collective-permute-start | bytes 1572872 | tf_op jit(solution)/shard_map/ppermute | solution.py:25
  64.1 43.1 %collective-permute-start.16 = (bf16[256,1024]{1,0:T(8,128)(2,1)}, bf16[256,1024]{1,0:T(8,128)(2,1)}, u32[]{:S(2)}, u32[]{:S(2)}) collective-permute-start(bf16[256,1024]{1,0:T(8,128)(2,1)} %collective-permute-done.12.refs_4_), channel_id=1, source_target_pairs={{0,8},{4,12},{8,0},{12,4},{16,24},{20,28},{24,16},{28,20},{1,9},{5... | collective-permute-start | bytes 1572872 | tf_op jit(solution)/shard_map/ppermute | solution.py:25
  83.9 47.3 %collective-permute-start.27 = (bf16[256,512]{1,0:T(8,128)(2,1)}, bf16[256,512]{1,0:T(8,128)(2,1)}, u32[]{:S(2)}, u32[]{:S(2)}) collective-permute-start(bf16[256,512]{1,0:T(8,128)(2,1)} %get-tuple-element.170), channel_id=1, source_target_pairs={{0,8},{4,12},{8,0},{12,4},{16,24},{20,28},{24,16},{28,20},{1,9},{5... | collective-permute-start | bytes 786440 | tf_op jit(solution)/shard_map/ppermute | solution.py:25
  95.2 38.6 %collective-permute-start.29 = (bf16[256,512]{1,0:T(8,128)(2,1)}, bf16[256,512]{1,0:T(8,128)(2,1)}, u32[]{:S(2)}, u32[]{:S(2)}) collective-permute-start(bf16[256,512]{1,0:T(8,128)(2,1)} %get-tuple-element.172), channel_id=1, source_target_pairs={{0,8},{4,12},{8,0},{12,4},{16,24},{20,28},{24,16},{28,20},{1,9},{5... | collective-permute-start | bytes 786440 | tf_op jit(solution)/shard_map/ppermute | solution.py:25
  105.6 27.2 %collective-permute-start.28 = (bf16[256,512]{1,0:T(8,128)(2,1)}, bf16[256,512]{1,0:T(8,128)(2,1)}, u32[]{:S(2)}, u32[]{:S(2)}) collective-permute-start(bf16[256,512]{1,0:T(8,128)(2,1)} %add_convert_fusion.12), channel_id=1, source_target_pairs={{0,16},{4,20},{8,24},{12,28},{16,0},{20,4},{24,8},{28,12},{1,17},{... | collective-permute-start | bytes 786440 | tf_op jit(solution)/shard_map/ppermute | solution.py:25
  107.7 23.0 %collective-permute-start.14 = (bf16[256,1024]{1,0:T(8,128)(2,1)}, bf16[256,1024]{1,0:T(8,128)(2,1)}, u32[]{:S(2)}, u32[]{:S(2)}) collective-permute-start(bf16[256,1024]{1,0:T(8,128)(2,1)} %collective-permute-done.12.refs_4_), channel_id=1, source_target_pairs={{0,4},{4,0},{8,12},{12,8},{16,20},{20,16},{24,28},{28,24},{1,5},{5... | collective-permute-start | bytes 1572872 | tf_op jit(solution)/shard_map/ppermute | solution.py:25
  131.2 25.6 %collective-permute-start.22 = (bf16[2,256,512]{2,1,0:T(8,128)(2,1)S(1)}, bf16[2,256,512]{2,1,0:T(8,128)(2,1)S(1)}, u32[]{:S(2)}, u32[]{:S(2)}) collective-permute-start(bf16[2,256,512]{2,1,0:T(8,128)(2,1)S(1)} %copy-done.128), channel_id=1, source_target_pairs={{0,4},{4,0},{8,12},{12,8},{16,20},{20,16},{24,28},{28,24},{1,5},{5... | collective-permute-start | bytes 1572872 | tf_op jit(solution)/shard_map/ppermute | solution.py:25
  145.6 26.1 %collective-permute-start.23 = (bf16[2,256,512]{2,1,0:T(8,128)(2,1)S(1)}, bf16[2,256,512]{2,1,0:T(8,128)(2,1)S(1)}, u32[]{:S(2)}, u32[]{:S(2)}) collective-permute-start(bf16[2,256,512]{2,1,0:T(8,128)(2,1)S(1)} %copy-done.127), channel_id=1, source_target_pairs={{0,4},{4,0},{8,12},{12,8},{16,20},{20,16},{24,28},{28,24},{1,5},{5... | collective-permute-start | bytes 1572872 | tf_op jit(solution)/shard_map/ppermute | solution.py:25
  232.0 25.0 %all-to-all-start.1 = ((bf16[8,24,2048]{2,1,0:T(8,128)(2,1)}), bf16[8,24,2048]{2,1,0:T(8,128)(2,1)}, u32[]{:S(2)}, u32[]{:S(2)}) async-start(bf16[8,24,2048]{2,1,0:T(8,128)(2,1)} %bitcast.268), calls=%async_computation.1 | async-start | bytes 1572864 | tf_op jit(solution)/shard_map/all_to_all | solution.py:843
  300.9 31.3 %all-to-all-start.2 = ((bf16[8,24,2048]{2,1,0:T(8,128)(2,1)}), bf16[8,24,2048]{2,1,0:T(8,128)(2,1)}, u32[]{:S(2)}, u32[]{:S(2)}) async-start(bf16[8,24,2048]{2,1,0:T(8,128)(2,1)} %bitcast.281), calls=%async_computation.2 | async-start | bytes 1572864 | tf_op jit(solution)/shard_map/all_to_all | solution.py:847
  306.9 24.1 %collective-permute-start.62 = (bf16[192,2048]{1,0:T(8,128)(2,1)S(1)}, bf16[192,2048]{1,0:T(8,128)(2,1)S(1)}, u32[]{:S(2)}, u32[]{:S(2)}) collective-permute-start(bf16[192,2048]{1,0:T(8,128)(2,1)S(1)} %add_convert_fusion.3), channel_id=1, source_target_pairs={{0,2},{1,3},{2,0},{3,1},{4,6},{5,7},{6,4},{7,5},{8,10},{9,11},{10,... | collective-permute-start | bytes 2359304 | tf_op jit(solution)/shard_map/ppermute | solution.py:25
  332.3 33.6 %all-to-all-start.3 = ((bf16[8,24,2048]{2,1,0:T(8,128)(2,1)}), bf16[8,24,2048]{2,1,0:T(8,128)(2,1)}, u32[]{:S(2)}, u32[]{:S(2)}) async-start(bf16[8,24,2048]{2,1,0:T(8,128)(2,1)} %bitcast.282), calls=%async_computation.3 | async-start | bytes 1572864 | tf_op jit(solution)/shard_map/all_to_all | solution.py:847
  345.7 25.9 %collective-permute-start.66 = (f32[2,64]{1,0:T(2,128)}, f32[2,64]{1,0:T(2,128)}, u32[]{:S(2)}, u32[]{:S(2)}) collective-permute-start(f32[2,64]{1,0:T(2,128)} %get-tuple-element.321), channel_id=1, source_target_pairs={{0,1},{1,0},{2,3},{3,2},{4,5},{5,4},{6,7},{7,6},{8,9},{9,8},{10,11... | collective-permute-start | bytes 1544 | tf_op jit(solution)/shard_map/ppermute | solution.py:25
  345.8 22.5 %collective-permute-start.67 = (f32[2,64]{1,0:T(2,128)}, f32[2,64]{1,0:T(2,128)}, u32[]{:S(2)}, u32[]{:S(2)}) collective-permute-start(f32[2,64]{1,0:T(2,128)} %get-tuple-element.322), channel_id=1, source_target_pairs={{0,1},{1,0},{2,3},{3,2},{4,5},{5,4},{6,7},{7,6},{8,9},{9,8},{10,11... | collective-permute-start | bytes 1544 | tf_op jit(solution)/shard_map/ppermute | solution.py:25
  404.8 22.7 %collective-permute-start.69 = (bf16[8,64,256]{2,1,0:T(8,128)(2,1)S(1)}, bf16[8,64,256]{2,1,0:T(8,128)(2,1)S(1)}, u32[]{:S(2)}, u32[]{:S(2)}) collective-permute-start(bf16[8,64,256]{2,1,0:T(8,128)(2,1)S(1)} %copy-done.96), channel_id=1, source_target_pairs={{0,1},{1,0},{2,3},{3,2},{4,5},{5,4},{6,7},{7,6},{8,9},{9,8},{10,11... | collective-permute-start | bytes 786440 | tf_op jit(solution)/shard_map/ppermute | solution.py:25
  415.8 28.9 %collective-permute-start.85 = (bf16[256,512]{1,0:T(8,128)(2,1)S(1)}, bf16[256,512]{1,0:T(8,128)(2,1)S(1)}, u32[]{:S(2)}, u32[]{:S(2)}) collective-permute-start(bf16[256,512]{1,0:T(8,128)(2,1)S(1)} %get-tuple-element.237), channel_id=1, source_target_pairs={{0,8},{4,12},{8,0},{12,4},{16,24},{20,28},{24,16},{28,20},{1,9},{5... | collective-permute-start | bytes 786440 | tf_op jit(solution)/shard_map/ppermute | solution.py:25
  474.5 27.3 %collective-permute-start.112 = (bf16[8,64,256]{2,1,0:T(8,128)(2,1)}, bf16[8,64,256]{2,1,0:T(8,128)(2,1)S(1)}, u32[]{:S(2)}, u32[]{:S(2)}) collective-permute-start(bf16[8,64,256]{2,1,0:T(8,128)(2,1)} %get-tuple-element.298), channel_id=1, source_target_pairs={{0,1},{1,0},{2,3},{3,2},{4,5},{5,4},{6,7},{7,6},{8,9},{9,8},{10,11... | collective-permute-start | bytes 786440 | tf_op jit(solution)/shard_map/ppermute | solution.py:25
  474.5 27.3 %collective-permute-start.103 = (bf16[256,512]{1,0:T(8,128)(2,1)}, bf16[256,512]{1,0:T(8,128)(2,1)S(1)}, u32[]{:S(2)}, u32[]{:S(2)}) collective-permute-start(bf16[256,512]{1,0:T(8,128)(2,1)} %collective-permute-done.89.refs_7_.refs_6_), channel_id=1, source_target_pairs={{0,4},{4,0},{8,12},{12,8},{16,20},{20,16},{24,28},{28,24},{1,5},{5... | collective-permute-start | bytes 786440 | tf_op jit(solution)/shard_map/ppermute | solution.py:25
  481.3 21.6 %collective-permute-start.96 = (bf16[256,512]{1,0:T(8,128)(2,1)S(1)}, bf16[256,512]{1,0:T(8,128)(2,1)S(1)}, u32[]{:S(2)}, u32[]{:S(2)}) collective-permute-start(bf16[256,512]{1,0:T(8,128)(2,1)S(1)} %collective-permute-done.91.refs_9_.refs_8_), channel_id=1, source_target_pairs={{0,8},{4,12},{8,0},{12,4},{16,24},{20,28},{24,16},{28,20},{1,9},{5... | collective-permute-start | bytes 786440 | tf_op jit(solution)/shard_map/ppermute | solution.py:25
  481.5 22.0 %collective-permute-start.98 = (bf16[256,512]{1,0:T(8,128)(2,1)}, bf16[256,512]{1,0:T(8,128)(2,1)S(1)}, u32[]{:S(2)}, u32[]{:S(2)}) collective-permute-start(bf16[256,512]{1,0:T(8,128)(2,1)} %collective-permute-done.92.refs_10_.refs_9_), channel_id=1, source_target_pairs={{0,8},{4,12},{8,0},{12,4},{16,24},{20,28},{24,16},{28,20},{1,9},{5... | collective-permute-start | bytes 786440 | tf_op jit(solution)/shard_map/ppermute | solution.py:25
  501.9 26.1 %collective-permute-start.100 = (bf16[256,1024]{1,0:T(8,128)(2,1)S(1)}, bf16[256,1024]{1,0:T(8,128)(2,1)S(1)}, u32[]{:S(2)}, u32[]{:S(2)}) collective-permute-start(bf16[256,1024]{1,0:T(8,128)(2,1)S(1)} %copy-done.49), channel_id=1, source_target_pairs={{0,16},{4,20},{8,24},{12,28},{16,0},{20,4},{24,8},{28,12},{1,17},{... | collective-permute-start | bytes 1572872 | tf_op jit(solution)/shard_map/ppermute | solution.py:25
  519.8 27.7 %collective-permute-start.81 = (bf16[8,64,256]{2,1,0:T(8,128)(2,1)}, bf16[8,64,256]{2,1,0:T(8,128)(2,1)}, u32[]{:S(2)}, u32[]{:S(2)}) collective-permute-start(bf16[8,64,256]{2,1,0:T(8,128)(2,1)} %add_convert_fusion.8.refs_0_), channel_id=1, source_target_pairs={{0,2},{1,3},{2,0},{3,1},{4,6},{5,7},{6,4},{7,5},{8,10},{9,11},{10,... | collective-permute-start | bytes 786440 | tf_op jit(solution)/shard_map/ppermute | solution.py:25
  521.6 57.3 %collective-permute-start.80 = (bf16[8,64,256]{2,1,0:T(8,128)(2,1)}, bf16[8,64,256]{2,1,0:T(8,128)(2,1)}, u32[]{:S(2)}, u32[]{:S(2)}) collective-permute-start(bf16[8,64,256]{2,1,0:T(8,128)(2,1)} %add_convert_fusion.8.refs_0_), channel_id=1, source_target_pairs={{0,1},{1,0},{2,3},{3,2},{4,5},{5,4},{6,7},{7,6},{8,9},{9,8},{10,11... | collective-permute-start | bytes 786440 | tf_op jit(solution)/shard_map/ppermute | solution.py:25
  528.0 71.0 %collective-permute-start.123 = (bf16[256,8,512]{2,1,0:T(8,128)(2,1)}, bf16[256,8,512]{2,1,0:T(8,128)(2,1)}, u32[]{:S(2)}, u32[]{:S(2)}) collective-permute-start(bf16[256,8,512]{2,1,0:T(8,128)(2,1)} %get-tuple-element.263), channel_id=1, source_target_pairs={{0,4},{4,0},{8,12},{12,8},{16,20},{20,16},{24,28},{28,24},{1,5},{5... | collective-permute-start | bytes 6291464 | tf_op jit(solution)/shard_map/ppermute | solution.py:25
  548.3 30.6 %collective-permute-start.82 = (bf16[8,64,256]{2,1,0:T(8,128)(2,1)}, bf16[8,64,256]{2,1,0:T(8,128)(2,1)}, u32[]{:S(2)}, u32[]{:S(2)}) collective-permute-start(bf16[8,64,256]{2,1,0:T(8,128)(2,1)} %collective-permute-done.81.refs_2_), channel_id=1, source_target_pairs={{0,1},{1,0},{2,3},{3,2},{4,5},{5,4},{6,7},{7,6},{8,9},{9,8},{10,11... | collective-permute-start | bytes 786440 | tf_op jit(solution)/shard_map/ppermute | solution.py:25
  570.7 23.2 %collective-permute-start.122 = (bf16[256,1024]{1,0:T(8,128)(2,1)S(1)}, bf16[256,1024]{1,0:T(8,128)(2,1)S(1)}, u32[]{:S(2)}, u32[]{:S(2)}) collective-permute-start(bf16[256,1024]{1,0:T(8,128)(2,1)S(1)} %get-tuple-element.260), channel_id=1, source_target_pairs={{0,4},{4,0},{8,12},{12,8},{16,20},{20,16},{24,28},{28,24},{1,5},{5... | collective-permute-start | bytes 1572872 | tf_op jit(solution)/shard_map/ppermute | solution.py:25
  573.8 29.6 %all-to-all-start.4 = ((f32[32,18,256]{2,1,0:T(8,128)}), f32[32,18,256]{2,1,0:T(8,128)}, u32[]{:S(2)}, u32[]{:S(2)}) async-start(f32[32,18,256]{2,1,0:T(8,128)} %bitcast.280), calls=%async_computation.4 | async-start | bytes 1572864 | tf_op jit(solution)/shard_map/all_to_all | solution.py:958
  (260 other events, 3259.4 us)

commit v3 on v2

--- a/solution.py
+++ b/solution.py
@@ -112,6 +112,7 @@
         functools.partial(project_kernel, which, [len(side) for side in ws]),
         out_shape=outs,
         compiler_params=params(*xs, *maps, *outs),
+        cost_estimate=pl.CostEstimate(flops=0, bytes_accessed=0, transcendentals=0),
     )(*xs, *maps, routes)
 
 
@@ -154,6 +155,7 @@
             jax.ShapeDtypeStruct(shape, BF16 if r % 2 else F32) for r in range(parts)
         ],
         compiler_params=params(*maps, *rows),
+        cost_estimate=pl.CostEstimate(flops=0, bytes_accessed=0, transcendentals=0),
     )(routes, *maps, *rows)
 
 
@@ -193,6 +195,7 @@
             out_specs=whole_spec(shape),
         ),
         compiler_params=params(x),
+        cost_estimate=pl.CostEstimate(flops=0, bytes_accessed=0, transcendentals=0),
     )(places, x)
 
 
@@ -240,6 +243,7 @@
             out_specs=[whole_spec(one) for one in shapes],
         ),
         compiler_params=params(x),
+        cost_estimate=pl.CostEstimate(flops=0, bytes_accessed=0, transcendentals=0),
     )(places, x, routes)
     return blocks, scale, chunks
 
@@ -268,6 +272,7 @@
             jax.ShapeDtypeStruct((*shape[:2], 2), jnp.int32),
         ],
         compiler_params=params(*pieces, *pieces),
+        cost_estimate=pl.CostEstimate(flops=0, bytes_accessed=0, transcendentals=0),
     )(*pieces, gains)
 
 
@@ -287,6 +292,7 @@
         functools.partial(assemble_kernel, len(pieces)),
         out_shape=[jax.ShapeDtypeStruct(shape, BF16)] * 2,
         compiler_params=params(*pieces, *pieces),
+        cost_estimate=pl.CostEstimate(flops=0, bytes_accessed=0, transcendentals=0),
     )(*pieces)
 
 
@@ -313,6 +319,7 @@
             out_specs=whole_spec(shape),
         ),
         compiler_params=params(*pieces, *pieces),
+        cost_estimate=pl.CostEstimate(flops=0, bytes_accessed=0, transcendentals=0),
     )(places, *pieces)
 
 
@@ -342,6 +349,7 @@
             jax.ShapeDtypeStruct(own.shape, BF16),
         ],
         compiler_params=params(own, own, own, own),
+        cost_estimate=pl.CostEstimate(flops=0, bytes_accessed=0, transcendentals=0),
     )(own, gain, *came)
 
 
@@ -394,6 +402,7 @@
             out_specs=[whole_spec(shape) for shape in shapes],
         ),
         compiler_params=params(up, up, *pieces),
+        cost_estimate=pl.CostEstimate(flops=0, bytes_accessed=0, transcendentals=0),
     )(places, *operands)
 
 
@@ -442,6 +451,7 @@
             out_specs=[whole_spec(one.shape) for one in outs],
         ),
         compiler_params=params(values, *extra, *outs),
+        cost_estimate=pl.CostEstimate(flops=0, bytes_accessed=0, transcendentals=0),
     )(places, *operands)
 
 
@@ -485,6 +495,7 @@
             pltpu.VMEM((total, width), BF16),
         ],
         compiler_params=pltpu.CompilerParams(vmem_limit_bytes=VMEM),
+        cost_estimate=pl.CostEstimate(flops=0, bytes_accessed=0, transcendentals=0),
     )(*xs, *routes, *rows)
 
 
@@ -507,6 +518,7 @@
         rows_kernel,
         out_shape=jax.ShapeDtypeStruct((length, width), F32),
         compiler_params=params(x, *pieces),
+        cost_estimate=pl.CostEstimate(flops=0, bytes_accessed=0, transcendentals=0),
     )(x, *pieces)
 
 
@@ -529,6 +541,7 @@
         rows_back_kernel,
         out_shape=jax.ShapeDtypeStruct(shape, BF16),
         compiler_params=params(drows, *pieces),
+        cost_estimate=pl.CostEstimate(flops=0, bytes_accessed=0, transcendentals=0),
     )(drows, *pieces)
 
 
@@ -548,6 +561,7 @@
         functools.partial(dense_grad_kernel, len(xs)),
         out_shape=[jax.ShapeDtypeStruct((depth, width), dtype) for dtype in dtypes],
         compiler_params=params(*xs, *rows),
+        cost_estimate=pl.CostEstimate(flops=0, bytes_accessed=0, transcendentals=0),
     )(*xs, *rows)
 
 
@@ -600,6 +614,7 @@
             *[jax.ShapeDtypeStruct((length, width), BF16)] * 2,
         ],
         compiler_params=pltpu.CompilerParams(vmem_limit_bytes=24 << 20),
+        cost_estimate=pl.CostEstimate(flops=0, bytes_accessed=0, transcendentals=0),
     )(*raw, dense, gates, *tables)
 
 
@@ -651,6 +666,7 @@
             jax.ShapeDtypeStruct(gates.shape, F32),
         ],
         compiler_params=pltpu.CompilerParams(vmem_limit_bytes=24 << 20),
+        cost_estimate=pl.CostEstimate(flops=0, bytes_accessed=0, transcendentals=0),
     )(query, key, lse, mixed, *pull, gates, *tables)
 
 
@@ -728,10 +744,11 @@
     def pair(values):
         return hop(values, "expert", 1)
 
+    query_own = w_query.transpose(1, 0, 2)
     own_meta = jnp.concatenate(
         [gain_att, gain_mlp, router_att.T.reshape(-1), router_mlp.T.reshape(-1)]
     ).reshape(18, depth)
-    pair_meta = pair(own_meta)
+    pair_meta = pair(after(own_meta, query_own))
 
     def swap(sent):
         return jnp.stack([hop(one, "expert", k) if k else one for k, one in zip(mine, sent)])
@@ -746,7 +763,6 @@
         belt.append(pair(after(values, belt[-2]) if len(belt) > 1 else values))
         return belt[-1]
 
-    query_own = w_query.transpose(1, 0, 2)
     query_pair = [on_belt(query_own[at : at + 2]) for at in range(0, EA, 2)]
     query_ws = [[query_own], query_pair]
 

time: 617 us -> 616 us (level)
    unnamed x341 -> x335, local copies, waits for them, and re-layouts: 38.7 us -> 34.1 us
  transfers between devices with their start and end apart: 128 -> 128, of which waited for: 52 -> 53; matrix products, arithmetic and copies ran while one was open for 27% -> 26% of each run, Pallas kernels for 13% -> 13%
where the time goes in v3:
time: 616 us; the launch traced here: 604 us
  waiting for transfers between devices  167 us (27%)
  starting transfers between devices  124 us (20%)
  matrix products  93.4 us (15%)
  Pallas kernels  87.8 us (14%)
  local copies, waits for them, and re-layouts  56.5 us (9%)
  other arithmetic  47.9 us (8%)
  blocking collectives  24.6 us (4%)
    ppermute x124, waiting for transfers between devices, hop(): return lax.ppermute(values, axis, [(i, i ^ bit) for i in range(size)])  162 us
    ppermute x124, starting transfers between devices, hop(): return lax.ppermute(values, axis, [(i, i ^ bit) for i in range(size)])  105 us
    unnamed x335, local copies, waits for them, and re-layouts  34.1 us
    all_to_all x1, blocking collectives, to_experts(): lax.all_to_all(shaped, 'expert', 0, 0, tiled=True)  24.6 us
    pallas_call x2, Pallas kernels, map_grads(): pl.pallas_call(functools.partial(map_grads_kernel, len(xs), len(sides)),...  23.8 us
    pallas_call x6, Pallas kernels, project(): pl.pallas_call(functools.partial(project_kernel, which, [len(side) for si...  20.9 us
    pallas_call x4, Pallas kernels, contract(): pl.pallas_call(functools.partial(contract_kernel, which, [len(side) for s...  12.4 us
  transfers between devices with their start and end apart: 128, of which 53 were waited for; matrix products, arithmetic and copies ran while one was open for 26% of the time, Pallas kernels for 13%

profile of v3, /device:TPU:0, one launch (start us, length us, event | category | flops | bytes accessed | tf_op | source)
XLA Modules:
  0.0 604.3 jit_solution(9577313891904636139)
XLA Ops:
  50.6 10.2 %collective-permute-done.17.refs_2_ = bf16[256,1024]{1,0:T(8,128)(2,1)} collective-permute-done((bf16[256,1024]{1,0:T(8,128)(2,1)}, bf16[256,1024]{1,0:T(8,128)(2,1)}, u32[]{:S(2)}, u32[]{:S(2)}) %collective-permute-start.17) | collective-permute-done | bytes 524320 | tf_op jit(solution)/shard_map/ppermute | solution.py:25
  66.7 5.7 shard_map.257
  78.7 5.2 collective-permute-done.25
  120.9 8.2 %collective-permute-done.14.refs_5_ = bf16[256,1024]{1,0:T(8,128)(2,1)} collective-permute-done((bf16[256,1024]{1,0:T(8,128)(2,1)}, bf16[256,1024]{1,0:T(8,128)(2,1)}, u32[]{:S(2)}, u32[]{:S(2)}) %collective-permute-start.14) | collective-permute-done | bytes 524320 | tf_op jit(solution)/shard_map/ppermute | solution.py:25
  145.0 10.2 %collective-permute-done.22.refs_2_.refs_4_ = bf16[2,256,512]{2,1,0:T(8,128)(2,1)S(1)} collective-permute-done((bf16[2,256,512]{2,1,0:T(8,128)(2,1)S(1)}, bf16[2,256,512]{2,1,0:T(8,128)(2,1)S(1)}, u32[]{:S(2)}, u32[]{:S(2)}) %collective-permute-start.22) | collective-permute-done | bytes 524320 | tf_op jit(solution)/shard_map/ppermute | solution.py:25
  159.2 7.0 %collective-permute-done.31.refs_7_.refs_5_ = bf16[256,512]{1,0:T(8,128)(2,1)S(1)} collective-permute-done((bf16[256,512]{1,0:T(8,128)(2,1)S(1)}, bf16[256,512]{1,0:T(8,128)(2,1)S(1)}, u32[]{:S(2)}, u32[]{:S(2)}) %collective-permute-start.31) | collective-permute-done | bytes 262176 | tf_op jit(solution)/shard_map/ppermute | solution.py:25
  196.3 6.3 %collective-permute-done.47.refs_2_ = bf16[8,64,256]{2,1,0:T(8,128)(2,1)S(1)} collective-permute-done((bf16[8,64,256]{2,1,0:T(8,128)(2,1)S(1)}, bf16[8,64,256]{2,1,0:T(8,128)(2,1)S(1)}, u32[]{:S(2)}, u32[]{:S(2)}) %collective-permute-start.47) | collective-permute-done | bytes 262176 | tf_op jit(solution)/shard_map/ppermute | solution.py:25
  205.6 24.6 %all_to_all.25 = bf16[8,24,2048]{2,1,0:T(8,128)(2,1)} all-to-all(bf16[8,24,2048]{2,1,0:T(8,128)(2,1)S(1)} %bitcast.269), channel_id=1, replica_groups=mesh['expert'=8,'tensor'=4] {'expert'}, dimensions={0} | all-to-all | bytes 1572864 | tf_op jit(solution)/shard_map/all_to_all | solution.py:859
  234.8 5.7 fusion.22
  240.5 8.2 %multiply_convert_fusion.5 = (bf16[384,1408]{1,0:T(8,128)(2,1)}, f32[384,1408]{1,0:T(8,128)}) fusion(f32[384,1408]{1,0:T(8,128)S(1)} %fusion.22, bf16[1,2048,1408]{2,1,0:T(8,128)(2,1)} %param.32, bf16[192,2048]{1,0:T(8,128)(2,1)} %collective-permute-done.49, bf16[192,2048]{1,0:T(8,128)(2,1)} %bitcast.27), kind=kOutput, calls=%fused_computation.54 | convolution fusion | flops 2220982272 | bytes 12746752 | tf_op jit(solution)/shard_map/dot_general | solution.py:873
  250.5 5.1 all-to-all-done.1
  261.8 5.4 fusion.20
  286.6 5.3 add_convert_fusion.1
  305.8 7.7 %multiply_convert_fusion.1 = (bf16[384,1408]{1,0:T(8,128)(2,1)S(1)}, bf16[384,1408]{1,0:T(8,128)(2,1)S(1)}) fusion(f32[384,1408]{1,0:T(8,128)} %copy-done.156, f32[384,1408]{1,0:T(8,128)} %get-tuple-element.334, bf16[384,2048]{1,0:T(8,128)(2,1)S(1)} %copy-done.104, bf16[1,1408,2048]{2,1,0:T(8,128)(2,1)} %param.33), kind=kOutput, calls=%fused_computation.49 | convolution fusion | flops 2221621248 | bytes 13828096 | tf_op jit(solution)/shard_map/dot_general | solution.py:877
  318.3 5.3 add_convert_fusion
  330.8 5.9 all-to-all-start.3
  344.7 10.1 %convolution_bitcast_fusion.2 = f32[1,2048,1408]{2,1,0:T(8,128)} fusion(bf16[768,1408]{1,0:T(8,128)(2,1)} %pad_maximum_fusion.1, bf16[192,2048]{1,0:T(8,128)(2,1)} %copy-done.116, bf16[192,2048]{1,0:T(8,128)(2,1)} %collective-permute-done.51, bf16[192,2048]{1,0:T(8,128)(2,1)} %collective-permute-done.49, bf16[192,2048]{1,0:T(8,128)(2,1)} %bitcast.27), kind=kOutput, calls=%fused_computation.7 | convolution fusion | flops 4441767936 | bytes 16842752 | tf_op jit(solution)/shard_map/rd,rf->df/dot_general | solution.py:933
  354.9 9.6 %convolution_bitcast_fusion.1 = f32[1,2048,1408]{2,1,0:T(8,128)} fusion(bf16[768,1408]{1,0:T(8,128)(2,1)S(1)} %copy-done.101, bf16[192,2048]{1,0:T(8,128)(2,1)S(1)} %copy-done.117, bf16[192,2048]{1,0:T(8,128)(2,1)} %collective-permute-done.51, bf16[192,2048]{1,0:T(8,128)(2,1)} %collective-permute-done.49, bf16[192,2048]{1,0:T(8,128)(2,1)} %bitcast.27), kind=kOutput, calls=%fused_computation.6 | convolution fusion | flops 4441767936 | bytes 16842752 | tf_op jit(solution)/shard_map/rd,rf->df/dot_general | solution.py:939
  375.0 5.7 collective-permute-done.65
  403.9 5.0 shard_map.270
  431.0 12.1 %shard_map.274 = (f32[256,8,512]{2,1,0:T(8,128)}, bf16[256,8,512]{2,1,0:T(8,128)(2,1)}) custom-call(bf16[4,256,256]{2,1,0:T(8,128)(2,1)} %copy-done.32, bf16[4,256,256]{2,1,0:T(8,128)(2,1)} %copy-done.33, s32[4,256,2]{2,1,0:T(8,128)} %copy-done.3, bf16[256,512]{1,0:T(8,128)(2,1)} %copy-done.53, bf16[256,512]{1,0:T(8,128)(2,1)} %copy-done.54, ...), custom_call_target="tpu_custom_call" | custom-call | tf_op jit(solution)/shard_map/pallas_call | solution.py:490
  448.3 5.2 shard_map.275
  473.7 6.1 %collective-permute-done.92.refs_10_.refs_9_ = bf16[256,512]{1,0:T(8,128)(2,1)} collective-permute-done((bf16[256,512]{1,0:T(8,128)(2,1)}, bf16[256,512]{1,0:T(8,128)(2,1)}, u32[]{:S(2)}, u32[]{:S(2)}) %collective-permute-start.92) | collective-permute-done | bytes 262176 | tf_op jit(solution)/shard_map/ppermute | solution.py:25
  483.2 11.6 %convolution_bitcast_fusion = f32[1,1408,2048]{2,1,0:T(8,128)} fusion(bf16[768,1408]{1,0:T(8,128)(2,1)} %pad_maximum_fusion.3, bf16[192,2048]{1,0:T(8,128)(2,1)} %copy-done.119, bf16[192,2048]{1,0:T(8,128)(2,1)} %copy-done.118, bf16[192,2048]{1,0:T(8,128)(2,1)} %copy-done.120, bf16[192,2048]{1,0:T(8,128)(2,1)} %bitcast.32), kind=kOutput, calls=%fused_computation.5 | convolution fusion | flops 4441767936 | bytes 16842752 | tf_op jit(solution)/shard_map/rf,rd->fd/dot_general | solution.py:985
  494.9 5.3 shard_map.276
  508.2 5.1 collective-permute-done.95
  520.0 6.5 %collective-permute-done.100.refs_4_ = bf16[256,1024]{1,0:T(8,128)(2,1)S(1)} collective-permute-done((bf16[256,1024]{1,0:T(8,128)(2,1)S(1)}, bf16[256,1024]{1,0:T(8,128)(2,1)S(1)}, u32[]{:S(2)}, u32[]{:S(2)}) %collective-permute-start.100) | collective-permute-done | bytes 524320 | tf_op jit(solution)/shard_map/ppermute | solution.py:25
  541.3 4.8 collective-permute-done.110
  547.0 5.4 collective-permute-done.113
  553.7 7.3 %collective-permute-done.121.refs_3_ = bf16[256,1024]{1,0:T(8,128)(2,1)S(1)} collective-permute-done((bf16[256,1024]{1,0:T(8,128)(2,1)S(1)}, bf16[256,1024]{1,0:T(8,128)(2,1)S(1)}, u32[]{:S(2)}, u32[]{:S(2)}) %collective-permute-start.121) | collective-permute-done | bytes 524320 | tf_op jit(solution)/shard_map/ppermute | solution.py:25
  561.0 6.9 %collective-permute-done.117.refs_5_ = bf16[256,1024]{1,0:T(8,128)(2,1)S(1)} collective-permute-done((bf16[256,1024]{1,0:T(8,128)(2,1)S(1)}, bf16[256,1024]{1,0:T(8,128)(2,1)S(1)}, u32[]{:S(2)}, u32[]{:S(2)}) %collective-permute-start.117) | collective-permute-done | bytes 524320 | tf_op jit(solution)/shard_map/ppermute | solution.py:25
  580.7 11.7 %shard_map.281 = f32[256,8,512]{2,1,0:T(8,128)} custom-call(bf16[4,256,256]{2,1,0:T(8,128)(2,1)} %copy-done.26, bf16[4,256,256]{2,1,0:T(8,128)(2,1)} %copy-done.122, s32[4,256,2]{2,1,0:T(8,128)} %copy-done.3, s32[4,256,2]{2,1,0:T(8,128)} %convert_bitcast_fusion.refs_3_, bf16[256,512]{1,0:T(8,128)(2,1)} %get-tuple-element.243.refs_5_.refs_4_, ...), custom_call_target="tpu_custom_call" | custom-call | tf_op jit(solution)/shard_map/pallas_call | solution.py:490
  (765 shorter events, 356.5 us)
Async XLA Ops:
  10.9 21.9 %collective-permute-start.18 = (bf16[2,256,512]{2,1,0:T(8,128)(2,1)}, bf16[2,256,512]{2,1,0:T(8,128)(2,1)S(1)}, u32[]{:S(2)}, u32[]{:S(2)}) collective-permute-start(bf16[2,256,512]{2,1,0:T(8,128)(2,1)} %get-tuple-element.293), channel_id=1, source_target_pairs={{0,4},{4,0},{8,12},{12,8},{16,20},{20,16},{24,28},{28,24},{1,5},{5... | collective-permute-start | bytes 1572872 | tf_op jit(solution)/shard_map/ppermute | solution.py:25
  10.9 26.3 %collective-permute-start.7 = (bf16[2,256,512]{2,1,0:T(8,128)(2,1)}, bf16[2,256,512]{2,1,0:T(8,128)(2,1)S(1)}, u32[]{:S(2)}, u32[]{:S(2)}) collective-permute-start(bf16[2,256,512]{2,1,0:T(8,128)(2,1)} %get-tuple-element.296), channel_id=1, source_target_pairs={{0,4},{4,0},{8,12},{12,8},{16,20},{20,16},{24,28},{28,24},{1,5},{5... | collective-permute-start | bytes 1572872 | tf_op jit(solution)/shard_map/ppermute | solution.py:25
  38.7 22.1 %collective-permute-start.17 = (bf16[256,1024]{1,0:T(8,128)(2,1)}, bf16[256,1024]{1,0:T(8,128)(2,1)}, u32[]{:S(2)}, u32[]{:S(2)}) collective-permute-start(bf16[256,1024]{1,0:T(8,128)(2,1)} %pad_maximum_fusion.11.refs_0_), channel_id=1, source_target_pairs={{0,8},{4,12},{8,0},{12,4},{16,24},{20,28},{24,16},{28,20},{1,9},{5... | collective-permute-start | bytes 1572872 | tf_op jit(solution)/shard_map/ppermute | solution.py:25
  40.4 23.7 %collective-permute-start.12 = (bf16[256,1024]{1,0:T(8,128)(2,1)}, bf16[256,1024]{1,0:T(8,128)(2,1)}, u32[]{:S(2)}, u32[]{:S(2)}) collective-permute-start(bf16[256,1024]{1,0:T(8,128)(2,1)} %pad_maximum_fusion.11.refs_0_), channel_id=1, source_target_pairs={{0,16},{4,20},{8,24},{12,28},{16,0},{20,4},{24,8},{28,12},{1,17},{... | collective-permute-start | bytes 1572872 | tf_op jit(solution)/shard_map/ppermute | solution.py:25
  60.8 43.3 %collective-permute-start.20 = (bf16[256,1024]{1,0:T(8,128)(2,1)}, bf16[256,1024]{1,0:T(8,128)(2,1)}, u32[]{:S(2)}, u32[]{:S(2)}) collective-permute-start(bf16[256,1024]{1,0:T(8,128)(2,1)} %collective-permute-done.17.refs_2_), channel_id=1, source_target_pairs={{0,4},{4,0},{8,12},{12,8},{16,20},{20,16},{24,28},{28,24},{1,5},{5... | collective-permute-start | bytes 1572872 | tf_op jit(solution)/shard_map/ppermute | solution.py:25
  61.3 44.8 %collective-permute-start.13 = (bf16[256,1024]{1,0:T(8,128)(2,1)}, bf16[256,1024]{1,0:T(8,128)(2,1)}, u32[]{:S(2)}, u32[]{:S(2)}) collective-permute-start(bf16[256,1024]{1,0:T(8,128)(2,1)} %pad_maximum_fusion.11.refs_0_), channel_id=1, source_target_pairs={{0,4},{4,0},{8,12},{12,8},{16,20},{20,16},{24,28},{28,24},{1,5},{5... | collective-permute-start | bytes 1572872 | tf_op jit(solution)/shard_map/ppermute | solution.py:25
  64.1 41.5 %collective-permute-start.16 = (bf16[256,1024]{1,0:T(8,128)(2,1)}, bf16[256,1024]{1,0:T(8,128)(2,1)}, u32[]{:S(2)}, u32[]{:S(2)}) collective-permute-start(bf16[256,1024]{1,0:T(8,128)(2,1)} %collective-permute-done.12.refs_4_), channel_id=1, source_target_pairs={{0,8},{4,12},{8,0},{12,4},{16,24},{20,28},{24,16},{28,20},{1,9},{5... | collective-permute-start | bytes 1572872 | tf_op jit(solution)/shard_map/ppermute | solution.py:25
  83.9 45.7 %collective-permute-start.27 = (bf16[256,512]{1,0:T(8,128)(2,1)}, bf16[256,512]{1,0:T(8,128)(2,1)}, u32[]{:S(2)}, u32[]{:S(2)}) collective-permute-start(bf16[256,512]{1,0:T(8,128)(2,1)} %get-tuple-element.172), channel_id=1, source_target_pairs={{0,8},{4,12},{8,0},{12,4},{16,24},{20,28},{24,16},{28,20},{1,9},{5... | collective-permute-start | bytes 786440 | tf_op jit(solution)/shard_map/ppermute | solution.py:25
  93.6 38.7 %collective-permute-start.29 = (bf16[256,512]{1,0:T(8,128)(2,1)}, bf16[256,512]{1,0:T(8,128)(2,1)}, u32[]{:S(2)}, u32[]{:S(2)}) collective-permute-start(bf16[256,512]{1,0:T(8,128)(2,1)} %get-tuple-element.174), channel_id=1, source_target_pairs={{0,8},{4,12},{8,0},{12,4},{16,24},{20,28},{24,16},{28,20},{1,9},{5... | collective-permute-start | bytes 786440 | tf_op jit(solution)/shard_map/ppermute | solution.py:25
  104.1 27.1 %collective-permute-start.28 = (bf16[256,512]{1,0:T(8,128)(2,1)}, bf16[256,512]{1,0:T(8,128)(2,1)}, u32[]{:S(2)}, u32[]{:S(2)}) collective-permute-start(bf16[256,512]{1,0:T(8,128)(2,1)} %add_convert_fusion.12), channel_id=1, source_target_pairs={{0,16},{4,20},{8,24},{12,28},{16,0},{20,4},{24,8},{28,12},{1,17},{... | collective-permute-start | bytes 786440 | tf_op jit(solution)/shard_map/ppermute | solution.py:25
  106.1 23.0 %collective-permute-start.14 = (bf16[256,1024]{1,0:T(8,128)(2,1)}, bf16[256,1024]{1,0:T(8,128)(2,1)}, u32[]{:S(2)}, u32[]{:S(2)}) collective-permute-start(bf16[256,1024]{1,0:T(8,128)(2,1)} %collective-permute-done.12.refs_4_), channel_id=1, source_target_pairs={{0,4},{4,0},{8,12},{12,8},{16,20},{20,16},{24,28},{28,24},{1,5},{5... | collective-permute-start | bytes 1572872 | tf_op jit(solution)/shard_map/ppermute | solution.py:25
  129.6 25.6 %collective-permute-start.22 = (bf16[2,256,512]{2,1,0:T(8,128)(2,1)S(1)}, bf16[2,256,512]{2,1,0:T(8,128)(2,1)S(1)}, u32[]{:S(2)}, u32[]{:S(2)}) collective-permute-start(bf16[2,256,512]{2,1,0:T(8,128)(2,1)S(1)} %copy-done.125), channel_id=1, source_target_pairs={{0,4},{4,0},{8,12},{12,8},{16,20},{20,16},{24,28},{28,24},{1,5},{5... | collective-permute-start | bytes 1572872 | tf_op jit(solution)/shard_map/ppermute | solution.py:25
  144.5 25.7 %collective-permute-start.23 = (bf16[2,256,512]{2,1,0:T(8,128)(2,1)S(1)}, bf16[2,256,512]{2,1,0:T(8,128)(2,1)S(1)}, u32[]{:S(2)}, u32[]{:S(2)}) collective-permute-start(bf16[2,256,512]{2,1,0:T(8,128)(2,1)S(1)} %copy-done.124), channel_id=1, source_target_pairs={{0,4},{4,0},{8,12},{12,8},{16,20},{20,16},{24,28},{28,24},{1,5},{5... | collective-permute-start | bytes 1572872 | tf_op jit(solution)/shard_map/ppermute | solution.py:25
  230.5 25.0 %all-to-all-start.1 = ((bf16[8,24,2048]{2,1,0:T(8,128)(2,1)}), bf16[8,24,2048]{2,1,0:T(8,128)(2,1)}, u32[]{:S(2)}, u32[]{:S(2)}) async-start(bf16[8,24,2048]{2,1,0:T(8,128)(2,1)} %bitcast.268), calls=%async_computation.1 | async-start | bytes 1572864 | tf_op jit(solution)/shard_map/all_to_all | solution.py:859
  255.6 21.5 %collective-permute-start.56 = (bf16[192,2048]{1,0:T(8,128)(2,1)}, bf16[192,2048]{1,0:T(8,128)(2,1)S(1)}, u32[]{:S(2)}, u32[]{:S(2)}) collective-permute-start(bf16[192,2048]{1,0:T(8,128)(2,1)} %bitcast.32), channel_id=1, source_target_pairs={{0,2},{1,3},{2,0},{3,1},{4,6},{5,7},{6,4},{7,5},{8,10},{9,11},{10,... | collective-permute-start | bytes 2359304 | tf_op jit(solution)/shard_map/ppermute | solution.py:25
  299.5 31.4 %all-to-all-start.2 = ((bf16[8,24,2048]{2,1,0:T(8,128)(2,1)}), bf16[8,24,2048]{2,1,0:T(8,128)(2,1)}, u32[]{:S(2)}, u32[]{:S(2)}) async-start(bf16[8,24,2048]{2,1,0:T(8,128)(2,1)} %bitcast.280), calls=%async_computation.2 | async-start | bytes 1572864 | tf_op jit(solution)/shard_map/all_to_all | solution.py:863
  305.5 24.1 %collective-permute-start.62 = (bf16[192,2048]{1,0:T(8,128)(2,1)S(1)}, bf16[192,2048]{1,0:T(8,128)(2,1)S(1)}, u32[]{:S(2)}, u32[]{:S(2)}) collective-permute-start(bf16[192,2048]{1,0:T(8,128)(2,1)S(1)} %add_convert_fusion.3), channel_id=1, source_target_pairs={{0,2},{1,3},{2,0},{3,1},{4,6},{5,7},{6,4},{7,5},{8,10},{9,11},{10,... | collective-permute-start | bytes 2359304 | tf_op jit(solution)/shard_map/ppermute | solution.py:25
  330.8 33.7 %all-to-all-start.3 = ((bf16[8,24,2048]{2,1,0:T(8,128)(2,1)}), bf16[8,24,2048]{2,1,0:T(8,128)(2,1)}, u32[]{:S(2)}, u32[]{:S(2)}) async-start(bf16[8,24,2048]{2,1,0:T(8,128)(2,1)} %bitcast.281), calls=%async_computation.3 | async-start | bytes 1572864 | tf_op jit(solution)/shard_map/all_to_all | solution.py:863
  344.2 25.8 %collective-permute-start.66 = (f32[2,64]{1,0:T(2,128)}, f32[2,64]{1,0:T(2,128)}, u32[]{:S(2)}, u32[]{:S(2)}) collective-permute-start(f32[2,64]{1,0:T(2,128)} %get-tuple-element.323), channel_id=1, source_target_pairs={{0,1},{1,0},{2,3},{3,2},{4,5},{5,4},{6,7},{7,6},{8,9},{9,8},{10,11... | collective-permute-start | bytes 1544 | tf_op jit(solution)/shard_map/ppermute | solution.py:25
  344.4 22.5 %collective-permute-start.67 = (f32[2,64]{1,0:T(2,128)}, f32[2,64]{1,0:T(2,128)}, u32[]{:S(2)}, u32[]{:S(2)}) collective-permute-start(f32[2,64]{1,0:T(2,128)} %get-tuple-element.324), channel_id=1, source_target_pairs={{0,1},{1,0},{2,3},{3,2},{4,5},{5,4},{6,7},{7,6},{8,9},{9,8},{10,11... | collective-permute-start | bytes 1544 | tf_op jit(solution)/shard_map/ppermute | solution.py:25
  403.2 22.7 %collective-permute-start.69 = (bf16[8,64,256]{2,1,0:T(8,128)(2,1)S(1)}, bf16[8,64,256]{2,1,0:T(8,128)(2,1)S(1)}, u32[]{:S(2)}, u32[]{:S(2)}) collective-permute-start(bf16[8,64,256]{2,1,0:T(8,128)(2,1)S(1)} %copy-done.94), channel_id=1, source_target_pairs={{0,1},{1,0},{2,3},{3,2},{4,5},{5,4},{6,7},{7,6},{8,9},{9,8},{10,11... | collective-permute-start | bytes 786440 | tf_op jit(solution)/shard_map/ppermute | solution.py:25
  414.3 28.8 %collective-permute-start.85 = (bf16[256,512]{1,0:T(8,128)(2,1)S(1)}, bf16[256,512]{1,0:T(8,128)(2,1)S(1)}, u32[]{:S(2)}, u32[]{:S(2)}) collective-permute-start(bf16[256,512]{1,0:T(8,128)(2,1)S(1)} %get-tuple-element.239), channel_id=1, source_target_pairs={{0,8},{4,12},{8,0},{12,4},{16,24},{20,28},{24,16},{28,20},{1,9},{5... | collective-permute-start | bytes 786440 | tf_op jit(solution)/shard_map/ppermute | solution.py:25
  472.9 27.3 %collective-permute-start.112 = (bf16[8,64,256]{2,1,0:T(8,128)(2,1)}, bf16[8,64,256]{2,1,0:T(8,128)(2,1)S(1)}, u32[]{:S(2)}, u32[]{:S(2)}) collective-permute-start(bf16[8,64,256]{2,1,0:T(8,128)(2,1)} %get-tuple-element.300), channel_id=1, source_target_pairs={{0,1},{1,0},{2,3},{3,2},{4,5},{5,4},{6,7},{7,6},{8,9},{9,8},{10,11... | collective-permute-start | bytes 786440 | tf_op jit(solution)/shard_map/ppermute | solution.py:25
  473.0 27.4 %collective-permute-start.103 = (bf16[256,512]{1,0:T(8,128)(2,1)}, bf16[256,512]{1,0:T(8,128)(2,1)S(1)}, u32[]{:S(2)}, u32[]{:S(2)}) collective-permute-start(bf16[256,512]{1,0:T(8,128)(2,1)} %collective-permute-done.89.refs_7_.refs_6_), channel_id=1, source_target_pairs={{0,4},{4,0},{8,12},{12,8},{16,20},{20,16},{24,28},{28,24},{1,5},{5... | collective-permute-start | bytes 786440 | tf_op jit(solution)/shard_map/ppermute | solution.py:25
  480.0 21.9 %collective-permute-start.98 = (bf16[256,512]{1,0:T(8,128)(2,1)}, bf16[256,512]{1,0:T(8,128)(2,1)S(1)}, u32[]{:S(2)}, u32[]{:S(2)}) collective-permute-start(bf16[256,512]{1,0:T(8,128)(2,1)} %collective-permute-done.92.refs_10_.refs_9_), channel_id=1, source_target_pairs={{0,8},{4,12},{8,0},{12,4},{16,24},{20,28},{24,16},{28,20},{1,9},{5... | collective-permute-start | bytes 786440 | tf_op jit(solution)/shard_map/ppermute | solution.py:25
  500.4 26.1 %collective-permute-start.100 = (bf16[256,1024]{1,0:T(8,128)(2,1)S(1)}, bf16[256,1024]{1,0:T(8,128)(2,1)S(1)}, u32[]{:S(2)}, u32[]{:S(2)}) collective-permute-start(bf16[256,1024]{1,0:T(8,128)(2,1)S(1)} %copy-done.48), channel_id=1, source_target_pairs={{0,16},{4,20},{8,24},{12,28},{16,0},{20,4},{24,8},{28,12},{1,17},{... | collective-permute-start | bytes 1572872 | tf_op jit(solution)/shard_map/ppermute | solution.py:25
  518.2 27.9 %collective-permute-start.81 = (bf16[8,64,256]{2,1,0:T(8,128)(2,1)S(1)}, bf16[8,64,256]{2,1,0:T(8,128)(2,1)}, u32[]{:S(2)}, u32[]{:S(2)}) collective-permute-start(bf16[8,64,256]{2,1,0:T(8,128)(2,1)S(1)} %copy-done.68), channel_id=1, source_target_pairs={{0,2},{1,3},{2,0},{3,1},{4,6},{5,7},{6,4},{7,5},{8,10},{9,11},{10,... | collective-permute-start | bytes 786440 | tf_op jit(solution)/shard_map/ppermute | solution.py:25
  520.0 58.0 %collective-permute-start.80 = (bf16[8,64,256]{2,1,0:T(8,128)(2,1)S(1)}, bf16[8,64,256]{2,1,0:T(8,128)(2,1)}, u32[]{:S(2)}, u32[]{:S(2)}) collective-permute-start(bf16[8,64,256]{2,1,0:T(8,128)(2,1)S(1)} %copy-done.68), channel_id=1, source_target_pairs={{0,1},{1,0},{2,3},{3,2},{4,5},{5,4},{6,7},{7,6},{8,9},{9,8},{10,11... | collective-permute-start | bytes 786440 | tf_op jit(solution)/shard_map/ppermute | solution.py:25
  526.5 70.8 %collective-permute-start.123 = (bf16[256,8,512]{2,1,0:T(8,128)(2,1)}, bf16[256,8,512]{2,1,0:T(8,128)(2,1)}, u32[]{:S(2)}, u32[]{:S(2)}) collective-permute-start(bf16[256,8,512]{2,1,0:T(8,128)(2,1)} %get-tuple-element.265), channel_id=1, source_target_pairs={{0,4},{4,0},{8,12},{12,8},{16,20},{20,16},{24,28},{28,24},{1,5},{5... | collective-permute-start | bytes 6291464 | tf_op jit(solution)/shard_map/ppermute | solution.py:25
  546.8 31.2 %collective-permute-start.82 = (bf16[8,64,256]{2,1,0:T(8,128)(2,1)}, bf16[8,64,256]{2,1,0:T(8,128)(2,1)}, u32[]{:S(2)}, u32[]{:S(2)}) collective-permute-start(bf16[8,64,256]{2,1,0:T(8,128)(2,1)} %collective-permute-done.81.refs_2_), channel_id=1, source_target_pairs={{0,1},{1,0},{2,3},{3,2},{4,5},{5,4},{6,7},{7,6},{8,9},{9,8},{10,11... | collective-permute-start | bytes 786440 | tf_op jit(solution)/shard_map/ppermute | solution.py:25
  570.0 22.9 %collective-permute-start.122 = (bf16[256,1024]{1,0:T(8,128)(2,1)}, bf16[256,1024]{1,0:T(8,128)(2,1)}, u32[]{:S(2)}, u32[]{:S(2)}) collective-permute-start(bf16[256,1024]{1,0:T(8,128)(2,1)} %get-tuple-element.262), channel_id=1, source_target_pairs={{0,4},{4,0},{8,12},{12,8},{16,20},{20,16},{24,28},{28,24},{1,5},{5... | collective-permute-start | bytes 1572872 | tf_op jit(solution)/shard_map/ppermute | solution.py:25
  573.0 28.7 %all-to-all-start.4 = ((f32[32,18,256]{2,1,0:T(8,128)}), f32[32,18,256]{2,1,0:T(8,128)}, u32[]{:S(2)}, u32[]{:S(2)}) async-start(f32[32,18,256]{2,1,0:T(8,128)} %bitcast.75), calls=%async_computation.4 | async-start | bytes 1572864 | tf_op jit(solution)/shard_map/all_to_all | solution.py:974
  (257 other events, 3182.2 us)
